TPU v7x, 32 devices: a whole 2x2x4 slice. The times are simulated.
32 devices in a mesh: fsdp: 2 (over x), ctx: 4 (over y, core), tp: 4 (over z).
Axes of the slice: x: 2, y: 2, z: 4, core: 2. Of those that a mesh axis runs over, the one named last changes fastest.
Arguments:
- tokens: bfloat16 [8192, 2048], P(('fsdp', 'ctx'), 'tp'), may hold values from -6 to 6
- memory: bfloat16 [8192, 4096], P(('fsdp', 'ctx'), 'tp'), may hold values from -6 to 6
- dealing: int32 [8192], P(('fsdp', 'ctx')), may hold values from 0 to 8191, as said below
- cotangent: bfloat16 [8192, 2048], P(('fsdp', 'ctx'), 'tp'), may hold values from -6 to 6
- gain_first: float32 [2048], replicated, may hold values from 0.25 to 1.75
- gain_second: float32 [2048], replicated, may hold values from 0.25 to 1.75
- memory_gate: bfloat16 [2048, 4096], P(('fsdp', 'ctx'), 'tp'), may hold values from -0.125 to 0.125
- memory_out: bfloat16 [4096, 2048], P('tp', ('fsdp', 'ctx')), may hold values from -0.09375 to 0.09375
- hidden_gate: bfloat16 [2048, 8192], P(('fsdp', 'ctx'), 'tp'), may hold values from -0.125 to 0.125
- hidden_up: bfloat16 [2048, 8192], P(('fsdp', 'ctx'), 'tp'), may hold values from -0.125 to 0.125
- hidden_down: bfloat16 [8192, 2048], P('tp', ('fsdp', 'ctx')), may hold values from -0.0625 to 0.0625
Outputs:
- block_out: bfloat16 [8192, 2048], P(('fsdp', 'ctx'), 'tp')
- grad_tokens: float32 [8192, 2048], P(('fsdp', 'ctx'), 'tp')
- grad_memory: float32 [8192, 4096], P(('fsdp', 'ctx'), 'tp')
- grad_gain_first: float32 [2048], replicated
- grad_gain_second: float32 [2048], replicated
- grad_memory_gate: float32 [2048, 4096], P(('fsdp', 'ctx'), 'tp')
- grad_memory_out: float32 [4096, 2048], P('tp', ('fsdp', 'ctx'))
- grad_hidden_gate: float32 [2048, 8192], P(('fsdp', 'ctx'), 'tp')
- grad_hidden_up: float32 [2048, 8192], P(('fsdp', 'ctx'), 'tp')
- grad_hidden_down: float32 [8192, 2048], P('tp', ('fsdp', 'ctx'))
Inputs may be any that keep to these rules, and one draw needn't show every extreme that they name: dealing holds every number of 0 to 8191 once; the 1024 slots of each index of fsdp+ctx hold exactly 128 tokens of each index's own block of 1024 initial tokens.
All inputs are finite; a program needn't handle non-finite values.
Results may differ from a plain program's by a relative error of at most 0.0075.
Values may be sent and summed in bfloat16 or wider, within the bound.
A program may use at most 256 MiB of HBM per device.

v0:
```python
import jax
import jax.numpy as jnp
from jax import lax
from jax.sharding import PartitionSpec as P

EPS = 1e-06


def silu_grad(values):
    sigma = jax.nn.sigmoid(values)
    return sigma * (1.0 + values * (1.0 - sigma))


def normalize(values):
    inverse = lax.rsqrt(jnp.mean(values * values, axis=-1, keepdims=True) + EPS)
    return (values * inverse, inverse)


def norm_back(grad_in, unit_rows, inverse, gain):
    scaled = grad_in * gain
    centred = scaled - unit_rows * jnp.mean(scaled * unit_rows, axis=-1, keepdims=True)
    return (inverse * centred, jnp.sum(grad_in * unit_rows, axis=0))


def contract_rows(left, right):
    return lax.dot_general(
        left, right, (((0,), (0,)), ((), ())), preferred_element_type=jnp.float32
    )


def contract_cols(left, right):
    return lax.dot_general(
        left, right, (((1,), (1,)), ((), ())), preferred_element_type=jnp.float32
    )


def backward_weights(memory_gate, memory_out, hidden_gate, hidden_up, hidden_down):
    return (
        lax.all_gather(memory_gate, ("fsdp", "ctx"), axis=0, tiled=True),
        lax.all_gather(memory_out, ("fsdp", "ctx"), axis=1, tiled=True),
        lax.all_gather(hidden_gate, ("fsdp", "ctx"), axis=0, tiled=True),
        lax.all_gather(hidden_up, ("fsdp", "ctx"), axis=0, tiled=True),
        lax.all_gather(hidden_down, ("fsdp", "ctx"), axis=1, tiled=True),
    )


def shards(
    tokens,
    memory,
    dealing,
    cotangent,
    gain_first,
    gain_second,
    memory_gate,
    memory_out,
    hidden_gate,
    hidden_up,
    hidden_down,
):
    groups = lax.axis_size(("fsdp", "ctx"))
    group_index = lax.axis_index(("fsdp", "ctx"))
    rows = dealing.shape[0]
    block = rows // groups
    order = jnp.argsort(dealing)
    sent_rows = memory[order].reshape(groups, block, memory.shape[1])
    arrived = lax.all_to_all(sent_rows, ("fsdp", "ctx"), split_axis=0, concat_axis=0, tiled=True)
    arrived_ids = lax.all_to_all(
        dealing[order].reshape(groups, block),
        ("fsdp", "ctx"),
        split_axis=0,
        concat_axis=0,
        tiled=True,
    )
    places = arrived_ids.reshape(rows) - group_index * rows
    memory_tokens = arrived.reshape(rows, memory.shape[1])[jnp.argsort(places)]
    memory_f = memory_tokens.astype(jnp.float32)
    gathered = (
        lax.all_gather(memory_gate, ("fsdp", "ctx"), axis=0, tiled=True),
        lax.all_gather(memory_out, ("fsdp", "ctx"), axis=1, tiled=True),
        lax.all_gather(hidden_gate, ("fsdp", "ctx"), axis=0, tiled=True),
        lax.all_gather(hidden_up, ("fsdp", "ctx"), axis=0, tiled=True),
        lax.all_gather(hidden_down, ("fsdp", "ctx"), axis=1, tiled=True),
    )
    gate_w, out_w, up_a_w, up_b_w, down_w = gathered
    width = tokens.shape[1]
    column = lax.axis_index("tp") * width
    full_tokens, full_cot = (
        lax.all_gather(tokens, "tp", axis=1, tiled=True),
        lax.all_gather(cotangent, "tp", axis=1, tiled=True),
    )
    inputs = full_tokens.astype(jnp.float32)
    unit_first, inv_first = normalize(inputs)
    first = (unit_first * gain_first).astype(jnp.bfloat16)
    gate_pre = jnp.dot(first, gate_w, preferred_element_type=jnp.float32)
    activated = jax.nn.silu(gate_pre)
    mixed = (memory_f * activated).astype(jnp.bfloat16)
    middle = inputs + lax.psum(jnp.dot(mixed, out_w, preferred_element_type=jnp.float32), "tp")
    unit_second, inv_second = normalize(middle)
    second = (unit_second * gain_second).astype(jnp.bfloat16)
    up_a = jnp.dot(second, up_a_w, preferred_element_type=jnp.float32)
    up_b = jnp.dot(second, up_b_w, preferred_element_type=jnp.float32)
    swish_a = jax.nn.silu(up_a)
    swished = (swish_a * up_b).astype(jnp.bfloat16)
    output = middle + lax.psum(jnp.dot(swished, down_w, preferred_element_type=jnp.float32), "tp")
    block_out = lax.dynamic_slice_in_dim(output, column, width, 1).astype(jnp.bfloat16)
    gate_w, out_w, up_a_w, up_b_w, down_w = backward_weights(
        memory_gate, memory_out, hidden_gate, hidden_up, hidden_down
    )
    d_swished = contract_cols(full_cot, down_w)
    grad_down = contract_rows(swished, full_cot)
    d_a = (d_swished * up_b * silu_grad(up_a)).astype(jnp.bfloat16)
    d_b = (d_swished * swish_a).astype(jnp.bfloat16)
    grad_up_a = contract_rows(second, d_a)
    grad_up_b = contract_rows(second, d_b)
    d_second = lax.psum(contract_cols(d_a, up_a_w) + contract_cols(d_b, up_b_w), "tp")
    middle_norm, gain_two_part = norm_back(d_second, unit_second, inv_second, gain_second)
    d_middle = full_cot.astype(jnp.float32) + middle_norm
    d_branch = d_middle.astype(jnp.bfloat16)
    d_mixed = contract_cols(d_branch, out_w)
    grad_out = contract_rows(mixed, d_branch)
    memory_term = d_mixed * activated
    d_gate = (d_mixed * memory_f * silu_grad(gate_pre)).astype(jnp.bfloat16)
    grad_gate = contract_rows(first, d_gate)
    d_first = lax.psum(contract_cols(d_gate, gate_w), "tp")
    input_norm, gain_one_part = norm_back(d_first, unit_first, inv_first, gain_first)
    grad_inputs = lax.dynamic_slice_in_dim(d_middle + input_norm, column, width, 1)
    grad_gain_first, grad_gain_second = lax.psum((gain_one_part, gain_two_part), ("fsdp", "ctx"))
    back_rows = memory_term[places].reshape(groups, block, memory.shape[1])
    returned = lax.all_to_all(back_rows, ("fsdp", "ctx"), split_axis=0, concat_axis=0, tiled=True)
    grad_memory = returned.reshape(rows, memory.shape[1])[jnp.argsort(order)]
    sums = (
        lax.psum_scatter(grad_gate, ("fsdp", "ctx"), scatter_dimension=0, tiled=True),
        lax.psum_scatter(grad_out, ("fsdp", "ctx"), scatter_dimension=1, tiled=True),
        lax.psum_scatter(grad_up_a, ("fsdp", "ctx"), scatter_dimension=0, tiled=True),
        lax.psum_scatter(grad_up_b, ("fsdp", "ctx"), scatter_dimension=0, tiled=True),
        lax.psum_scatter(grad_down, ("fsdp", "ctx"), scatter_dimension=1, tiled=True),
    )
    return (
        block_out,
        grad_inputs,
        grad_memory,
        grad_gain_first,
        grad_gain_second,
        sums[0],
        sums[1],
        sums[2],
        sums[3],
        sums[4],
    )


def solution(mesh):
    in_specs = (
        P(("fsdp", "ctx"), "tp"),
        P(("fsdp", "ctx"), "tp"),
        P(("fsdp", "ctx")),
        P(("fsdp", "ctx"), "tp"),
        P(),
        P(),
        P(("fsdp", "ctx"), "tp"),
        P("tp", ("fsdp", "ctx")),
        P(("fsdp", "ctx"), "tp"),
        P(("fsdp", "ctx"), "tp"),
        P("tp", ("fsdp", "ctx")),
    )
    out_specs = (
        P(("fsdp", "ctx"), "tp"),
        P(("fsdp", "ctx"), "tp"),
        P(("fsdp", "ctx"), "tp"),
        P(),
        P(),
        P(("fsdp", "ctx"), "tp"),
        P("tp", ("fsdp", "ctx")),
        P(("fsdp", "ctx"), "tp"),
        P(("fsdp", "ctx"), "tp"),
        P("tp", ("fsdp", "ctx")),
    )
    return jax.shard_map(shards, mesh=mesh, in_specs=in_specs, out_specs=out_specs, check_vma=False)
```

profile of v0, /device:TPU:0, one launch (start us, length us, event | category | flops | bytes accessed | tf_op | source)
XLA Modules:
  0.0 2175.9 jit_solution(10311108215693475763)
XLA Ops:
  43.1 20.7 all-to-all-done
  69.1 24.1 %all-gather.8.cloned.1.call-done = bf16[1024,2048]{1,0:T(8,128)(2,1)} async-done(((bf16[1024,512]{1,0:T(8,128)(2,1)}), bf16[1024,2048]{1,0:T(8,128)(2,1)}) %all-gather.8.cloned.1.call-update) | async-done | bytes 4194320 | tf_op jit(solution)/shard_map/all_gather | solution.py:88
  96.3 34.1 %all-gather.10.cloned.1.call-done = bf16[2048,1024]{1,0:T(8,128)(2,1)} async-done(((bf16[256,1024]{1,0:T(8,128)(2,1)}), bf16[2048,1024]{1,0:T(8,128)(2,1)}) %all-gather.10.cloned.1.call-update) | async-done | bytes 4194320 | tf_op jit(solution)/shard_map/all_gather | solution.py:78
  140.4 29.3 %all-gather.12.cloned.1.call-done = bf16[1024,2048]{1,0:T(8,128)(2,1)} async-done(((bf16[1024,256]{1,0:T(8,128)(2,1)}), bf16[1024,2048]{1,0:T(8,128)(2,1)}) %all-gather.12.cloned.1.call-update) | async-done | bytes 4194320 | tf_op jit(solution)/shard_map/all_gather | solution.py:79
  183.7 288.3 %all-reduce.6.cloned.1.call-done = f32[1024,2048]{1,0:T(8,128)} async-done(((f32[1024,2048]{1,0:T(8,128)}), f32[1024,2048]{1,0:T(8,128)}) %all-reduce.6.cloned.1.call-update) | async-done | bytes 8388624 | tf_op jit(solution)/shard_map/psum | solution.py:97
  484.1 43.1 %all-gather.16.cloned.1.call-done = bf16[2048,2048]{1,0:T(8,128)(2,1)} async-done(((bf16[256,2048]{1,0:T(8,128)(2,1)}), bf16[2048,2048]{1,0:T(8,128)(2,1)}) %all-gather.16.cloned.1.call-update) | async-done | bytes 8388624 | tf_op jit(solution)/shard_map/all_gather | solution.py:81
  527.1 15.0 fusion.22
  542.1 41.2 %all-gather.14.cloned.1.call-done = bf16[2048,2048]{1,0:T(8,128)(2,1)} async-done(((bf16[256,2048]{1,0:T(8,128)(2,1)}), bf16[2048,2048]{1,0:T(8,128)(2,1)}) %all-gather.14.cloned.1.call-update) | async-done | bytes 8388624 | tf_op jit(solution)/shard_map/all_gather | solution.py:80
  597.8 67.8 %all-gather.20.cloned.1.call-done = bf16[1024,2048]{1,0:T(8,128)(2,1)} async-done(((bf16[1024,512]{1,0:T(8,128)(2,1)}), bf16[1024,2048]{1,0:T(8,128)(2,1)}) %all-gather.20.cloned.1.call-update) | async-done | bytes 4194320 | tf_op jit(solution)/shard_map/all_gather | solution.py:89
  665.7 56.4 %all-gather.18.cloned.1.call-done = bf16[2048,2048]{1,0:T(8,128)(2,1)} async-done(((bf16[2048,256]{1,0:T(8,128)(2,1)}), bf16[2048,2048]{1,0:T(8,128)(2,1)}) %all-gather.18.cloned.1.call-update) | async-done | bytes 8388624 | tf_op jit(solution)/shard_map/all_gather | solution.py:82
  722.1 21.8 %multiply_convert_fusion = (bf16[1024,2048]{1,0:T(8,128)(2,1)}, bf16[1024,2048]{1,0:T(8,128)(2,1)}, bf16[1024,2048]{1,0:T(8,128)(2,1)}) fusion(f32[1024,2048]{1,0:T(8,128)} %fusion.21, f32[1024,2048]{1,0:T(8,128)} %fusion.22, bf16[1024,2048]{1,0:T(8,128)(2,1)} %all-gather.20.cloned.1.call-done, bf16[2048,2048]{1,0:T(8,128)(2,1)} %all-gather.18.cloned.1.call-done), kind=kOutput, calls=%fused_computation.14 | convolution fusion | flops 8621391872 | bytes 41943040 | tf_op jit(solution)/shard_map/dot_general | solution.py:32
  770.5 14.7 fusion.23
  785.2 276.2 %all-reduce.8.cloned.1.call-done = f32[1024,2048]{1,0:T(8,128)} async-done(((f32[1024,2048]{1,0:T(8,128)}), f32[1024,2048]{1,0:T(8,128)}) %all-reduce.8.cloned.1.call-update) | async-done | bytes 8388624 | tf_op jit(solution)/shard_map/psum | solution.py:115
  1122.2 15.3 fusion.28
  1137.6 15.4 fusion.27
  1153.2 15.5 fusion.26
  1187.0 43.8 %all-to-all-done.2 = f32[8,128,1024]{2,1,0:T(8,128)} async-done(((f32[8,128,1024]{2,1,0:T(8,128)}), f32[8,128,1024]{2,1,0:T(8,128)}, u32[]{:S(2)}, u32[]{:S(2)}) %all-to-all-start.2) | async-done | bytes 4194336 | tf_op jit(solution)/shard_map/all_to_all | solution.py:129
  1239.3 419.8 %all-reduce.10.cloned.1.call-done = (f32[1024,2048]{1,0:T(8,128)}, f32[1024,2048]{1,0:T(8,128)}) async-done(((f32[1024,2048]{1,0:T(8,128)}, f32[1024,2048]{1,0:T(8,128)}), (f32[1024,2048]{1,0:T(8,128)}, f32[1024,2048]{1,0:T(8,128)})) %all-reduce.10.cloned.1.call-update) | async-done | bytes 16777232 | tf_op jit(solution)/shard_map/psum | solution.py:104
  1669.2 24.7 %all-reduce = (f32[2048]{0:T(1024)}, f32[2048]{0:T(1024)}) all-reduce(f32[2048]{0:T(1024)S(1)} %get-tuple-element.18, f32[2048]{0:T(1024)S(1)} %copy-done.11), channel_id=1, replica_groups=mesh['fsdp'=2,'ctx'=4,'tp'=4] {'fsdp','ctx'}, use_global_device_ids=true, to_apply=%region_12.13 | all-reduce | flops 4096 | bytes 32768 | tf_op jit(solution)/shard_map/psum | solution.py:127
  1700.4 33.0 %reduce-scatter.8.cloned.1.call-done = f32[1024,256]{1,0:T(8,128)} async-done(((f32[1024,2048]{1,0:T(8,128)}), f32[1024,256]{1,0:T(8,128)}) %reduce-scatter.8.cloned.1.call-update) | async-done | bytes 1048592 | tf_op jit(solution)/shard_map/reduce_scatter | solution.py:133
  1733.5 75.6 %reduce-scatter.6.cloned.1.call-done = f32[256,1024]{1,0:T(8,128)} async-done(((f32[2048,1024]{1,0:T(8,128)}), f32[256,1024]{1,0:T(8,128)}) %reduce-scatter.6.cloned.1.call-update) | async-done | bytes 1048592 | tf_op jit(solution)/shard_map/reduce_scatter | solution.py:132
  1809.1 120.1 %reduce-scatter.14.cloned.1.call-done = f32[2048,256]{1,0:T(8,128)} async-done(((f32[2048,2048]{1,0:T(8,128)}), f32[2048,256]{1,0:T(8,128)}) %reduce-scatter.14.cloned.1.call-update) | async-done | bytes 2097168 | tf_op jit(solution)/shard_map/reduce_scatter | solution.py:136
  1929.2 120.0 %reduce-scatter.12.cloned.1.call-done = f32[256,2048]{1,0:T(8,128)} async-done(((f32[2048,2048]{1,0:T(8,128)}), f32[256,2048]{1,0:T(8,128)}) %reduce-scatter.12.cloned.1.call-update) | async-done | bytes 2097168 | tf_op jit(solution)/shard_map/reduce_scatter | solution.py:135
  2049.2 120.0 %reduce-scatter.10.cloned.1.call-done = f32[256,2048]{1,0:T(8,128)} async-done(((f32[2048,2048]{1,0:T(8,128)}), f32[256,2048]{1,0:T(8,128)}) %reduce-scatter.10.cloned.1.call-update) | async-done | bytes 2097168 | tf_op jit(solution)/shard_map/reduce_scatter | solution.py:134
  (110 shorter events, 225.7 us)
Async XLA Ops:
  7.2 21.3 copy-start
  7.2 86.0 %all-gather.8.cloned.1.call-start = ((), (), s32[]{:S(2)}) async-start(), calls=%async_computation.8 | async-start | bytes 5242880 | tf_op jit(solution)/shard_map/all_gather | solution.py:88
  7.9 122.4 %all-gather.10.cloned.1.call-start = ((), (), s32[]{:S(2)}) async-start(), calls=%async_computation.9 | async-start | bytes 4718592 | tf_op jit(solution)/shard_map/all_gather | solution.py:78
  8.7 161.0 %all-gather.12.cloned.1.call-start = ((), (), s32[]{:S(2)}) async-start(), calls=%async_computation.10 | async-start | bytes 4718592 | tf_op jit(solution)/shard_map/all_gather | solution.py:79
  23.3 10.5 all-to-all-start.1
  33.9 29.9 %all-to-all-start = ((bf16[8,128,1024]{2,1,0:T(8,128)(2,1)}), bf16[8,128,1024]{2,1,0:T(8,128)(2,1)S(1)}, u32[]{:S(2)}, u32[]{:S(2)}) async-start(bf16[8,128,1024]{2,1,0:T(8,128)(2,1)} %bitcast.35), calls=%async_computation | async-start | bytes 4194304 | tf_op jit(solution)/shard_map/all_to_all | solution.py:66
  38.1 433.9 %all-reduce.6.cloned.1.call-start = ((), (), s32[]{:S(2)}) async-start(), calls=%async_computation.11 | async-start | bytes 16777216 | tf_op jit(solution)/shard_map/psum | solution.py:97
  69.1 61.2 %copy-start.15 = (f32[2048]{0:T(1024)S(1)}, f32[2048]{0:T(1024)}, u32[]{:S(2)}) copy-start(f32[2048]{0:T(1024)} %param.15) | copy-start | bytes 24580
  96.3 44.1 %copy-start.9 = (f32[1024]{0:T(1024)}, f32[1024]{0:T(1024)S(1)}, u32[]{:S(2)}) copy-start(f32[1024]{0:T(1024)S(1)} %add_rsqrt_fusion.1) | copy-start | bytes 12292
  96.3 73.4 %copy-start.7 = (bf16[1024,1024]{1,0:T(8,128)(2,1)S(1)}, bf16[1024,1024]{1,0:T(8,128)(2,1)}, u32[]{:S(2)}) copy-start(bf16[1024,1024]{1,0:T(8,128)(2,1)} %gather_fusion.2) | copy-start | bytes 6291460
  181.0 346.2 %all-gather.16.cloned.1.call-start = ((), (), s32[]{:S(2)}) async-start(), calls=%async_computation.13 | async-start | bytes 9437184 | tf_op jit(solution)/shard_map/all_gather | solution.py:81
  181.6 401.8 %all-gather.14.cloned.1.call-start = ((), (), s32[]{:S(2)}) async-start(), calls=%async_computation.12 | async-start | bytes 9437184 | tf_op jit(solution)/shard_map/all_gather | solution.py:80
  182.1 483.5 %all-gather.20.cloned.1.call-start = ((), (), s32[]{:S(2)}) async-start(), calls=%async_computation.15 | async-start | bytes 5242880 | tf_op jit(solution)/shard_map/all_gather | solution.py:89
  182.9 539.2 %all-gather.18.cloned.1.call-start = ((), (), s32[]{:S(2)}) async-start(), calls=%async_computation.14 | async-start | bytes 9437184 | tf_op jit(solution)/shard_map/all_gather | solution.py:82
  183.6 297.6 %copy-start.8 = (f32[2048]{0:T(1024)S(1)}, f32[2048]{0:T(1024)}, u32[]{:S(2)}) copy-start(f32[2048]{0:T(1024)} %param.16) | copy-start | bytes 24580
  183.6 877.8 %all-reduce.8.cloned.1.call-start = ((), (), s32[]{:S(2)}) async-start(), calls=%async_computation.16 | async-start | bytes 16777216 | tf_op jit(solution)/shard_map/psum | solution.py:115
  770.4 888.7 %all-reduce.10.cloned.1.call-start = ((), (), s32[]{:S(2)}) async-start(), calls=%async_computation.22 | async-start | bytes 33554432 | tf_op jit(solution)/shard_map/psum | solution.py:104
  1096.7 636.8 %reduce-scatter.8.cloned.1.call-start = ((), (), s32[]{:S(2)}) async-start(), calls=%async_computation.18 | async-start | bytes 9437184 | tf_op jit(solution)/shard_map/reduce_scatter | solution.py:133
  1110.1 699.0 %reduce-scatter.6.cloned.1.call-start = ((), (), s32[]{:S(2)}) async-start(), calls=%async_computation.17 | async-start | bytes 9437184 | tf_op jit(solution)/shard_map/reduce_scatter | solution.py:132
  1121.7 807.5 %reduce-scatter.14.cloned.1.call-start = ((), (), s32[]{:S(2)}) async-start(), calls=%async_computation.21 | async-start | bytes 18874368 | tf_op jit(solution)/shard_map/reduce_scatter | solution.py:136
  1137.6 911.6 %reduce-scatter.12.cloned.1.call-start = ((), (), s32[]{:S(2)}) async-start(), calls=%async_computation.20 | async-start | bytes 18874368 | tf_op jit(solution)/shard_map/reduce_scatter | solution.py:135
  1153.0 1016.1 %reduce-scatter.10.cloned.1.call-start = ((), (), s32[]{:S(2)}) async-start(), calls=%async_computation.19 | async-start | bytes 18874368 | tf_op jit(solution)/shard_map/reduce_scatter | solution.py:134
  1177.9 52.9 %all-to-all-start.2 = ((f32[8,128,1024]{2,1,0:T(8,128)}), f32[8,128,1024]{2,1,0:T(8,128)}, u32[]{:S(2)}, u32[]{:S(2)}) async-start(f32[8,128,1024]{2,1,0:T(8,128)} %bitcast.34), calls=%async_computation.2 | async-start | bytes 8388608 | tf_op jit(solution)/shard_map/all_to_all | solution.py:129
  1693.9 475.3 %copy-start.1 = (bf16[1024,1024]{1,0:T(8,128)(2,1)S(1)}, bf16[1024,1024]{1,0:T(8,128)(2,1)}, u32[]{:S(2)}) copy-start(bf16[1024,1024]{1,0:T(8,128)(2,1)} %param.12) | copy-start | bytes 6291460
  (14 other events, 106.5 us)
Sparse Core Ops, SparseCore 0:
  9.6 83.5 all-gather.7
  95.1 35.2 all-gather.9
  132.2 37.4 all-gather.11
  181.1 290.8 all-reduce.5
  473.7 53.3 all-gather.15
  528.9 54.3 all-gather.13
  584.9 80.7 all-gather.19
  667.6 54.4 all-gather.17
  770.5 290.8 all-reduce.7
  1096.8 562.2 all-reduce.9
  1663.2 70.2 reduce-scatter.7
  1737.7 71.2 reduce-scatter.5
  1813.2 115.9 reduce-scatter.13
  1933.2 115.9 reduce-scatter.11
  2053.2 115.9 reduce-scatter.9
where the time goes:
time: 2180 us
  waiting for transfers between devices  1820 us (83%)
  matrix products  204 us (9%)
  other arithmetic  54.8 us (3%)
  local copies, waits for them, and re-layouts  44.6 us (2%)
  blocking collectives  24.7 us (1%)
    psum x1, waiting for transfers between devices, shards(): lax.psum(jnp.dot(swished, down_w, preferred_element_type=jnp.float32), 'tp')  420 us
    psum x1, waiting for transfers between devices, shards(): lax.psum(jnp.dot(mixed, out_w, preferred_element_type=jnp.float32), 'tp')  288 us
    psum x1, waiting for transfers between devices, shards(): lax.psum(contract_cols(d_a, up_a_w) + contract_cols(d_b, up_b_w), 'tp')  276 us
    reduce_scatter x1, waiting for transfers between devices, shards(): lax.psum_scatter(grad_down, ('fsdp', 'ctx'), scatter_dimension=1, tiled=T...  120 us
    reduce_scatter x1, waiting for transfers between devices, shards(): lax.psum_scatter(grad_up_b, ('fsdp', 'ctx'), scatter_dimension=0, tiled=T...  120 us
    reduce_scatter x1, waiting for transfers between devices, shards(): lax.psum_scatter(grad_up_a, ('fsdp', 'ctx'), scatter_dimension=0, tiled=T...  120 us
    reduce_scatter x1, waiting for transfers between devices, shards(): lax.psum_scatter(grad_gate, ('fsdp', 'ctx'), scatter_dimension=0, tiled=T...  75.6 us
    dot_general x5, matrix products, contract_rows(): lax.dot_general(left, right, (((0,), (0,)), ((), ())), preferred_element_...  70.1 us
  transfers between devices with their start and end apart: 18, of which 17 were waited for; matrix products, arithmetic and copies ran while one was open for 9% of the time, Pallas kernels for 0%

commit v1 on v0

--- a/solution.py
+++ b/solution.py
@@ -16,12 +16,6 @@
     return (values * inverse, inverse)
 
 
-def norm_back(grad_in, unit_rows, inverse, gain):
-    scaled = grad_in * gain
-    centred = scaled - unit_rows * jnp.mean(scaled * unit_rows, axis=-1, keepdims=True)
-    return (inverse * centred, jnp.sum(grad_in * unit_rows, axis=0))
-
-
 def contract_rows(left, right):
     return lax.dot_general(
         left, right, (((0,), (0,)), ((), ())), preferred_element_type=jnp.float32
@@ -34,14 +28,20 @@
     )
 
 
-def backward_weights(memory_gate, memory_out, hidden_gate, hidden_up, hidden_down):
-    return (
-        lax.all_gather(memory_gate, ("fsdp", "ctx"), axis=0, tiled=True),
-        lax.all_gather(memory_out, ("fsdp", "ctx"), axis=1, tiled=True),
-        lax.all_gather(hidden_gate, ("fsdp", "ctx"), axis=0, tiled=True),
-        lax.all_gather(hidden_up, ("fsdp", "ctx"), axis=0, tiled=True),
-        lax.all_gather(hidden_down, ("fsdp", "ctx"), axis=1, tiled=True),
-    )
+def sum_scatter(part):
+    return lax.psum_scatter(
+        part.astype(jnp.bfloat16), "tp", scatter_dimension=1, tiled=True
+    ).astype(jnp.float32)
+
+
+def mean_over(values, features):
+    return lax.psum(jnp.sum(values, axis=-1, keepdims=True), "tp") / features
+
+
+def grad_scatter(part, dimension):
+    return lax.psum_scatter(
+        part.astype(jnp.bfloat16), ("fsdp", "ctx"), scatter_dimension=dimension, tiled=True
+    ).astype(jnp.float32)
 
 
 def shards(
@@ -94,46 +94,55 @@
     gate_pre = jnp.dot(first, gate_w, preferred_element_type=jnp.float32)
     activated = jax.nn.silu(gate_pre)
     mixed = (memory_f * activated).astype(jnp.bfloat16)
-    middle = inputs + lax.psum(jnp.dot(mixed, out_w, preferred_element_type=jnp.float32), "tp")
-    unit_second, inv_second = normalize(middle)
-    second = (unit_second * gain_second).astype(jnp.bfloat16)
+    features = full_tokens.shape[1]
+    own = lambda array: lax.dynamic_slice_in_dim(array, column, width, array.ndim - 1)
+    gain_one, gain_two = own(gain_first), own(gain_second)
+    shard_tokens = tokens.astype(jnp.float32)
+    middle = shard_tokens + sum_scatter(jnp.dot(mixed, out_w, preferred_element_type=jnp.float32))
+    inv_second = lax.rsqrt(mean_over(middle * middle, features) + EPS)
+    unit_second = middle * inv_second
+    second = lax.all_gather((unit_second * gain_two).astype(jnp.bfloat16), "tp", axis=1, tiled=True)
     up_a = jnp.dot(second, up_a_w, preferred_element_type=jnp.float32)
     up_b = jnp.dot(second, up_b_w, preferred_element_type=jnp.float32)
     swish_a = jax.nn.silu(up_a)
     swished = (swish_a * up_b).astype(jnp.bfloat16)
-    output = middle + lax.psum(jnp.dot(swished, down_w, preferred_element_type=jnp.float32), "tp")
-    block_out = lax.dynamic_slice_in_dim(output, column, width, 1).astype(jnp.bfloat16)
-    gate_w, out_w, up_a_w, up_b_w, down_w = backward_weights(
-        memory_gate, memory_out, hidden_gate, hidden_up, hidden_down
-    )
+    output = middle + sum_scatter(jnp.dot(swished, down_w, preferred_element_type=jnp.float32))
+    block_out = output.astype(jnp.bfloat16)
     d_swished = contract_cols(full_cot, down_w)
     grad_down = contract_rows(swished, full_cot)
     d_a = (d_swished * up_b * silu_grad(up_a)).astype(jnp.bfloat16)
     d_b = (d_swished * swish_a).astype(jnp.bfloat16)
     grad_up_a = contract_rows(second, d_a)
     grad_up_b = contract_rows(second, d_b)
-    d_second = lax.psum(contract_cols(d_a, up_a_w) + contract_cols(d_b, up_b_w), "tp")
-    middle_norm, gain_two_part = norm_back(d_second, unit_second, inv_second, gain_second)
-    d_middle = full_cot.astype(jnp.float32) + middle_norm
-    d_branch = d_middle.astype(jnp.bfloat16)
+    d_second = sum_scatter(contract_cols(d_a, up_a_w) + contract_cols(d_b, up_b_w))
+    scaled = d_second * gain_two
+    middle_norm = inv_second * (scaled - unit_second * mean_over(scaled * unit_second, features))
+    gain_two_part = jnp.sum(d_second * unit_second, axis=0)
+    d_middle = cotangent.astype(jnp.float32) + middle_norm
+    d_branch = lax.all_gather(d_middle.astype(jnp.bfloat16), "tp", axis=1, tiled=True)
     d_mixed = contract_cols(d_branch, out_w)
     grad_out = contract_rows(mixed, d_branch)
     memory_term = d_mixed * activated
     d_gate = (d_mixed * memory_f * silu_grad(gate_pre)).astype(jnp.bfloat16)
     grad_gate = contract_rows(first, d_gate)
-    d_first = lax.psum(contract_cols(d_gate, gate_w), "tp")
-    input_norm, gain_one_part = norm_back(d_first, unit_first, inv_first, gain_first)
-    grad_inputs = lax.dynamic_slice_in_dim(d_middle + input_norm, column, width, 1)
-    grad_gain_first, grad_gain_second = lax.psum((gain_one_part, gain_two_part), ("fsdp", "ctx"))
-    back_rows = memory_term[places].reshape(groups, block, memory.shape[1])
+    d_first = sum_scatter(contract_cols(d_gate, gate_w))
+    unit_own = shard_tokens * inv_first
+    scaled = d_first * gain_one
+    input_norm = inv_first * (scaled - unit_own * mean_over(scaled * unit_own, features))
+    gain_one_part = jnp.sum(d_first * unit_own, axis=0)
+    grad_inputs = d_middle + input_norm
+    parts = lax.psum(jnp.stack([gain_one_part, gain_two_part]), ("fsdp", "ctx"))
+    gains = lax.all_gather(parts, "tp", axis=1, tiled=True)
+    grad_gain_first, grad_gain_second = gains[0], gains[1]
+    back_rows = memory_term.astype(jnp.bfloat16)[places].reshape(groups, block, memory.shape[1])
     returned = lax.all_to_all(back_rows, ("fsdp", "ctx"), split_axis=0, concat_axis=0, tiled=True)
-    grad_memory = returned.reshape(rows, memory.shape[1])[jnp.argsort(order)]
+    grad_memory = returned.reshape(rows, memory.shape[1])[jnp.argsort(order)].astype(jnp.float32)
     sums = (
-        lax.psum_scatter(grad_gate, ("fsdp", "ctx"), scatter_dimension=0, tiled=True),
-        lax.psum_scatter(grad_out, ("fsdp", "ctx"), scatter_dimension=1, tiled=True),
-        lax.psum_scatter(grad_up_a, ("fsdp", "ctx"), scatter_dimension=0, tiled=True),
-        lax.psum_scatter(grad_up_b, ("fsdp", "ctx"), scatter_dimension=0, tiled=True),
-        lax.psum_scatter(grad_down, ("fsdp", "ctx"), scatter_dimension=1, tiled=True),
+        grad_scatter(grad_gate, 0),
+        grad_scatter(grad_out, 1),
+        grad_scatter(grad_up_a, 0),
+        grad_scatter(grad_up_b, 0),
+        grad_scatter(grad_down, 1),
     )
     return (
         block_out,

time: 2180 us -> 1340 us (0.61)
  waiting for transfers between devices: 1820 us -> 961 us
  blocking collectives: 24.7 us -> 60.9 us
    psum x3 -> x0, waiting for transfers between devices: 984 us -> none  [the longest x1 420 us: shards(): lax.psum(jnp.dot(swished, down_w, preferred_element_type=jnp.float32), 'tp')]
    all_gather x0 -> x2, waiting for transfers between devices: none -> 119 us  [the longest x1 82.9 us: shards(): lax.all_gather((unit_second * gain_two).astype(jnp.bfloat16), 'tp', axis=...]
    reduce_scatter x5 -> x9, waiting for transfers between devices: 469 us -> 525 us  [the longest x4 268 us: sum_scatter(): lax.psum_scatter(part.astype(jnp.bfloat16), 'tp', scatter_dimension=1, ti...]
    all_to_all x1, waiting for transfers between devices: 43.8 us -> 0.01 us  [shards(): lax.all_to_all(back_rows, ('fsdp', 'ctx'), split_axis=0, concat_axis=0, t...]
    psum x1 -> x4, blocking collectives: 24.7 us -> 46.9 us  [the longest x3 33.2 us: mean_over(): return lax.psum(jnp.sum(values, axis=-1, keepdims=True), 'tp') / features]
  transfers between devices with their start and end apart: 18 -> 21, of which waited for: 17 -> 19; matrix products, arithmetic and copies ran while one was open for 9% -> 16% of each run, Pallas kernels for 0% -> 0%
where the time goes in v1:
time: 1340 us; the launch traced here: 1330 us
  waiting for transfers between devices  961 us (72%)
  matrix products  195 us (15%)
  blocking collectives  60.9 us (5%)
  other arithmetic  50.6 us (4%)
  local copies, waits for them, and re-layouts  33.7 us (3%)
  between operations  14.9 us (1%)
  starting transfers between devices  14.5 us (1%)
    reduce_scatter x4, waiting for transfers between devices, sum_scatter(): lax.psum_scatter(part.astype(jnp.bfloat16), 'tp', scatter_dimension=1, ti...  268 us
    reduce_scatter x5, waiting for transfers between devices, grad_scatter(): lax.psum_scatter(part.astype(jnp.bfloat16), ('fsdp', 'ctx'), scatter_dime...  257 us
    all_gather x1, waiting for transfers between devices, shards(): lax.all_gather((unit_second * gain_two).astype(jnp.bfloat16), 'tp', axis=...  82.9 us
    dot_general x5, matrix products, contract_cols(): lax.dot_general(left, right, (((1,), (1,)), ((), ())), preferred_element_...  72 us
    all_gather x1, waiting for transfers between devices, shards(): lax.all_gather(cotangent, 'tp', axis=1, tiled=True)  68.1 us
    dot_general x5, matrix products, contract_rows(): lax.dot_general(left, right, (((0,), (0,)), ((), ())), preferred_element_...  59.8 us
    all_gather x1, waiting for transfers between devices, shards(): lax.all_gather(hidden_down, ('fsdp', 'ctx'), axis=1, tiled=True)  56.6 us
    all_gather x1, waiting for transfers between devices, shards(): lax.all_gather(hidden_up, ('fsdp', 'ctx'), axis=0, tiled=True)  40.6 us
  transfers between devices with their start and end apart: 21, of which 19 were waited for; matrix products, arithmetic and copies ran while one was open for 16% of the time, Pallas kernels for 0%

profile of v1, /device:TPU:0, one launch (start us, length us, event | category | flops | bytes accessed | tf_op | source)
XLA Modules:
  0.0 1330.2 jit_solution(13561346961598353501)
XLA Ops:
  43.1 20.7 %all-to-all-done = bf16[8,128,1024]{2,1,0:T(8,128)(2,1)S(1)} async-done(((bf16[8,128,1024]{2,1,0:T(8,128)(2,1)}), bf16[8,128,1024]{2,1,0:T(8,128)(2,1)S(1)}, u32[]{:S(2)}, u32[]{:S(2)}) %all-to-all-start) | async-done | bytes 2097184 | tf_op jit(solution)/shard_map/all_to_all | solution.py:66
  69.1 24.1 %all-gather.10.cloned.1.call-done = bf16[1024,2048]{1,0:T(8,128)(2,1)} async-done(((bf16[1024,512]{1,0:T(8,128)(2,1)}), bf16[1024,2048]{1,0:T(8,128)(2,1)}) %all-gather.10.cloned.1.call-update) | async-done | bytes 4194320 | tf_op jit(solution)/shard_map/all_gather | solution.py:88
  96.3 34.1 %all-gather.12.cloned.1.call-done = bf16[2048,1024]{1,0:T(8,128)(2,1)} async-done(((bf16[256,1024]{1,0:T(8,128)(2,1)}), bf16[2048,1024]{1,0:T(8,128)(2,1)}) %all-gather.12.cloned.1.call-update) | async-done | bytes 4194320 | tf_op jit(solution)/shard_map/all_gather | solution.py:78
  140.4 29.3 %all-gather.14.cloned.1.call-done = bf16[1024,2048]{1,0:T(8,128)(2,1)} async-done(((bf16[1024,256]{1,0:T(8,128)(2,1)}), bf16[1024,2048]{1,0:T(8,128)(2,1)}) %all-gather.14.cloned.1.call-update) | async-done | bytes 4194320 | tf_op jit(solution)/shard_map/all_gather | solution.py:79
  181.1 75.5 %reduce-scatter.10.cloned.1.call-done = bf16[1024,512]{1,0:T(8,128)(2,1)} async-done(((bf16[1024,2048]{1,0:T(8,128)(2,1)}), bf16[1024,512]{1,0:T(8,128)(2,1)}) %reduce-scatter.10.cloned.1.call-update) | async-done | bytes 1048592 | tf_op jit(solution)/shard_map/reduce_scatter | solution.py:32
  274.3 39.1 %all-gather.18.cloned.1.call-done = bf16[2048,2048]{1,0:T(8,128)(2,1)} async-done(((bf16[256,2048]{1,0:T(8,128)(2,1)}), bf16[2048,2048]{1,0:T(8,128)(2,1)}) %all-gather.18.cloned.1.call-update) | async-done | bytes 8388624 | tf_op jit(solution)/shard_map/all_gather | solution.py:80
  313.4 82.9 %all-gather.16.cloned.1.call-done = bf16[1024,2048]{1,0:T(8,128)(2,1)} async-done(((bf16[1024,512]{1,0:T(8,128)(2,1)}), bf16[1024,2048]{1,0:T(8,128)(2,1)}) %all-gather.16.cloned.1.call-update) | async-done | bytes 4194320 | tf_op jit(solution)/shard_map/all_gather | solution.py:104
  396.3 14.4 %fusion.32 = f32[1024,2048]{1,0:T(8,128)} fusion(bf16[1024,2048]{1,0:T(8,128)(2,1)} %all-gather.16.cloned.1.call-done, bf16[2048,2048]{1,0:T(8,128)(2,1)} %all-gather.18.cloned.1.call-done), kind=kOutput, calls=%fused_computation.72 | convolution fusion | flops 8589934592 | bytes 20971520 | tf_op jit(solution)/shard_map/dot_general | solution.py:105
  410.7 40.6 %all-gather.20.cloned.1.call-done = bf16[2048,2048]{1,0:T(8,128)(2,1)} async-done(((bf16[256,2048]{1,0:T(8,128)(2,1)}), bf16[2048,2048]{1,0:T(8,128)(2,1)}) %all-gather.20.cloned.1.call-update) | async-done | bytes 8388624 | tf_op jit(solution)/shard_map/all_gather | solution.py:81
  451.3 14.4 %fusion.33 = f32[1024,2048]{1,0:T(8,128)} fusion(bf16[1024,2048]{1,0:T(8,128)(2,1)} %all-gather.16.cloned.1.call-done, bf16[2048,2048]{1,0:T(8,128)(2,1)} %all-gather.20.cloned.1.call-done), kind=kOutput, calls=%fused_computation.73 | convolution fusion | flops 8589934592 | bytes 20971520 | tf_op jit(solution)/shard_map/dot_general | solution.py:106
  465.7 68.1 %all-gather.24.cloned.1.call-done = bf16[1024,2048]{1,0:T(8,128)(2,1)} async-done(((bf16[1024,512]{1,0:T(8,128)(2,1)}), bf16[1024,2048]{1,0:T(8,128)(2,1)}) %all-gather.24.cloned.1.call-update) | async-done | bytes 4194320 | tf_op jit(solution)/shard_map/all_gather | solution.py:89
  533.8 56.6 %all-gather.22.cloned.1.call-done = bf16[2048,2048]{1,0:T(8,128)(2,1)} async-done(((bf16[2048,256]{1,0:T(8,128)(2,1)}), bf16[2048,2048]{1,0:T(8,128)(2,1)}) %all-gather.22.cloned.1.call-update) | async-done | bytes 8388624 | tf_op jit(solution)/shard_map/all_gather | solution.py:82
  590.3 21.7 %multiply_convert_fusion = (bf16[1024,2048]{1,0:T(8,128)(2,1)}, bf16[1024,2048]{1,0:T(8,128)(2,1)}, bf16[1024,2048]{1,0:T(8,128)(2,1)}) fusion(f32[1024,2048]{1,0:T(8,128)} %fusion.32, f32[1024,2048]{1,0:T(8,128)} %fusion.33, bf16[1024,2048]{1,0:T(8,128)(2,1)} %all-gather.24.cloned.1.call-done, bf16[2048,2048]{1,0:T(8,128)(2,1)} %all-gather.22.cloned.1.call-done), kind=kOutput, calls=%fused_computation.11 | convolution fusion | flops 8621391872 | bytes 41943040 | tf_op jit(solution)/shard_map/dot_general | solution.py:26
  612.0 14.8 %fusion.34 = f32[1024,2048]{1,0:T(8,128)} fusion(bf16[1024,2048]{1,0:T(8,128)(2,1)} %get-tuple-element.23, bf16[2048,2048]{1,0:T(8,128)(2,1)} %all-gather.18.cloned.1.call-done), kind=kOutput, calls=%fused_computation.74 | convolution fusion | flops 8589934592 | bytes 20971520 | tf_op jit(solution)/shard_map/dot_general | solution.py:26
  639.2 76.9 %reduce-scatter.14.cloned.1.call-done = bf16[1024,512]{1,0:T(8,128)(2,1)} async-done(((bf16[1024,2048]{1,0:T(8,128)(2,1)}), bf16[1024,512]{1,0:T(8,128)(2,1)}) %reduce-scatter.14.cloned.1.call-update) | async-done | bytes 1048592 | tf_op jit(solution)/shard_map/reduce_scatter | solution.py:32
  732.2 14.4 %convolution_convert_fusion.2 = bf16[2048,2048]{1,0:T(8,128)(2,1)} fusion(bf16[1024,2048]{1,0:T(8,128)(2,1)} %all-gather.16.cloned.1.call-done, bf16[1024,2048]{1,0:T(8,128)(2,1)} %get-tuple-element.23), kind=kOutput, calls=%fused_computation.18 | convolution fusion | flops 8594128896 | bytes 16777216 | tf_op jit(solution)/shard_map/dot_general | solution.py:20
  760.9 14.2 %convolution_convert_fusion = bf16[2048,2048]{1,0:T(8,128)(2,1)} fusion(bf16[1024,2048]{1,0:T(8,128)(2,1)} %get-tuple-element.24, bf16[1024,2048]{1,0:T(8,128)(2,1)} %all-gather.24.cloned.1.call-done), kind=kOutput, calls=%fused_computation.16 | convolution fusion | flops 8594128896 | bytes 16777216 | tf_op jit(solution)/shard_map/dot_general | solution.py:20
  775.2 36.2 %all-gather.26.cloned.1.call-done = bf16[1024,2048]{1,0:T(8,128)(2,1)} async-done(((bf16[1024,512]{1,0:T(8,128)(2,1)}), bf16[1024,2048]{1,0:T(8,128)(2,1)}) %all-gather.26.cloned.1.call-update) | async-done | bytes 4194320 | tf_op jit(solution)/shard_map/all_gather | solution.py:122
  891.0 84.1 %reduce-scatter.24.cloned.1.call-done = bf16[256,2048]{1,0:T(8,128)(2,1)} async-done(((bf16[2048,2048]{1,0:T(8,128)(2,1)}), bf16[256,2048]{1,0:T(8,128)(2,1)}) %reduce-scatter.24.cloned.1.call-update) | async-done | bytes 1048592 | tf_op jit(solution)/shard_map/reduce_scatter | solution.py:42
  977.9 71.8 %reduce-scatter.26.cloned.1.call-done = bf16[2048,256]{1,0:T(8,128)(2,1)} async-done(((bf16[2048,2048]{1,0:T(8,128)(2,1)}), bf16[2048,256]{1,0:T(8,128)(2,1)}) %reduce-scatter.26.cloned.1.call-update) | async-done | bytes 1048592 | tf_op jit(solution)/shard_map/reduce_scatter | solution.py:42
  1062.1 42.5 %reduce-scatter.20.cloned.1.call-done = bf16[1024,256]{1,0:T(8,128)(2,1)} async-done(((bf16[1024,2048]{1,0:T(8,128)(2,1)}), bf16[1024,256]{1,0:T(8,128)(2,1)}) %reduce-scatter.20.cloned.1.call-update) | async-done | bytes 524304 | tf_op jit(solution)/shard_map/reduce_scatter | solution.py:42
  1106.7 52.5 %reduce-scatter.18.cloned.1.call-done = bf16[256,1024]{1,0:T(8,128)(2,1)} async-done(((bf16[2048,1024]{1,0:T(8,128)(2,1)}), bf16[256,1024]{1,0:T(8,128)(2,1)}) %reduce-scatter.18.cloned.1.call-update) | async-done | bytes 524304 | tf_op jit(solution)/shard_map/reduce_scatter | solution.py:42
  1161.3 76.9 %reduce-scatter.16.cloned.1.call-done = bf16[1024,512]{1,0:T(8,128)(2,1)} async-done(((bf16[1024,2048]{1,0:T(8,128)(2,1)}), bf16[1024,512]{1,0:T(8,128)(2,1)}) %reduce-scatter.16.cloned.1.call-update) | async-done | bytes 1048592 | tf_op jit(solution)/shard_map/reduce_scatter | solution.py:32
  1279.9 38.3 %reduce-scatter.12.cloned.1.call-done = bf16[1024,512]{1,0:T(8,128)(2,1)} async-done(((bf16[1024,2048]{1,0:T(8,128)(2,1)}), bf16[1024,512]{1,0:T(8,128)(2,1)}) %reduce-scatter.12.cloned.1.call-update) | async-done | bytes 1048592 | tf_op jit(solution)/shard_map/reduce_scatter | solution.py:32
  (131 shorter events, 271.2 us)
Async XLA Ops:
  7.2 86.0 %all-gather.10.cloned.1.call-start = ((), (), s32[]{:S(2)}) async-start(), calls=%async_computation.12 | async-start | bytes 5242880 | tf_op jit(solution)/shard_map/all_gather | solution.py:88
  7.9 122.4 %all-gather.12.cloned.1.call-start = ((), (), s32[]{:S(2)}) async-start(), calls=%async_computation.13 | async-start | bytes 4718592 | tf_op jit(solution)/shard_map/all_gather | solution.py:78
  8.7 161.0 %all-gather.14.cloned.1.call-start = ((), (), s32[]{:S(2)}) async-start(), calls=%async_computation.14 | async-start | bytes 4718592 | tf_op jit(solution)/shard_map/all_gather | solution.py:79
  23.3 10.5 all-to-all-start.1
  33.9 29.9 %all-to-all-start = ((bf16[8,128,1024]{2,1,0:T(8,128)(2,1)}), bf16[8,128,1024]{2,1,0:T(8,128)(2,1)S(1)}, u32[]{:S(2)}, u32[]{:S(2)}) async-start(bf16[8,128,1024]{2,1,0:T(8,128)(2,1)} %bitcast.47), calls=%async_computation | async-start | bytes 4194304 | tf_op jit(solution)/shard_map/all_to_all | solution.py:66
  38.1 218.6 %reduce-scatter.10.cloned.1.call-start = ((), (), s32[]{:S(2)}) async-start(), calls=%async_computation.15 | async-start | bytes 5242880 | tf_op jit(solution)/shard_map/reduce_scatter | solution.py:32
  179.7 77.0 %copy-start.3 = (bf16[1024,512]{1,0:T(8,128)(2,1)S(1)}, bf16[1024,512]{1,0:T(8,128)(2,1)}, u32[]{:S(2)}) copy-start(bf16[1024,512]{1,0:T(8,128)(2,1)} %param.11) | copy-start | bytes 3145732
  179.7 133.7 %all-gather.18.cloned.1.call-start = ((), (), s32[]{:S(2)}) async-start(), calls=%async_computation.17 | async-start | bytes 9437184 | tf_op jit(solution)/shard_map/all_gather | solution.py:80
  180.3 216.0 %all-gather.16.cloned.1.call-start = ((), (), s32[]{:S(2)}) async-start(), calls=%async_computation.16 | async-start | bytes 5242880 | tf_op jit(solution)/shard_map/all_gather | solution.py:104
  271.8 179.5 %all-gather.20.cloned.1.call-start = ((), (), s32[]{:S(2)}) async-start(), calls=%async_computation.18 | async-start | bytes 9437184 | tf_op jit(solution)/shard_map/all_gather | solution.py:81
  272.6 261.2 %all-gather.24.cloned.1.call-start = ((), (), s32[]{:S(2)}) async-start(), calls=%async_computation.21 | async-start | bytes 5242880 | tf_op jit(solution)/shard_map/all_gather | solution.py:89
  273.4 317.0 %all-gather.22.cloned.1.call-start = ((), (), s32[]{:S(2)}) async-start(), calls=%async_computation.19 | async-start | bytes 9437184 | tf_op jit(solution)/shard_map/all_gather | solution.py:82
  274.1 442.0 %reduce-scatter.14.cloned.1.call-start = ((), (), s32[]{:S(2)}) async-start(), calls=%async_computation.22 | async-start | bytes 5242880 | tf_op jit(solution)/shard_map/reduce_scatter | solution.py:32
  639.1 77.0 %copy-start.4 = (bf16[1024,512]{1,0:T(8,128)(2,1)S(1)}, bf16[1024,512]{1,0:T(8,128)(2,1)}, u32[]{:S(2)}) copy-start(bf16[1024,512]{1,0:T(8,128)(2,1)} %reduce-scatter.10.cloned.1.call-done) | copy-start | bytes 3145732
  639.1 90.1 %copy-start.5 = (bf16[1024,512]{1,0:T(8,128)(2,1)S(1)}, bf16[1024,512]{1,0:T(8,128)(2,1)}, u32[]{:S(2)}) copy-start(bf16[1024,512]{1,0:T(8,128)(2,1)} %param.14) | copy-start | bytes 3145732
  639.1 172.4 %all-gather.26.cloned.1.call-start = ((), (), s32[]{:S(2)}) async-start(), calls=%async_computation.23 | async-start | bytes 5242880 | tf_op jit(solution)/shard_map/all_gather | solution.py:122
  732.2 156.0 %reduce-scatter.22.cloned.1.call-start = ((), (), s32[]{:S(2)}) async-start(), calls=%async_computation.27 | async-start | bytes 9437184 | tf_op jit(solution)/shard_map/reduce_scatter | solution.py:42
  746.6 228.4 %reduce-scatter.24.cloned.1.call-start = ((), (), s32[]{:S(2)}) async-start(), calls=%async_computation.28 | async-start | bytes 9437184 | tf_op jit(solution)/shard_map/reduce_scatter | solution.py:42
  760.8 288.9 %reduce-scatter.26.cloned.1.call-start = ((), (), s32[]{:S(2)}) async-start(), calls=%async_computation.29 | async-start | bytes 9437184 | tf_op jit(solution)/shard_map/reduce_scatter | solution.py:42
  775.2 329.4 %reduce-scatter.20.cloned.1.call-start = ((), (), s32[]{:S(2)}) async-start(), calls=%async_computation.26 | async-start | bytes 4718592 | tf_op jit(solution)/shard_map/reduce_scatter | solution.py:42
  821.8 337.4 %reduce-scatter.18.cloned.1.call-start = ((), (), s32[]{:S(2)}) async-start(), calls=%async_computation.25 | async-start | bytes 4718592 | tf_op jit(solution)/shard_map/reduce_scatter | solution.py:42
  843.9 394.3 %reduce-scatter.16.cloned.1.call-start = ((), (), s32[]{:S(2)}) async-start(), calls=%async_computation.24 | async-start | bytes 5242880 | tf_op jit(solution)/shard_map/reduce_scatter | solution.py:32
  853.6 464.6 %reduce-scatter.12.cloned.1.call-start = ((), (), s32[]{:S(2)}) async-start(), calls=%async_computation.20 | async-start | bytes 5242880 | tf_op jit(solution)/shard_map/reduce_scatter | solution.py:32
  873.8 178.6 %all-to-all-start.2 = ((bf16[8,128,1024]{2,1,0:T(8,128)(2,1)}), bf16[8,128,1024]{2,1,0:T(8,128)(2,1)S(1)}, u32[]{:S(2)}, u32[]{:S(2)}) async-start(bf16[8,128,1024]{2,1,0:T(8,128)(2,1)} %bitcast.48), calls=%async_computation.6 | async-start | bytes 4194304 | tf_op jit(solution)/shard_map/all_to_all | solution.py:138
  (16 other events, 349.2 us)
Sparse Core Ops, SparseCore 0:
  9.6 83.5 all-gather.9
  95.1 35.2 all-gather.11
  132.2 37.4 all-gather.13
  179.8 76.7 reduce-scatter.9
  258.5 54.8 all-gather.17
  315.5 80.7 all-gather.15
  398.4 52.9 all-gather.19
  453.0 80.7 all-gather.23
  535.8 54.4 all-gather.21
  639.2 76.7 reduce-scatter.13
  732.3 79.1 all-gather.25
  814.8 73.3 reduce-scatter.21
  892.1 82.9 reduce-scatter.23
  978.4 71.2 reduce-scatter.25
  1053.3 51.2 reduce-scatter.19
  1107.8 51.2 reduce-scatter.17
  1161.4 76.7 reduce-scatter.15
  1240.3 77.7 reduce-scatter.11

commit v2 on v1

--- a/solution.py
+++ b/solution.py
@@ -1,9 +1,498 @@
 import jax
 import jax.numpy as jnp
 from jax import lax
+from jax.experimental import pallas as pl
+from jax.experimental.pallas import tpu as pltpu
 from jax.sharding import PartitionSpec as P
 
 EPS = 1e-06
+VMEM_LIMIT = 60 * 2**20
+
+
+MESH = pl.DeviceIdType.MESH
+JOBS = 8
+
+
+def dot_nt(left, right):
+    return lax.dot_general(left, right, (((1,), (1,)), ((), ())), preferred_element_type=jnp.float32)
+
+
+def dot_tn(left, right):
+    return lax.dot_general(left, right, (((0,), (0,)), ((), ())), preferred_element_type=jnp.float32)
+
+
+class Place:
+    def __init__(self):
+        self.f, self.c, self.t = lax.axis_index("fsdp"), lax.axis_index("ctx"), lax.axis_index("tp")
+        self.y, self.k = self.c // 2, self.c % 2
+
+    def at(self, flip_f, flip_y, flip_k):
+        f = self.f + flip_f * (1 - 2 * self.f)
+        y = self.y + flip_y * (1 - 2 * self.y)
+        k = self.k + flip_k * (1 - 2 * self.k)
+        return f, y * 2 + k
+
+    def sibling(self):
+        return (*self.at(0, 0, 1), self.t)
+
+    def first(self):
+        return (*self.at(1 - self.k, self.k, 0), self.t)
+
+    def second(self):
+        return (*self.at(self.k, 1 - self.k, 0), self.t)
+
+    def along(self, t):
+        return (self.f, self.c, t)
+
+    def owner(self, slot, flip_k):
+        alpha, beta = 1 - slot // 2, 1 - slot % 2
+        parity = self.k + flip_k * (1 - 2 * self.k)
+        f, c = self.at(alpha * (1 - parity) + beta * parity, beta * (1 - parity) + alpha * parity, flip_k)
+        return f * 4 + c
+
+
+def remote(source, target, send, recv, device):
+    return pltpu.make_async_remote_copy(
+        src_ref=source, dst_ref=target, send_sem=send, recv_sem=recv, device_id=device, device_id_type=MESH
+    )
+
+
+def greet(place):
+    barrier = pltpu.get_barrier_semaphore()
+    for partner in (place.sibling(), place.first(), place.second()):
+        pl.semaphore_signal(barrier, inc=1, device_id=partner, device_id_type=MESH)
+    for step in range(1, 4):
+        pl.semaphore_signal(barrier, inc=1, device_id=place.along((place.t + step) % 4), device_id_type=MESH)
+    pl.semaphore_wait(barrier, 6)
+
+
+class Gather:
+    def __init__(self, place, full, send, recv, rows, width):
+        self.place, self.full, self.send, self.recv, self.rows, self.width = place, full, send, recv, rows, width
+
+    def copy(self, chunk, shard, way, hop):
+        view = self.full.at[pl.ds(chunk * self.rows, self.rows), pl.ds(pl.multiple_of(shard * self.width, self.width), self.width)]
+        device = self.place.along(self.place.t + 1 - 2 * way)
+        return remote(view, view, self.send.at[chunk, way, hop], self.recv.at[chunk, shard], device)
+
+    def step(self, chunk, hop):
+        t = self.place.t
+
+        @pl.when(t - hop >= 0)
+        def _():
+            if hop > 0:
+                self.copy(chunk, t - hop, 0, hop).wait_recv()
+            if hop < 3:
+                @pl.when(t < 3)
+                def _():
+                    self.copy(chunk, t - hop, 0, hop).start()
+
+        @pl.when(t + hop <= 3)
+        def _():
+            if hop > 0:
+                self.copy(chunk, t + hop, 1, hop).wait_recv()
+            if hop < 3:
+                @pl.when(t > 0)
+                def _():
+                    self.copy(chunk, t + hop, 1, hop).start()
+
+    def finish(self, chunk):
+        t = self.place.t
+        for hop in range(3):
+            @pl.when((t - hop >= 0) & (t < 3))
+            def _():
+                self.copy(chunk, t - hop, 0, hop).wait_send()
+
+            @pl.when((t + hop <= 3) & (t > 0))
+            def _():
+                self.copy(chunk, t + hop, 1, hop).wait_send()
+
+
+class Scatter:
+    def __init__(self, place, slots, send, recv):
+        self.place, self.slots, self.send, self.recv = place, slots, send, recv
+
+    def block(self, step):
+        t = self.place.t
+        low, high = t % 2, t // 2
+        return (3 * (1 - high), 2 - 2 * low + high, 1 + low, t)[step]
+
+    def copy(self, chunk, step):
+        t, block = self.place.t, self.block(step)
+        up = (block > t).astype(jnp.int32)
+        last_down = (block == t - 1).astype(jnp.int32)
+        slot = block + last_down * (4 - block)
+        device = self.place.along(t - 1 + 2 * up)
+        return remote(self.slots.at[chunk, block], self.slots.at[chunk, slot], self.send.at[chunk, step], self.recv.at[chunk, slot], device)
+
+    def arrived(self, chunk, slot):
+        view = self.slots.at[chunk, slot]
+        remote(view, view, self.send.at[chunk, 0], self.recv.at[chunk, slot], self.place.along(self.place.t)).wait_recv()
+
+    def step(self, chunk, step, part):
+        t, block = self.place.t, self.block(step)
+        inner = ((block > t) & (t > 0)) | ((block < t) & (t < 3))
+
+        @pl.when(inner)
+        def _():
+            self.arrived(chunk, block)
+            self.slots[chunk, block] = (part() + self.slots[chunk, block].astype(jnp.float32)).astype(jnp.bfloat16)
+
+        @pl.when(jnp.logical_not(inner))
+        def _():
+            self.slots[chunk, block] = part().astype(jnp.bfloat16)
+
+        self.copy(chunk, step).start()
+
+    def own(self, chunk, held):
+        t = self.place.t
+
+        @pl.when(t > 0)
+        def _():
+            self.arrived(chunk, t)
+            held[...] += self.slots[chunk, t].astype(jnp.float32)
+
+        @pl.when(t < 3)
+        def _():
+            self.arrived(chunk, 4)
+            held[...] += self.slots[chunk, 4].astype(jnp.float32)
+
+    def finish(self, chunk):
+        for step in range(3):
+            self.copy(chunk, step).wait_send()
+
+
+def to_row(column):
+    return jnp.broadcast_to(column, (column.shape[0], 128)).T[:8]
+
+
+def back_kernel(
+    branch_own, cot_in, swi_in, h2_in, da_in, db_in, mixed_in, h1_in, gate_in, mem_in, out_w_in, gate_w_in, xhat_in, gain_ref, gg2_ref,
+    dh1_out, term_out, hd_out, hg_out, hu_out, mo_out, mg_out, gains_out, stats_out,
+    A1, A2, B1, B2, MX, DB, DG, WO, WG, SR, SS, H1S, H1R, H2S, H2R, OS, RZ, GP, MT, TS, XH, HO, GV, GR, GA, SV, SA,
+    load_sem, gate_sem, ag_send, ag_recv, rs_send, rs_recv, sib_send, sib_recv, h1_send, h1_recv, h2_send, h2_recv,
+    out_sem, small_send, small_recv, sib_free, first_free, second_free,
+):
+    place = Place()
+    t = place.t
+    chunk_rows, width = XH.shape
+    slab = OS.shape[0]
+    span = OS.shape[1]
+    cols = span // 2
+    chunks = 4
+
+    loads = {}
+
+    def load(name, source, target, slot):
+        loads[name] = pltpu.make_async_copy(source, target, load_sem.at[slot])
+        loads[name].start()
+
+    def need(*names):
+        for name in names:
+            if name in loads:
+                loads.pop(name).wait()
+
+    own_columns = pl.ds(pl.multiple_of(t * width, width), width)
+    load("branch", branch_own, DB.at[:, own_columns], 0)
+    load("cot", cot_in, A1, 1)
+    load("swi", swi_in, B1, 2)
+    load("h2", h2_in, A2, 3)
+    load("da", da_in, B2, 4)
+    load("out_w", out_w_in, WO, 5)
+    load("gate_w", gate_w_in, WG, 6)
+    load("mixed", mixed_in, MX, 7)
+    greet(place)
+
+    gather = Gather(place, DB, ag_send, ag_recv, chunk_rows, width)
+    scatter = Scatter(place, RZ, rs_send, rs_recv)
+    need("branch")
+    for chunk in range(chunks):
+        gather.step(chunk, 0)
+
+    jobs = [
+        (A1, B1, 0, hd_out, 0), (A1, B1, span, hd_out, span), (A2, B2, 0, hg_out, 0), (A2, B2, span, hg_out, span),
+        (A2, B1, 0, hu_out, 0), (A2, B1, span, hu_out, span), (DB, MX, 0, mo_out, 0), (A1, DG, 0, mg_out, 0),
+    ]
+
+    def tile(job, group, half):
+        left, right, offset = jobs[job][:3]
+        columns = pl.ds(pl.multiple_of(offset + half * cols, cols), cols)
+        return dot_tn(left[:, pl.ds(pl.multiple_of(group * slab, slab), slab)], right[:, columns])
+
+    def each_half(body):
+        @pl.loop(0, 2)
+        def _(half):
+            body(half, pl.ds(pl.multiple_of(half * cols, cols), cols))
+
+    def sib_copy(job, slot):
+        return remote(SS.at[slot], SR.at[job % 2, slot], sib_send.at[slot], sib_recv.at[job, slot], place.sibling())
+
+    def h1_copy(job, slot):
+        return remote(H1S.at[job % 2, slot], H1R.at[job % 2, slot], h1_send.at[job % 2, slot], h1_recv.at[job, slot], place.first())
+
+    def h2_copy(job):
+        return remote(H2S.at[job % 2], H2R.at[job % 2], h2_send.at[job % 2], h2_recv.at[job], place.second())
+
+    def to_sibling(job):
+        if job >= 2:
+            pl.semaphore_wait(sib_free, 1)
+
+        @pl.loop(0, 4)
+        def _(slot):
+            if job >= 1:
+                sib_copy(job - 1, slot).wait_send()
+            group = place.owner(slot, 1)
+
+            def body(half, at):
+                SS[slot, :, at] = tile(job, group, half).astype(jnp.bfloat16)
+
+            each_half(body)
+            sib_copy(job, slot).start()
+
+    def to_first(job):
+        if job >= 2:
+            pl.semaphore_wait(first_free, 1)
+
+        @pl.loop(0, 2)
+        def _(slot):
+            if job >= 2:
+                h1_copy(job - 2, slot).wait_send()
+            group = place.owner(slot, 0)
+            sib_copy(job, slot).wait_recv()
+
+            def body(half, at):
+                H1S[job % 2, slot, :, at] = (tile(job, group, half) + SR[job % 2, slot, :, at].astype(jnp.float32)).astype(jnp.bfloat16)
+
+            each_half(body)
+            h1_copy(job, slot).start()
+
+    def to_second(job):
+        if job >= 2:
+            pl.semaphore_wait(second_free, 1)
+            h2_copy(job - 2).wait_send()
+        group = place.owner(2, 0)
+        sib_copy(job, 2).wait_recv()
+        h1_copy(job, 0).wait_recv()
+
+        def body(half, at):
+            H2S[job % 2, :, at] = (
+                tile(job, group, half) + SR[job % 2, 2, :, at].astype(jnp.float32) + H1R[job % 2, 0, :, at].astype(jnp.float32)
+            ).astype(jnp.bfloat16)
+
+        each_half(body)
+        h2_copy(job).start()
+
+    def out_copy(job):
+        return pltpu.make_async_copy(OS, jobs[job][3].at[:, pl.ds(jobs[job][4], span)], out_sem)
+
+    def to_output(job):
+        group = place.owner(3, 0)
+        sib_copy(job, 3).wait_recv()
+        h1_copy(job, 1).wait_recv()
+        h2_copy(job).wait_recv()
+        if job >= 1:
+            out_copy(job - 1).wait()
+
+        def body(half, at):
+            OS[:, at] = (
+                tile(job, group, half) + SR[job % 2, 3, :, at].astype(jnp.float32)
+                + H1R[job % 2, 1, :, at].astype(jnp.float32) + H2R[job % 2, :, at].astype(jnp.float32)
+            )
+
+        each_half(body)
+        out_copy(job).start()
+        if job + 2 < JOBS:
+            for free, device in ((sib_free, place.sibling()), (first_free, place.first()), (second_free, place.second())):
+                pl.semaphore_signal(free, inc=1, device_id=device, device_id_type=MESH)
+
+    def gate_loads(chunk):
+        rows = pl.ds(chunk * chunk_rows, chunk_rows)
+        return (
+            pltpu.make_async_copy(gate_in.at[rows], GP, gate_sem.at[0]),
+            pltpu.make_async_copy(mem_in.at[rows], MT, gate_sem.at[1]),
+        )
+
+    def term_store(chunk):
+        return pltpu.make_async_copy(TS, term_out.at[pl.ds(chunk * chunk_rows, chunk_rows)], gate_sem.at[2])
+
+    def channels(chunk):
+        rows = pl.ds(chunk * chunk_rows, chunk_rows)
+        for copy in gate_loads(chunk):
+            copy.wait()
+        if chunk > 0:
+            term_store(chunk - 1).wait()
+
+        def body(half, at):
+            d_mixed = dot_nt(DB[rows, :], WO[at, :])
+            pre = GP[:, at]
+            sigma = jax.nn.sigmoid(pre)
+            TS[:, at] = (d_mixed * (pre * sigma)).astype(jnp.bfloat16)
+            DG[rows, at] = (d_mixed * MT[:, at].astype(jnp.float32) * (sigma * (1.0 + pre * (1.0 - sigma)))).astype(jnp.bfloat16)
+
+        each_half(body)
+        term_store(chunk).start()
+        if chunk + 1 < chunks:
+            for copy in gate_loads(chunk + 1):
+                copy.start()
+
+    def first_part(chunk, block):
+        return dot_nt(DG[pl.ds(chunk * chunk_rows, chunk_rows), :], WG[pl.ds(pl.multiple_of(block * width, width), width), :])
+
+    def first_step(chunk, step):
+        scatter.step(chunk, step, lambda: first_part(chunk, scatter.block(step)))
+
+    def own_copies(chunk):
+        rows = pl.ds(chunk * chunk_rows, chunk_rows)
+        return (
+            pltpu.make_async_copy(xhat_in.at[rows], XH, gate_sem.at[3]),
+            pltpu.make_async_copy(HO, dh1_out.at[rows], gate_sem.at[4]),
+        )
+
+    def own_step(chunk):
+        load_xhat, store = own_copies(chunk)
+        load_xhat.start()
+        if chunk > 0:
+            own_copies(chunk - 1)[1].wait()
+        HO[...] = first_part(chunk, t)
+        scatter.own(chunk, HO)
+        load_xhat.wait()
+        product = HO[...] * XH[...]
+        if chunk == 0:
+            GV[0, 0:1] = jnp.sum(product, axis=0, keepdims=True)
+        else:
+            GV[0, 0:1] += jnp.sum(product, axis=0, keepdims=True)
+        SV[:, pl.ds(chunk * chunk_rows, chunk_rows)] = to_row(jnp.sum(product * gain_ref[...], axis=1, keepdims=True))
+        store.start()
+
+    def sum_copy(step):
+        device = (place.sibling(), place.first(), place.second())[step]
+        return remote(GV.at[step], GR.at[step], small_send.at[step], small_recv.at[step], device)
+
+    def to_line(step, what):
+        device = place.along((t + step) % 4)
+        if what == 0:
+            return remote(SV, SA.at[t], small_send.at[2 + step], small_recv.at[2 + step], device)
+        return remote(GV.at[3], GA.at[t], small_send.at[5 + step], small_recv.at[5 + step], device)
+
+    for copy in gate_loads(0):
+        copy.start()
+
+    def events(iteration):
+        if iteration == 0:
+            for chunk in range(2):
+                gather.step(chunk, 1)
+        if iteration == 1:
+            for chunk in range(2, 4):
+                gather.step(chunk, 1)
+            for chunk in range(2):
+                gather.step(chunk, 2)
+        if iteration == 2:
+            for chunk in range(2, 4):
+                gather.step(chunk, 2)
+            gather.step(0, 3)
+            gather.step(1, 3)
+        if iteration == 3:
+            need("out_w", "gate_w")
+            gather.step(2, 3)
+            gather.step(3, 3)
+            for chunk in range(4):
+                channels(chunk)
+                first_step(chunk, 0)
+        if iteration == 4:
+            for chunk in range(4):
+                first_step(chunk, 1)
+        if iteration == 5:
+            for chunk in range(4):
+                first_step(chunk, 2)
+        if iteration == 6:
+            for chunk in range(4):
+                own_step(chunk)
+            for step in range(1, 4):
+                to_line(step, 0).start()
+            GV[0, 1:2] = gg2_ref[...]
+            sum_copy(0).start()
+        if 7 <= iteration < 10:
+            step = iteration - 7
+            sum_copy(step).wait_recv()
+            GV[step + 1] = GV[step] + GR[step]
+            if step < 2:
+                sum_copy(step + 1).start()
+            else:
+                for ahead in range(1, 4):
+                    to_line(ahead, 1).start()
+
+    GV[0] = jnp.zeros_like(GV[0])
+    for iteration in range(JOBS + 2):
+        if iteration >= 2:
+            to_output(iteration - 2)
+            if iteration == 3:
+                load("db", db_in, B1, 2)
+                load("h1", h1_in, A1, 1)
+        if iteration < JOBS:
+            need(*{0: ("cot", "swi"), 2: ("h2", "da"), 4: ("db",), 6: ("mixed",), 7: ("h1",)}.get(iteration, ()))
+            to_sibling(iteration)
+            to_first(iteration)
+        if 1 <= iteration <= JOBS:
+            to_second(iteration - 1)
+        events(iteration)
+
+    for step in range(1, 4):
+        to_line(step, 0).wait()
+        to_line(step, 1).wait()
+    SA[t] = SV[...]
+    GA[t] = GV[3]
+    stats_out[...] = SA[0] + SA[1] + SA[2] + SA[3]
+    gains_out[...] = GA[...]
+    for chunk in range(4):
+        gather.finish(chunk)
+        scatter.finish(chunk)
+    for step in range(3):
+        sum_copy(step).wait_send()
+    for slot in range(4):
+        sib_copy(JOBS - 1, slot).wait_send()
+    for job in (JOBS - 2, JOBS - 1):
+        for slot in range(2):
+            h1_copy(job, slot).wait_send()
+        h2_copy(job).wait_send()
+    term_store(3).wait()
+    own_copies(3)[1].wait()
+    out_copy(JOBS - 1).wait()
+
+
+def back_call(branch_own, cot, swi, h2, da, db, mixed, h1, gate, mem, out_w, gate_w, xhat, gain, gg2):
+    rows, features = cot.shape
+    channels, hidden = mixed.shape[1], swi.shape[1]
+    width, slab, part = features // 4, features // 8, rows // 4
+    bf, f32 = jnp.bfloat16, jnp.float32
+    shape = jax.ShapeDtypeStruct
+    anywhere, vmem = pl.BlockSpec(memory_space=pl.ANY), pl.BlockSpec(memory_space=pltpu.VMEM)
+    dma = pltpu.SemaphoreType.DMA
+    regular = pltpu.SemaphoreType.REGULAR
+    V = pltpu.VMEM
+    macs = rows * features * (3 * hidden + 4 * channels)
+    return pl.pallas_call(
+        back_kernel,
+        name="backward",
+        out_shape=(
+            shape((rows, width), f32), shape((rows, channels), bf), shape((slab, hidden), f32), shape((slab, hidden), f32),
+            shape((slab, hidden), f32), shape((slab, channels), f32), shape((slab, channels), f32), shape((4, 8, width), f32),
+            shape((8, rows), f32),
+        ),
+        in_specs=[anywhere] * 13 + [vmem] * 2,
+        out_specs=(anywhere,) * 7 + (vmem,) * 2,
+        scratch_shapes=[
+            V((rows, features), bf), V((rows, features), bf), V((rows, hidden), bf), V((rows, hidden), bf), V((rows, channels), bf),
+            V((rows, features), bf), V((rows, channels), bf), V((channels, features), bf), V((features, channels), bf),
+            V((2, 4, slab, channels), bf), V((4, slab, channels), bf), V((2, 2, slab, channels), bf), V((2, 2, slab, channels), bf),
+            V((2, slab, channels), bf), V((2, slab, channels), bf), V((slab, channels), f32), V((4, 5, part, width), bf),
+            V((part, channels), f32), V((part, channels), bf), V((part, channels), bf), V((part, width), f32), V((part, width), f32),
+            V((4, 8, width), f32), V((3, 8, width), f32), V((4, 8, width), f32), V((8, rows), f32), V((4, 8, rows), f32),
+            dma((8,)), dma((5,)), dma((4, 2, 3)), dma((4, 4)), dma((4, 3)), dma((4, 5)), dma((4,)), dma((JOBS, 4)), dma((2, 2)),
+            dma((JOBS, 2)), dma((2,)), dma((JOBS,)), dma, dma((9,)), dma((9,)), regular, regular, regular,
+        ],
+        compiler_params=pltpu.CompilerParams(collective_id=1, has_side_effects=True, vmem_limit_bytes=VMEM_LIMIT),
+        cost_estimate=pl.CostEstimate(flops=2 * macs, bytes_accessed=64 * 2**20, transcendentals=rows * channels),
+    )(branch_own, cot, swi, h2, da, db, mixed, h1, gate, mem, out_w, gate_w, xhat, gain, gg2)
 
 
 def silu_grad(values):
@@ -109,41 +598,47 @@
     output = middle + sum_scatter(jnp.dot(swished, down_w, preferred_element_type=jnp.float32))
     block_out = output.astype(jnp.bfloat16)
     d_swished = contract_cols(full_cot, down_w)
-    grad_down = contract_rows(swished, full_cot)
     d_a = (d_swished * up_b * silu_grad(up_a)).astype(jnp.bfloat16)
     d_b = (d_swished * swish_a).astype(jnp.bfloat16)
-    grad_up_a = contract_rows(second, d_a)
-    grad_up_b = contract_rows(second, d_b)
     d_second = sum_scatter(contract_cols(d_a, up_a_w) + contract_cols(d_b, up_b_w))
     scaled = d_second * gain_two
     middle_norm = inv_second * (scaled - unit_second * mean_over(scaled * unit_second, features))
     gain_two_part = jnp.sum(d_second * unit_second, axis=0)
     d_middle = cotangent.astype(jnp.float32) + middle_norm
-    d_branch = lax.all_gather(d_middle.astype(jnp.bfloat16), "tp", axis=1, tiled=True)
-    d_mixed = contract_cols(d_branch, out_w)
-    grad_out = contract_rows(mixed, d_branch)
-    memory_term = d_mixed * activated
-    d_gate = (d_mixed * memory_f * silu_grad(gate_pre)).astype(jnp.bfloat16)
-    grad_gate = contract_rows(first, d_gate)
-    d_first = sum_scatter(contract_cols(d_gate, gate_w))
     unit_own = shard_tokens * inv_first
-    scaled = d_first * gain_one
-    input_norm = inv_first * (scaled - unit_own * mean_over(scaled * unit_own, features))
-    gain_one_part = jnp.sum(d_first * unit_own, axis=0)
+    if lax.axis_size("fsdp") == 2 and lax.axis_size("ctx") == 4 and lax.axis_size("tp") == 4:
+        (
+            d_first, back, grad_down, grad_up_a, grad_up_b, grad_out, grad_gate, gains, stats,
+        ) = back_call(
+            d_middle.astype(jnp.bfloat16), full_cot, swished, second, d_a, d_b, mixed, first, gate_pre, memory_tokens,
+            out_w, gate_w, unit_own, gain_one[None], gain_two_part[None],
+        )
+        input_norm = inv_first * (d_first * gain_one - unit_own * (stats[0][:, None] / features))
+        grad_gain_first, grad_gain_second = gains[:, 0].reshape(features), gains[:, 1].reshape(features)
+        sums = (grad_gate, grad_out.T, grad_up_a, grad_up_b, grad_down.T)
+    else:
+        d_branch = lax.all_gather(d_middle.astype(jnp.bfloat16), "tp", axis=1, tiled=True)
+        d_mixed = contract_cols(d_branch, out_w)
+        back = (d_mixed * activated).astype(jnp.bfloat16)
+        d_gate = (d_mixed * memory_f * silu_grad(gate_pre)).astype(jnp.bfloat16)
+        d_first = sum_scatter(contract_cols(d_gate, gate_w))
+        scaled = d_first * gain_one
+        input_norm = inv_first * (scaled - unit_own * mean_over(scaled * unit_own, features))
+        gain_one_part = jnp.sum(d_first * unit_own, axis=0)
+        parts = lax.psum(jnp.stack([gain_one_part, gain_two_part]), ("fsdp", "ctx"))
+        gains = lax.all_gather(parts, "tp", axis=1, tiled=True)
+        grad_gain_first, grad_gain_second = gains[0], gains[1]
+        sums = (
+            grad_scatter(contract_rows(first, d_gate), 0),
+            grad_scatter(contract_rows(mixed, d_branch), 1),
+            grad_scatter(contract_rows(second, d_a), 0),
+            grad_scatter(contract_rows(second, d_b), 0),
+            grad_scatter(contract_rows(swished, full_cot), 1),
+        )
     grad_inputs = d_middle + input_norm
-    parts = lax.psum(jnp.stack([gain_one_part, gain_two_part]), ("fsdp", "ctx"))
-    gains = lax.all_gather(parts, "tp", axis=1, tiled=True)
-    grad_gain_first, grad_gain_second = gains[0], gains[1]
-    back_rows = memory_term.astype(jnp.bfloat16)[places].reshape(groups, block, memory.shape[1])
+    back_rows = back[places].reshape(groups, block, memory.shape[1])
     returned = lax.all_to_all(back_rows, ("fsdp", "ctx"), split_axis=0, concat_axis=0, tiled=True)
     grad_memory = returned.reshape(rows, memory.shape[1])[jnp.argsort(order)].astype(jnp.float32)
-    sums = (
-        grad_scatter(grad_gate, 0),
-        grad_scatter(grad_out, 1),
-        grad_scatter(grad_up_a, 0),
-        grad_scatter(grad_up_b, 0),
-        grad_scatter(grad_down, 1),
-    )
     return (
         block_out,
         grad_inputs,

time: 1340 us -> 1060 us (0.79)
  waiting for transfers between devices: 961 us -> 542 us
  Pallas kernels: 0 us -> 261 us
  matrix products: 195 us -> 113 us
  blocking collectives: 60.9 us -> 22.2 us
    pallas_call x0 -> x1, Pallas kernels: none -> 261 us  [back_call(): pl.pallas_call(back_kernel, name='backward', out_shape=(shape((rows, widt...]
    reduce_scatter x5 -> x0, waiting for transfers between devices: 257 us -> none  [grad_scatter(): lax.psum_scatter(part.astype(jnp.bfloat16), ('fsdp', 'ctx'), scatter_dime...]
    reduce_scatter x4 -> x3, waiting for transfers between devices: 268 us -> 138 us  [sum_scatter(): lax.psum_scatter(part.astype(jnp.bfloat16), 'tp', scatter_dimension=1, ti...]
    dot_general x5 -> x0, matrix products: 59.8 us -> none  [contract_rows(): lax.dot_general(left, right, (((0,), (0,)), ((), ())), preferred_element_...]
    all_gather x1 -> x0, waiting for transfers between devices: 36.2 us -> none  [shards(): lax.all_gather(d_middle.astype(jnp.bfloat16), 'tp', axis=1, tiled=True)]
    dot_general x5 -> x3, matrix products: 72 us -> 49.3 us  [contract_cols(): lax.dot_general(left, right, (((1,), (1,)), ((), ())), preferred_element_...]
    all_gather x1 -> x0, blocking collectives: 13.9 us -> none  [shards(): gains = lax.all_gather(parts, 'tp', axis=1, tiled=True)]
    psum x1 -> x0, blocking collectives: 13.7 us -> none  [shards(): parts = lax.psum(jnp.stack([gain_one_part, gain_two_part]), ('fsdp', 'ctx'))]
  transfers between devices with their start and end apart: 21 -> 14, of which waited for: 19 -> 12; matrix products, arithmetic and copies ran while one was open for 16% -> 12% of each run, Pallas kernels for 0% -> 25%
where the time goes in v2:
time: 1060 us; the launch traced here: 1050 us
  waiting for transfers between devices  542 us (51%)
  Pallas kernels  261 us (25%)
  matrix products  113 us (11%)
  local copies, waits for them, and re-layouts  45 us (4%)
  other arithmetic  40.7 us (4%)
  blocking collectives  22.2 us (2%)
  between operations  14.5 us (1%)
  starting transfers between devices  13.5 us (1%)
    pallas_call x1, Pallas kernels, back_call(): pl.pallas_call(back_kernel, name='backward', out_shape=(shape((rows, widt...  261 us
    reduce_scatter x3, waiting for transfers between devices, sum_scatter(): lax.psum_scatter(part.astype(jnp.bfloat16), 'tp', scatter_dimension=1, ti...  138 us
    all_gather x1, waiting for transfers between devices, shards(): lax.all_gather((unit_second * gain_two).astype(jnp.bfloat16), 'tp', axis=...  82.9 us
    all_gather x1, waiting for transfers between devices, shards(): lax.all_gather(cotangent, 'tp', axis=1, tiled=True)  67.9 us
    all_gather x1, waiting for transfers between devices, shards(): lax.all_gather(hidden_down, ('fsdp', 'ctx'), axis=1, tiled=True)  56.6 us
    dot_general x3, matrix products, contract_cols(): lax.dot_general(left, right, (((1,), (1,)), ((), ())), preferred_element_...  49.3 us
    all_gather x1, waiting for transfers between devices, shards(): lax.all_gather(hidden_up, ('fsdp', 'ctx'), axis=0, tiled=True)  40.5 us
    all_gather x1, waiting for transfers between devices, shards(): lax.all_gather(hidden_gate, ('fsdp', 'ctx'), axis=0, tiled=True)  39.1 us
  transfers between devices with their start and end apart: 14, of which 12 were waited for; matrix products, arithmetic and copies ran while one was open for 12% of the time, Pallas kernels for 25%

profile of v2, /device:TPU:0, one launch (start us, length us, event | category | flops | bytes accessed | tf_op | source)
XLA Modules:
  0.0 1051.5 jit_solution(5151026947884263302)
XLA Ops:
  14.5 8.8 gather_fusion.1
  43.1 20.7 %all-to-all-done = bf16[8,128,1024]{2,1,0:T(8,128)(2,1)S(1)} async-done(((bf16[8,128,1024]{2,1,0:T(8,128)(2,1)}), bf16[8,128,1024]{2,1,0:T(8,128)(2,1)S(1)}, u32[]{:S(2)}, u32[]{:S(2)}) %all-to-all-start) | async-done | bytes 2097184 | tf_op jit(solution)/shard_map/all_to_all | solution.py:555
  69.1 24.1 %all-gather.9.cloned.1.call-done = bf16[1024,2048]{1,0:T(8,128)(2,1)} async-done(((bf16[1024,512]{1,0:T(8,128)(2,1)}), bf16[1024,2048]{1,0:T(8,128)(2,1)}) %all-gather.9.cloned.1.call-update) | async-done | bytes 4194320 | tf_op jit(solution)/shard_map/all_gather | solution.py:577
  99.7 30.7 %all-gather.11.cloned.1.call-done.gate_w_in = bf16[2048,1024]{1,0:T(8,128)(2,1)} async-done(((bf16[256,1024]{1,0:T(8,128)(2,1)}), bf16[2048,1024]{1,0:T(8,128)(2,1)}) %all-gather.11.cloned.1.call-update) | async-done | bytes 4194320 | tf_op jit(solution)/shard_map/all_gather | solution.py:567
  130.3 11.0 %multiply_convert_fusion.3 = (bf16[1024,1024]{1,0:T(8,128)(2,1)}, f32[1024,1024]{1,0:T(8,128)}) fusion(bf16[1024,1024]{1,0:T(8,128)(2,1)S(1)} %copy-done.7, bf16[1024,2048]{1,0:T(8,128)(2,1)} %fusion.2.h1_in, bf16[2048,1024]{1,0:T(8,128)(2,1)} %all-gather.11.cloned.1.call-done.gate_w_in), kind=kOutput, calls=%fused_computation.16 | convolution fusion | flops 4302307328 | bytes 16777216 | tf_op jit(solution)/shard_map/dot_general | solution.py:583
  141.4 28.3 %all-gather.13.cloned.1.call-done.out_w_in = bf16[1024,2048]{1,0:T(8,128)(2,1)} async-done(((bf16[1024,256]{1,0:T(8,128)(2,1)}), bf16[1024,2048]{1,0:T(8,128)(2,1)}) %all-gather.13.cloned.1.call-update) | async-done | bytes 4194320 | tf_op jit(solution)/shard_map/all_gather | solution.py:568
  169.7 9.3 convolution_convert_fusion.1
  180.4 75.5 %reduce-scatter.4.cloned.1.call-done = bf16[1024,512]{1,0:T(8,128)(2,1)} async-done(((bf16[1024,2048]{1,0:T(8,128)(2,1)}), bf16[1024,512]{1,0:T(8,128)(2,1)}) %reduce-scatter.4.cloned.1.call-update) | async-done | bytes 1048592 | tf_op jit(solution)/shard_map/reduce_scatter | solution.py:521
  257.5 11.2 %psum.14 = f32[1024,1]{0,1:T(1,128)S(1)} all-reduce(f32[1024,1]{0,1:T(1,128)S(1)} %bitcast.50), channel_id=1, replica_groups=mesh['fsdp'=2,'ctx'=4,'tp'=4] {'tp'}, use_global_device_ids=true, to_apply=%region_5.6 | all-reduce | flops 1024 | bytes 8192 | tf_op jit(solution)/shard_map/psum | solution.py:527
  273.6 39.1 %all-gather.17.cloned.1.call-done = bf16[2048,2048]{1,0:T(8,128)(2,1)} async-done(((bf16[256,2048]{1,0:T(8,128)(2,1)}), bf16[2048,2048]{1,0:T(8,128)(2,1)}) %all-gather.17.cloned.1.call-update) | async-done | bytes 8388624 | tf_op jit(solution)/shard_map/all_gather | solution.py:569
  312.7 82.9 %all-gather.15.cloned.1.call-done.h2_in = bf16[1024,2048]{1,0:T(8,128)(2,1)} async-done(((bf16[1024,512]{1,0:T(8,128)(2,1)}), bf16[1024,2048]{1,0:T(8,128)(2,1)}) %all-gather.15.cloned.1.call-update) | async-done | bytes 4194320 | tf_op jit(solution)/shard_map/all_gather | solution.py:593
  395.6 14.5 %fusion.16 = f32[1024,2048]{1,0:T(8,128)} fusion(bf16[1024,2048]{1,0:T(8,128)(2,1)} %all-gather.15.cloned.1.call-done.h2_in, bf16[2048,2048]{1,0:T(8,128)(2,1)} %all-gather.17.cloned.1.call-done), kind=kOutput, calls=%fused_computation.49 | convolution fusion | flops 8589934592 | bytes 20971520 | tf_op jit(solution)/shard_map/dot_general | solution.py:594
  410.1 40.5 %all-gather.19.cloned.1.call-done = bf16[2048,2048]{1,0:T(8,128)(2,1)} async-done(((bf16[256,2048]{1,0:T(8,128)(2,1)}), bf16[2048,2048]{1,0:T(8,128)(2,1)}) %all-gather.19.cloned.1.call-update) | async-done | bytes 8388624 | tf_op jit(solution)/shard_map/all_gather | solution.py:570
  450.6 14.6 %fusion.17 = f32[1024,2048]{1,0:T(8,128)} fusion(bf16[1024,2048]{1,0:T(8,128)(2,1)} %all-gather.15.cloned.1.call-done.h2_in, bf16[2048,2048]{1,0:T(8,128)(2,1)} %all-gather.19.cloned.1.call-done), kind=kOutput, calls=%fused_computation.50 | convolution fusion | flops 8589934592 | bytes 20971520 | tf_op jit(solution)/shard_map/dot_general | solution.py:595
  465.2 67.9 %all-gather.23.cloned.1.call-done.cot_in = bf16[1024,2048]{1,0:T(8,128)(2,1)} async-done(((bf16[1024,512]{1,0:T(8,128)(2,1)}), bf16[1024,2048]{1,0:T(8,128)(2,1)}) %all-gather.23.cloned.1.call-update) | async-done | bytes 4194320 | tf_op jit(solution)/shard_map/all_gather | solution.py:578
  533.0 56.6 %all-gather.21.cloned.1.call-done = bf16[2048,2048]{1,0:T(8,128)(2,1)} async-done(((bf16[2048,256]{1,0:T(8,128)(2,1)}), bf16[2048,2048]{1,0:T(8,128)(2,1)}) %all-gather.21.cloned.1.call-update) | async-done | bytes 8388624 | tf_op jit(solution)/shard_map/all_gather | solution.py:571
  589.6 21.9 %multiply_convert_fusion = (bf16[1024,2048]{1,0:T(8,128)(2,1)}, bf16[1024,2048]{1,0:T(8,128)(2,1)}, bf16[1024,2048]{1,0:T(8,128)(2,1)}) fusion(f32[1024,2048]{1,0:T(8,128)} %fusion.16, f32[1024,2048]{1,0:T(8,128)} %fusion.17, bf16[1024,2048]{1,0:T(8,128)(2,1)} %all-gather.23.cloned.1.call-done.cot_in, bf16[2048,2048]{1,0:T(8,128)(2,1)} %all-gather.21.cloned.1.call-done), kind=kOutput, calls=%fused_computation.11 | convolution fusion | flops 8621391872 | bytes 41943040 | tf_op jit(solution)/shard_map/dot_general | solution.py:515
  611.5 15.2 %fusion.18 = f32[1024,2048]{1,0:T(8,128)} fusion(bf16[1024,2048]{1,0:T(8,128)(2,1)} %get-tuple-element.59.da_in, bf16[2048,2048]{1,0:T(8,128)(2,1)} %all-gather.17.cloned.1.call-done), kind=kOutput, calls=%fused_computation.51 | convolution fusion | flops 8589934592 | bytes 20971520 | tf_op jit(solution)/shard_map/dot_general | solution.py:515
  626.7 12.2 %add_convert_fusion = bf16[1024,2048]{1,0:T(8,128)(2,1)} fusion(f32[1024,2048]{1,0:T(8,128)} %fusion.18, bf16[1024,2048]{1,0:T(8,128)(2,1)S(1)} %copy-done.17, bf16[2048,2048]{1,0:T(8,128)(2,1)S(1)} %copy-done.16), kind=kOutput, calls=%fused_computation.10 | convolution fusion | flops 8594128896 | bytes 25165824 | tf_op jit(solution)/shard_map/dot_general | solution.py:515
  639.0 13.9 %convolution_convert_fusion = bf16[1024,2048]{1,0:T(8,128)(2,1)} fusion(bf16[1024,2048]{1,0:T(8,128)(2,1)} %get-tuple-element.60.swi_in, bf16[2048,2048]{1,0:T(8,128)(2,1)} %all-gather.21.cloned.1.call-done), kind=kOutput, calls=%fused_computation.17 | convolution fusion | flops 8592031744 | bytes 16777216 | tf_op jit(solution)/shard_map/dot_general | solution.py:598
  653.6 62.3 %reduce-scatter.8.cloned.1.call-done = bf16[1024,512]{1,0:T(8,128)(2,1)} async-done(((bf16[1024,2048]{1,0:T(8,128)(2,1)}), bf16[1024,512]{1,0:T(8,128)(2,1)}) %reduce-scatter.8.cloned.1.call-update) | async-done | bytes 1048592 | tf_op jit(solution)/shard_map/reduce_scatter | solution.py:521
  718.6 11.0 %psum.15 = f32[1024,1]{0,1:T(1,128)S(1)} all-reduce(f32[1024,1]{0,1:T(1,128)S(1)} %bitcast.49), channel_id=1, replica_groups=mesh['fsdp'=2,'ctx'=4,'tp'=4] {'tp'}, use_global_device_ids=true, to_apply=%region_9.10 | all-reduce | flops 1024 | bytes 8192 | tf_op jit(solution)/shard_map/psum | solution.py:527
  733.0 261.1 %backward.1 = (f32[1024,512]{1,0:T(8,128)}, bf16[1024,1024]{1,0:T(8,128)(2,1)}, f32[256,2048]{1,0:T(8,128)}, f32[256,2048]{1,0:T(8,128)}, f32[256,2048]{1,0:T(8,...) custom-call(bf16[1024,512]{1,0:T(8,128)(2,1)} %get-tuple-element.64.branch_own, ...), custom_call_target="tpu_custom_call" | custom-call | flops 42949672960 | bytes 67108864 | tf_op jit(solution)/shard_map/backward/pallas_call | solution.py:473
  1022.5 8.8 all-to-all-done.2
  (98 shorter events, 95.1 us)
Async XLA Ops:
  7.2 21.3 %copy-start = (bf16[1024,1024]{1,0:T(8,128)(2,1)S(1)}, bf16[1024,1024]{1,0:T(8,128)(2,1)}, u32[]{:S(2)}) copy-start(bf16[1024,1024]{1,0:T(8,128)(2,1)} %param.12) | copy-start | bytes 6291460
  7.2 86.0 %all-gather.9.cloned.1.call-start = ((), (), s32[]{:S(2)}) async-start(), calls=%async_computation.6 | async-start | bytes 5242880 | tf_op jit(solution)/shard_map/all_gather | solution.py:577
  7.9 122.4 %all-gather.11.cloned.1.call-start = ((), (), s32[]{:S(2)}) async-start(), calls=%async_computation.7 | async-start | bytes 4718592 | tf_op jit(solution)/shard_map/all_gather | solution.py:567
  8.7 161.0 %all-gather.13.cloned.1.call-start = ((), (), s32[]{:S(2)}) async-start(), calls=%async_computation.8 | async-start | bytes 4718592 | tf_op jit(solution)/shard_map/all_gather | solution.py:568
  14.5 19.4 %copy-start.12 = (s32[1024]{0:T(1024)}, s32[1024]{0:T(1024)S(1)}, u32[]{:S(2)}) copy-start(s32[1024]{0:T(1024)S(1)} %get-tuple-element.22) | copy-start | bytes 12292
  23.3 10.5 %all-to-all-start.1 = ((s32[8,1,128]{2,1,0:T(1,128)}), s32[8,1,128]{2,1,0:T(1,128)S(1)}, u32[]{:S(2)}, u32[]{:S(2)}) async-start(s32[8,1,128]{2,1,0:T(1,128)} %bitcast.2), calls=%async_computation.1 | async-start | bytes 8192 | tf_op jit(solution)/shard_map/all_to_all | solution.py:556
  33.9 29.9 %all-to-all-start = ((bf16[8,128,1024]{2,1,0:T(8,128)(2,1)}), bf16[8,128,1024]{2,1,0:T(8,128)(2,1)S(1)}, u32[]{:S(2)}, u32[]{:S(2)}) async-start(bf16[8,128,1024]{2,1,0:T(8,128)(2,1)} %bitcast.38), calls=%async_computation | async-start | bytes 4194304 | tf_op jit(solution)/shard_map/all_to_all | solution.py:555
  38.1 217.8 %reduce-scatter.4.cloned.1.call-start = ((), (), s32[]{:S(2)}) async-start(), calls=%async_computation.9 | async-start | bytes 5242880 | tf_op jit(solution)/shard_map/reduce_scatter | solution.py:521
  69.1 27.3 %copy-start.14 = (f32[2048]{0:T(1024)S(1)}, f32[2048]{0:T(1024)}, u32[]{:S(2)}) copy-start(f32[2048]{0:T(1024)} %param.15) | copy-start | bytes 24580
  96.6 33.7 %copy-start.7 = (bf16[1024,1024]{1,0:T(8,128)(2,1)S(1)}, bf16[1024,1024]{1,0:T(8,128)(2,1)}, u32[]{:S(2)}) copy-start(bf16[1024,1024]{1,0:T(8,128)(2,1)} %gather_fusion.2) | copy-start | bytes 6291460
  179.0 77.0 %copy-start.3 = (bf16[1024,512]{1,0:T(8,128)(2,1)S(1)}, bf16[1024,512]{1,0:T(8,128)(2,1)}, u32[]{:S(2)}) copy-start(bf16[1024,512]{1,0:T(8,128)(2,1)} %param.11) | copy-start | bytes 3145732
  179.0 133.7 %all-gather.17.cloned.1.call-start = ((), (), s32[]{:S(2)}) async-start(), calls=%async_computation.11 | async-start | bytes 9437184 | tf_op jit(solution)/shard_map/all_gather | solution.py:569
  179.6 216.0 %all-gather.15.cloned.1.call-start = ((), (), s32[]{:S(2)}) async-start(), calls=%async_computation.10 | async-start | bytes 5242880 | tf_op jit(solution)/shard_map/all_gather | solution.py:593
  271.3 179.3 %all-gather.19.cloned.1.call-start = ((), (), s32[]{:S(2)}) async-start(), calls=%async_computation.12 | async-start | bytes 9437184 | tf_op jit(solution)/shard_map/all_gather | solution.py:570
  272.1 260.9 %all-gather.23.cloned.1.call-start = ((), (), s32[]{:S(2)}) async-start(), calls=%async_computation.15 | async-start | bytes 5242880 | tf_op jit(solution)/shard_map/all_gather | solution.py:578
  272.8 316.8 %all-gather.21.cloned.1.call-start = ((), (), s32[]{:S(2)}) async-start(), calls=%async_computation.13 | async-start | bytes 9437184 | tf_op jit(solution)/shard_map/all_gather | solution.py:571
  273.6 442.3 %reduce-scatter.8.cloned.1.call-start = ((), (), s32[]{:S(2)}) async-start(), calls=%async_computation.16 | async-start | bytes 5242880 | tf_op jit(solution)/shard_map/reduce_scatter | solution.py:521
  611.5 15.2 %copy-start.16 = (bf16[2048,2048]{1,0:T(8,128)(2,1)S(1)}, bf16[2048,2048]{1,0:T(8,128)(2,1)}, u32[]{:S(2)}) copy-start(bf16[2048,2048]{1,0:T(8,128)(2,1)} %all-gather.19.cloned.1.call-done) | copy-start | bytes 25165828
  611.5 15.2 %copy-start.17 = (bf16[1024,2048]{1,0:T(8,128)(2,1)S(1)}, bf16[1024,2048]{1,0:T(8,128)(2,1)}, u32[]{:S(2)}) copy-start(bf16[1024,2048]{1,0:T(8,128)(2,1)} %get-tuple-element.58.db_in) | copy-start | bytes 12582916
  639.0 378.8 %reduce-scatter.6.cloned.1.call-start = ((), (), s32[]{:S(2)}) async-start(), calls=%async_computation.14 | async-start | bytes 5242880 | tf_op jit(solution)/shard_map/reduce_scatter | solution.py:521
  652.9 63.0 %copy-start.4 = (bf16[1024,512]{1,0:T(8,128)(2,1)S(1)}, bf16[1024,512]{1,0:T(8,128)(2,1)}, u32[]{:S(2)}) copy-start(bf16[1024,512]{1,0:T(8,128)(2,1)} %reduce-scatter.4.cloned.1.call-done) | copy-start | bytes 3145732
  652.9 76.8 %copy-start.6 = (bf16[1024,512]{1,0:T(8,128)(2,1)S(1)}, bf16[1024,512]{1,0:T(8,128)(2,1)}, u32[]{:S(2)}) copy-start(bf16[1024,512]{1,0:T(8,128)(2,1)} %param.14) | copy-start | bytes 3145732
  1001.9 29.4 %all-to-all-start.2 = ((bf16[8,128,1024]{2,1,0:T(8,128)(2,1)}), bf16[8,128,1024]{2,1,0:T(8,128)(2,1)S(1)}, u32[]{:S(2)}, u32[]{:S(2)}) async-start(bf16[8,128,1024]{2,1,0:T(8,128)(2,1)} %bitcast.39), calls=%async_computation.5 | async-start | bytes 4194304 | tf_op jit(solution)/shard_map/all_to_all | solution.py:640
  1005.7 12.1 %copy-start.15 = (f32[512]{0:T(512)S(1)}, f32[512]{0:T(512)}, u32[]{:S(2)}) copy-start(f32[512]{0:T(512)} %dynamic_slice.7) | copy-start | bytes 6148
  (8 other events, 30.6 us)
Sparse Core Ops, SparseCore 0:
  9.6 83.5 all-gather.8
  95.1 35.2 all-gather.10
  132.2 37.4 all-gather.12
  179.1 76.7 reduce-scatter.3
  257.8 54.8 all-gather.16
  314.8 80.7 all-gather.14
  397.6 52.9 all-gather.18
  452.2 80.7 all-gather.22
  535.1 54.4 all-gather.20
  639.1 76.7 reduce-scatter.7
  718.2 106.4 reduce-scatter.5

commit v3 on v2

--- a/solution.py
+++ b/solution.py
@@ -6,7 +6,7 @@
 from jax.sharding import PartitionSpec as P
 
 EPS = 1e-06
-VMEM_LIMIT = 60 * 2**20
+VMEM_LIMIT = 62 * 2**20
 
 
 MESH = pl.DeviceIdType.MESH
@@ -67,13 +67,14 @@
 
 
 class Gather:
-    def __init__(self, place, full, send, recv, rows, width):
-        self.place, self.full, self.send, self.recv, self.rows, self.width = place, full, send, recv, rows, width
+    def __init__(self, place, full, send, recv, rows, width, own=None):
+        self.place, self.full, self.send, self.recv, self.rows, self.width, self.mine = place, full, send, recv, rows, width, own
 
     def copy(self, chunk, shard, way, hop):
         view = self.full.at[pl.ds(chunk * self.rows, self.rows), pl.ds(pl.multiple_of(shard * self.width, self.width), self.width)]
         device = self.place.along(self.place.t + 1 - 2 * way)
-        return remote(view, view, self.send.at[chunk, way, hop], self.recv.at[chunk, shard], device)
+        source = view if hop > 0 or self.mine is None else self.mine.at[pl.ds(chunk * self.rows, self.rows)]
+        return remote(source, view, self.send.at[chunk, way, hop], self.recv.at[chunk, shard], device)
 
     def step(self, chunk, hop):
         t = self.place.t
@@ -111,6 +112,7 @@
 class Scatter:
     def __init__(self, place, slots, send, recv):
         self.place, self.slots, self.send, self.recv = place, slots, send, recv
+        self.ring = slots.shape[0]
 
     def block(self, step):
         t = self.place.t
@@ -118,48 +120,48 @@
         return (3 * (1 - high), 2 - 2 * low + high, 1 + low, t)[step]
 
     def copy(self, chunk, step):
-        t, block = self.place.t, self.block(step)
+        t, block, ring = self.place.t, self.block(step), chunk % self.ring
         up = (block > t).astype(jnp.int32)
         last_down = (block == t - 1).astype(jnp.int32)
         slot = block + last_down * (4 - block)
         device = self.place.along(t - 1 + 2 * up)
-        return remote(self.slots.at[chunk, block], self.slots.at[chunk, slot], self.send.at[chunk, step], self.recv.at[chunk, slot], device)
+        return remote(self.slots.at[ring, block], self.slots.at[ring, slot], self.send.at[chunk, step], self.recv.at[chunk, slot], device)
 
     def arrived(self, chunk, slot):
-        view = self.slots.at[chunk, slot]
+        view = self.slots.at[chunk % self.ring, slot]
         remote(view, view, self.send.at[chunk, 0], self.recv.at[chunk, slot], self.place.along(self.place.t)).wait_recv()
 
-    def step(self, chunk, step, part):
-        t, block = self.place.t, self.block(step)
-        inner = ((block > t) & (t > 0)) | ((block < t) & (t < 3))
-
-        @pl.when(inner)
-        def _():
+    def step(self, chunk, step, part, inside):
+        block, ring = self.block(step), chunk % self.ring
+        value = part(block)
+        if inside:
             self.arrived(chunk, block)
-            self.slots[chunk, block] = (part() + self.slots[chunk, block].astype(jnp.float32)).astype(jnp.bfloat16)
-
-        @pl.when(jnp.logical_not(inner))
-        def _():
-            self.slots[chunk, block] = part().astype(jnp.bfloat16)
-
+            value += self.slots[ring, block].astype(jnp.float32)
+        self.slots[ring, block] = value.astype(jnp.bfloat16)
         self.copy(chunk, step).start()
 
     def own(self, chunk, held):
-        t = self.place.t
+        t, ring = self.place.t, chunk % self.ring
 
         @pl.when(t > 0)
         def _():
             self.arrived(chunk, t)
-            held[...] += self.slots[chunk, t].astype(jnp.float32)
+            held[...] += self.slots[ring, t].astype(jnp.float32)
 
         @pl.when(t < 3)
         def _():
             self.arrived(chunk, 4)
-            held[...] += self.slots[chunk, 4].astype(jnp.float32)
+            held[...] += self.slots[ring, 4].astype(jnp.float32)
 
     def finish(self, chunk):
         for step in range(3):
             self.copy(chunk, step).wait_send()
+
+
+def by_place(place, ends, inside):
+    is_end = (place.t == 0) | (place.t == 3)
+    pl.when(is_end)(ends)
+    pl.when(jnp.logical_not(is_end))(inside)
 
 
 def to_row(column):
@@ -225,16 +227,16 @@
             body(half, pl.ds(pl.multiple_of(half * cols, cols), cols))
 
     def sib_copy(job, slot):
-        return remote(SS.at[slot], SR.at[job % 2, slot], sib_send.at[slot], sib_recv.at[job, slot], place.sibling())
+        return remote(SS.at[slot], SR.at[job % 3, slot], sib_send.at[slot], sib_recv.at[job, slot], place.sibling())
 
     def h1_copy(job, slot):
-        return remote(H1S.at[job % 2, slot], H1R.at[job % 2, slot], h1_send.at[job % 2, slot], h1_recv.at[job, slot], place.first())
+        return remote(H1S.at[job % 2, slot], H1R.at[job % 3, slot], h1_send.at[job % 2, slot], h1_recv.at[job, slot], place.first())
 
     def h2_copy(job):
         return remote(H2S.at[job % 2], H2R.at[job % 2], h2_send.at[job % 2], h2_recv.at[job], place.second())
 
     def to_sibling(job):
-        if job >= 2:
+        if job >= 3:
             pl.semaphore_wait(sib_free, 1)
 
         @pl.loop(0, 4)
@@ -250,7 +252,7 @@
             sib_copy(job, slot).start()
 
     def to_first(job):
-        if job >= 2:
+        if job >= 3:
             pl.semaphore_wait(first_free, 1)
 
         @pl.loop(0, 2)
@@ -261,7 +263,7 @@
             sib_copy(job, slot).wait_recv()
 
             def body(half, at):
-                H1S[job % 2, slot, :, at] = (tile(job, group, half) + SR[job % 2, slot, :, at].astype(jnp.float32)).astype(jnp.bfloat16)
+                H1S[job % 2, slot, :, at] = (tile(job, group, half) + SR[job % 3, slot, :, at].astype(jnp.float32)).astype(jnp.bfloat16)
 
             each_half(body)
             h1_copy(job, slot).start()
@@ -276,7 +278,7 @@
 
         def body(half, at):
             H2S[job % 2, :, at] = (
-                tile(job, group, half) + SR[job % 2, 2, :, at].astype(jnp.float32) + H1R[job % 2, 0, :, at].astype(jnp.float32)
+                tile(job, group, half) + SR[job % 3, 2, :, at].astype(jnp.float32) + H1R[job % 3, 0, :, at].astype(jnp.float32)
             ).astype(jnp.bfloat16)
 
         each_half(body)
@@ -295,14 +297,14 @@
 
         def body(half, at):
             OS[:, at] = (
-                tile(job, group, half) + SR[job % 2, 3, :, at].astype(jnp.float32)
-                + H1R[job % 2, 1, :, at].astype(jnp.float32) + H2R[job % 2, :, at].astype(jnp.float32)
+                tile(job, group, half) + SR[job % 3, 3, :, at].astype(jnp.float32)
+                + H1R[job % 3, 1, :, at].astype(jnp.float32) + H2R[job % 2, :, at].astype(jnp.float32)
             )
 
         each_half(body)
         out_copy(job).start()
-        if job + 2 < JOBS:
-            for free, device in ((sib_free, place.sibling()), (first_free, place.first()), (second_free, place.second())):
+        for ahead, free, device in ((3, sib_free, place.sibling()), (3, first_free, place.first()), (2, second_free, place.second())):
+            if job + ahead < JOBS:
                 pl.semaphore_signal(free, inc=1, device_id=device, device_id_type=MESH)
 
     def gate_loads(chunk):
@@ -338,8 +340,8 @@
     def first_part(chunk, block):
         return dot_nt(DG[pl.ds(chunk * chunk_rows, chunk_rows), :], WG[pl.ds(pl.multiple_of(block * width, width), width), :])
 
-    def first_step(chunk, step):
-        scatter.step(chunk, step, lambda: first_part(chunk, scatter.block(step)))
+    def first_step(chunk, step, inside):
+        scatter.step(chunk, step, lambda block: first_part(chunk, block), inside)
 
     def own_copies(chunk):
         rows = pl.ds(chunk * chunk_rows, chunk_rows)
@@ -377,42 +379,60 @@
     for copy in gate_loads(0):
         copy.start()
 
-    def events(iteration):
-        if iteration == 0:
-            for chunk in range(2):
-                gather.step(chunk, 1)
-        if iteration == 1:
-            for chunk in range(2, 4):
-                gather.step(chunk, 1)
-            for chunk in range(2):
-                gather.step(chunk, 2)
-        if iteration == 2:
-            for chunk in range(2, 4):
-                gather.step(chunk, 2)
+    def steps(ends, inside):
+        def run(pairs, inner):
+            for chunk, step in pairs:
+                first_step(chunk, step, inner)
+
+        by_place(place, lambda: run(ends, False), lambda: run(inside, True))
+
+    def events(iteration, late):
+        if (iteration, late) == (1, 0):
+            gather.step(0, 1)
+            gather.step(1, 1)
+        if (iteration, late) == (1, 1):
+            gather.step(2, 1)
+            gather.step(3, 1)
+        if (iteration, late) == (2, 1):
+            gather.step(0, 2)
+            gather.step(1, 2)
+        if (iteration, late) == (3, 0):
+            gather.step(2, 2)
+            gather.step(3, 2)
+            need("out_w", "gate_w")
             gather.step(0, 3)
+            channels(0)
+        if (iteration, late) == (3, 1):
             gather.step(1, 3)
-        if iteration == 3:
-            need("out_w", "gate_w")
+            channels(1)
+            steps([(0, 0), (1, 0)], [])
+        if (iteration, late) == (4, 0):
             gather.step(2, 3)
+            channels(2)
+        if (iteration, late) == (4, 1):
             gather.step(3, 3)
-            for chunk in range(4):
-                channels(chunk)
-                first_step(chunk, 0)
-        if iteration == 4:
-            for chunk in range(4):
-                first_step(chunk, 1)
-        if iteration == 5:
-            for chunk in range(4):
-                first_step(chunk, 2)
-        if iteration == 6:
-            for chunk in range(4):
-                own_step(chunk)
+            channels(3)
+            steps([(2, 0), (3, 0)], [(0, 0), (1, 0)])
+        if (iteration, late) == (5, 0):
+            steps([(0, 1), (1, 1)], [(2, 0), (3, 0)])
+        if (iteration, late) == (5, 1):
+            steps([(2, 1), (3, 1)], [(0, 1), (1, 1)])
+        if (iteration, late) == (6, 0):
+            steps([(0, 2), (1, 2)], [(2, 1), (3, 1), (0, 2), (1, 2)])
+        if (iteration, late) == (6, 1):
+            steps([(2, 2), (3, 2)], [(2, 2), (3, 2)])
+        if (iteration, late) == (7, 0):
+            own_step(0)
+            own_step(1)
+        if (iteration, late) == (7, 1):
+            own_step(2)
+            own_step(3)
             for step in range(1, 4):
                 to_line(step, 0).start()
             GV[0, 1:2] = gg2_ref[...]
             sum_copy(0).start()
-        if 7 <= iteration < 10:
-            step = iteration - 7
+        if late and 8 <= iteration < 11:
+            step = iteration - 8
             sum_copy(step).wait_recv()
             GV[step + 1] = GV[step] + GR[step]
             if step < 2:
@@ -423,18 +443,20 @@
 
     GV[0] = jnp.zeros_like(GV[0])
     for iteration in range(JOBS + 2):
+        if iteration < JOBS:
+            need(*{0: ("cot", "swi"), 2: ("h2", "da"), 4: ("db",), 6: ("mixed",), 7: ("h1",)}.get(iteration, ()))
+            to_sibling(iteration)
+            to_first(iteration)
+        events(iteration, 0)
+        if 1 <= iteration <= JOBS:
+            to_second(iteration - 1)
         if iteration >= 2:
             to_output(iteration - 2)
             if iteration == 3:
                 load("db", db_in, B1, 2)
                 load("h1", h1_in, A1, 1)
-        if iteration < JOBS:
-            need(*{0: ("cot", "swi"), 2: ("h2", "da"), 4: ("db",), 6: ("mixed",), 7: ("h1",)}.get(iteration, ()))
-            to_sibling(iteration)
-            to_first(iteration)
-        if 1 <= iteration <= JOBS:
-            to_second(iteration - 1)
-        events(iteration)
+        events(iteration, 1)
+    events(10, 1)
 
     for step in range(1, 4):
         to_line(step, 0).wait()
@@ -483,7 +505,7 @@
         scratch_shapes=[
             V((rows, features), bf), V((rows, features), bf), V((rows, hidden), bf), V((rows, hidden), bf), V((rows, channels), bf),
             V((rows, features), bf), V((rows, channels), bf), V((channels, features), bf), V((features, channels), bf),
-            V((2, 4, slab, channels), bf), V((4, slab, channels), bf), V((2, 2, slab, channels), bf), V((2, 2, slab, channels), bf),
+            V((3, 4, slab, channels), bf), V((4, slab, channels), bf), V((2, 2, slab, channels), bf), V((3, 2, slab, channels), bf),
             V((2, slab, channels), bf), V((2, slab, channels), bf), V((slab, channels), f32), V((4, 5, part, width), bf),
             V((part, channels), f32), V((part, channels), bf), V((part, channels), bf), V((part, width), f32), V((part, width), f32),
             V((4, 8, width), f32), V((3, 8, width), f32), V((4, 8, width), f32), V((8, rows), f32), V((4, 8, rows), f32),
@@ -495,6 +517,418 @@
     )(branch_own, cot, swi, h2, da, db, mixed, h1, gate, mem, out_w, gate_w, xhat, gain, gg2)
 
 
+class Spread:
+    def __init__(self, place, index, shard, view, send, recv, local):
+        self.place, self.index, self.shard, self.view, self.send, self.recv = place, index, shard, view, send, recv
+        self.local = local
+
+    def group(self, *flips):
+        f, c = self.place.at(*flips)
+        return f * 4 + c
+
+    def copy(self, group, device, slot):
+        view = self.view(group)
+        source = self.shard if slot < 3 else view
+        return remote(source, view, self.send.at[self.index, slot], self.recv.at[self.index, group], device)
+
+    def routes(self):
+        place = self.place
+        me, both = self.group(0, 0, 0), self.group(1, 1, 0)
+        first, second = self.group(1 - place.k, place.k, 0), self.group(place.k, 1 - place.k, 0)
+        return (
+            (me, place.first()), (me, place.second()), (me, place.sibling()), (second, place.first()), (first, place.sibling()),
+            (second, place.sibling()), (both, place.sibling()),
+        )
+
+    def start(self, slot):
+        group, device = self.routes()[slot]
+        self.copy(group, device, slot).start()
+
+    def arrived(self, group):
+        self.copy(group, self.place.sibling(), 3).wait_recv()
+
+    def stay(self):
+        return pltpu.make_async_copy(self.shard, self.view(self.group(0, 0, 0)), self.local.at[self.index])
+
+    def phase(self, number):
+        routes = self.routes()
+        if number == 0:
+            for slot in range(3):
+                self.start(slot)
+            self.stay().start()
+        if number == 1:
+            self.arrived(routes[3][0])
+            self.start(3)
+            self.start(5)
+            self.arrived(routes[4][0])
+            self.start(4)
+        if number == 2:
+            self.arrived(routes[6][0])
+            self.start(6)
+        if number == 3:
+            for flips in ((0, 0), (0, 1), (1, 0), (1, 1)):
+                self.arrived(self.group(*flips, 1))
+            self.stay().wait()
+
+    def finish(self):
+        for slot, (group, device) in enumerate(self.routes()):
+            self.copy(group, device, slot).wait_send()
+
+
+def to_column(row):
+    return jnp.broadcast_to(row, (128, row.shape[1])).T[:, 0:1]
+
+
+def front_kernel(
+    tokens, cotangent, mem_in, gate_w, out_w, up_a_w, up_b_w, down_w, gain1, gain2,
+    tok_full, cot_full, h2_full, h1_out, gate_out, mixed_out, swi_out, da_out, db_out, gate_w_out, out_w_out, block_out, dx1_out, branch_out,
+    inv_out, gg2_out,
+    WG, WO, WA, WB, WD, Z1, ZN, ZE, XC, CC, H1C, GPS, MXS, MT, SWI, DA, DB, X1, H2O, HO, DHQ, FS, BS, OWN, I2, SV, SA, SV2, SA2,
+    load_sem, store_sem, stage_sem, t_send, t_recv, c_send, c_recv, h_send, h_recv, r_send, r_recv, n_send, n_recv, e_send, e_recv,
+    w_send, w_recv, w_local, s_send, s_recv,
+):
+    place = Place()
+    t = place.t
+    rows, features = tok_full.shape
+    chunk_rows, width = HO.shape
+    channels, hidden = MXS.shape[2], SWI.shape[2]
+    half = channels // 2
+    slab = features // 8
+    own_columns = pl.ds(pl.multiple_of(t * width, width), width)
+
+    def rows_of(chunk):
+        return pl.ds(chunk * chunk_rows, chunk_rows)
+
+    def columns_of(block, size):
+        return pl.ds(pl.multiple_of(block * size, size), size)
+
+    def keep(index, source, target):
+        return pltpu.make_async_copy(source, target, stage_sem.at[index])
+
+    own_tokens = keep(0, tokens, tok_full.at[:, own_columns])
+    own_cot = keep(1, cotangent, cot_full.at[:, own_columns])
+    own_tokens.start()
+    own_cot.start()
+    greet(place)
+
+    tok_gather = Gather(place, tok_full, t_send, t_recv, chunk_rows, width, tokens)
+    cot_gather = Gather(place, cot_full, c_send, c_recv, chunk_rows, width, cotangent)
+    h2_gather = Gather(place, h2_full, h_send, h_recv, chunk_rows, width, H2O)
+    mix_scatter = Scatter(place, Z1, r_send, r_recv)
+    down_scatter = Scatter(place, ZN, n_send, n_recv)
+    up_scatter = Scatter(place, ZE, e_send, e_recv)
+    spreads = [
+        Spread(place, index, shard, view, w_send, w_recv, w_local)
+        for index, (shard, view) in enumerate((
+            (gate_w, lambda group: WG.at[columns_of(group, slab), :]),
+            (out_w, lambda group: WO.at[:, columns_of(group, slab)]),
+            (up_a_w, lambda group: WA.at[columns_of(group, slab), :]),
+            (up_b_w, lambda group: WB.at[columns_of(group, slab), :]),
+            (down_w, lambda group: WD.at[:, columns_of(group, slab)]),
+        ))
+    ]
+
+    def mem_load(chunk):
+        return pltpu.make_async_copy(mem_in.at[rows_of(chunk)], MT, load_sem.at[0])
+
+    def h1_store(chunk):
+        return pltpu.make_async_copy(H1C, h1_out.at[rows_of(chunk)], store_sem.at[0])
+
+    def gate_store(chunk):
+        return pltpu.make_async_copy(GPS, gate_out.at[rows_of(chunk)], store_sem.at[1])
+
+    def mixed_store(chunk):
+        return pltpu.make_async_copy(MXS.at[chunk % 2], mixed_out.at[rows_of(chunk)], store_sem.at[2 + chunk % 2])
+
+    def hidden_stores(chunk):
+        slot = chunk % 2
+        return [
+            pltpu.make_async_copy(source.at[slot], target.at[rows_of(chunk)], store_sem.at[4 + 2 * index + slot])
+            for index, (source, target) in enumerate(((SWI, swi_out), (DA, da_out), (DB, db_out)))
+        ]
+
+    def own_h2_store(chunk):
+        return pltpu.make_async_copy(H2O.at[rows_of(chunk)], h2_full.at[rows_of(chunk), own_columns], stage_sem.at[4 + chunk])
+
+    def small_store(source, target, chunk, index):
+        return pltpu.make_async_copy(source, target.at[rows_of(chunk)], store_sem.at[index])
+
+    def fetch(source, target, index):
+        copy = pltpu.make_async_copy(source, target, load_sem.at[index])
+        copy.start()
+        return copy
+
+    def stat_copy(chunk, step, which):
+        source, target = ((SV, SA), (SV2, SA2))[which]
+        columns = rows_of(chunk)
+        return remote(
+            source.at[:, columns], target.at[t, :, columns], s_send.at[which, chunk, step - 1], s_recv.at[which, chunk, step - 1],
+            place.along((t + step) % 4),
+        )
+
+    def stats(chunk, which):
+        source, target = ((SV, SA), (SV2, SA2))[which]
+        for step in range(1, 4):
+            stat_copy(chunk, step, which).wait_recv()
+        total = source[0:1, rows_of(chunk)]
+        for step in range(1, 4):
+            total = total + target[(t + step) % 4, 0:1, rows_of(chunk)]
+        return to_column(total)
+
+    def memory_unit(chunk):
+        if chunk == 0:
+            own_tokens.wait()
+        load = fetch(tok_full.at[rows_of(chunk)], XC, 1)
+        if chunk > 0:
+            h1_store(chunk - 1).wait()
+        load.wait()
+        square = jnp.zeros((chunk_rows, 1), jnp.float32)
+        for block in range(4):
+            values = XC[:, block * width:(block + 1) * width].astype(jnp.float32)
+            square += jnp.sum(values * values, axis=1, keepdims=True)
+        inverse = lax.rsqrt(square / features + EPS)
+        inv_out[rows_of(chunk)] = inverse
+        for block in range(4):
+            at = slice(block * width, (block + 1) * width)
+            H1C[:, at] = (XC[:, at].astype(jnp.float32) * inverse * gain1[:, at]).astype(jnp.bfloat16)
+        h1_store(chunk).start()
+        mem_load(chunk).wait()
+        if chunk > 0:
+            gate_store(chunk - 1).wait()
+        if chunk > 1:
+            mixed_store(chunk - 2).wait()
+
+        @pl.loop(0, 2)
+        def _(part):
+            at = columns_of(part, half)
+            pre = jnp.dot(H1C[...], WG[:, at], preferred_element_type=jnp.float32)
+            GPS[:, at] = pre
+            MXS[chunk % 2, :, at] = (MT[:, at].astype(jnp.float32) * (pre * jax.nn.sigmoid(pre))).astype(jnp.bfloat16)
+
+        gate_store(chunk).start()
+        mixed_store(chunk).start()
+        if chunk + 1 < 4:
+            mem_load(chunk + 1).start()
+
+    def mix_part(chunk, block):
+        return jnp.dot(MXS[chunk % 2], WO[:, columns_of(block, width)], preferred_element_type=jnp.float32)
+
+    def mix_own(chunk):
+        load = fetch(tokens.at[rows_of(chunk)], OWN, 2)
+        HO[...] = mix_part(chunk, t)
+        mix_scatter.own(chunk, HO)
+        load.wait()
+        middle = OWN[...].astype(jnp.float32) + HO[...]
+        X1[rows_of(chunk)] = middle
+        H2O[rows_of(chunk)] = (middle * gain2[...]).astype(jnp.bfloat16)
+        own_h2_store(chunk).start()
+        SV[:, rows_of(chunk)] = to_row(jnp.sum(middle * middle, axis=1, keepdims=True))
+        mix_scatter.finish(chunk)
+        h2_gather.step(chunk, 0)
+        for step in range(1, 4):
+            stat_copy(chunk, step, 0).start()
+
+    def feed_forward(chunk):
+        own_h2_store(chunk).wait()
+        if chunk == 0:
+            own_cot.wait()
+        loads = [fetch(h2_full.at[rows_of(chunk)], XC, 1), fetch(cot_full.at[rows_of(chunk)], CC, 3)]
+        inverse = lax.rsqrt(stats(chunk, 0) / features + EPS)
+        I2[rows_of(chunk)] = inverse
+        if chunk > 1:
+            for store in hidden_stores(chunk - 2):
+                store.wait()
+        for load in loads:
+            load.wait()
+
+        @pl.loop(0, 4)
+        def _(part):
+            at = columns_of(part, hidden // 4)
+            up_a = jnp.dot(XC[...], WA[:, at], preferred_element_type=jnp.float32) * inverse
+            up_b = jnp.dot(XC[...], WB[:, at], preferred_element_type=jnp.float32) * inverse
+            d_swi = dot_nt(CC[...], WD[at, :])
+            sigma = jax.nn.sigmoid(up_a)
+            swish = up_a * sigma
+            SWI[chunk % 2, :, at] = (swish * up_b).astype(jnp.bfloat16)
+            d_swi = d_swi * inverse
+            DA[chunk % 2, :, at] = (d_swi * up_b * (sigma * (1.0 + up_a * (1.0 - sigma)))).astype(jnp.bfloat16)
+            DB[chunk % 2, :, at] = (d_swi * swish).astype(jnp.bfloat16)
+
+        for store in hidden_stores(chunk):
+            store.start()
+
+    def down_part(chunk, block):
+        return jnp.dot(SWI[chunk % 2], WD[:, columns_of(block, width)], preferred_element_type=jnp.float32)
+
+    def up_part(chunk, block):
+        at = columns_of(block, width)
+        return dot_nt(DA[chunk % 2], WA[at, :]) + dot_nt(DB[chunk % 2], WB[at, :])
+
+    def hidden_own(chunk):
+        if chunk > 0:
+            small_store(BS.at[0], block_out, chunk - 1, 10).wait()
+        HO[...] = up_part(chunk, t)
+        up_scatter.own(chunk, HO)
+        middle = X1[rows_of(chunk)]
+        d_second = HO[...]
+        grads = jnp.sum(d_second * middle, axis=0, keepdims=True)
+        if chunk == 0:
+            gg2_out[...] = grads
+        else:
+            gg2_out[...] += grads
+        scaled = d_second * gain2[...]
+        DHQ[...] = scaled
+        SV2[:, rows_of(chunk)] = to_row(jnp.sum(scaled * middle, axis=1, keepdims=True) * I2[rows_of(chunk)])
+        HO[...] = down_part(chunk, t)
+        down_scatter.own(chunk, HO)
+        BS[0] = (middle + HO[...]).astype(jnp.bfloat16)
+        small_store(BS.at[0], block_out, chunk, 10).start()
+        up_scatter.finish(chunk)
+        down_scatter.finish(chunk)
+        for step in range(1, 4):
+            stat_copy(chunk, step, 1).start()
+
+    def close(chunk):
+        load = fetch(cotangent.at[rows_of(chunk)], OWN, 2)
+        mean = stats(chunk, 1) / features
+        if chunk > 0:
+            small_store(FS, dx1_out, chunk - 1, 11).wait()
+            small_store(BS.at[1], branch_out, chunk - 1, 12).wait()
+        load.wait()
+        unit = X1[rows_of(chunk)] * I2[rows_of(chunk)]
+        total = OWN[...].astype(jnp.float32) + DHQ[...] - unit * mean
+        FS[...] = total
+        BS[1] = total.astype(jnp.bfloat16)
+        small_store(FS, dx1_out, chunk, 11).start()
+        small_store(BS.at[1], branch_out, chunk, 12).start()
+
+    def mix_steps(chunk, ends, inside):
+        def run(steps, inner):
+            for step in steps:
+                mix_scatter.step(chunk, step, lambda block: mix_part(chunk, block), inner)
+
+        by_place(place, lambda: run(ends, False), lambda: run(inside, True))
+
+    def hidden_steps(chunk, ends, inside):
+        def run(steps, inner):
+            for step in steps:
+                up_scatter.step(chunk, step, lambda block: up_part(chunk, block), inner)
+                down_scatter.step(chunk, step, lambda block: down_part(chunk, block), inner)
+
+        by_place(place, lambda: run(ends, False), lambda: run(inside, True))
+
+    def pumps(turn):
+        for index, number in {
+            0: ((0, 0),), 1: ((0, 1), (1, 0)), 2: ((0, 2), (1, 1)), 3: ((0, 3), (1, 2), (2, 0), (1, 3)), 5: ((2, 1), (3, 0)),
+            6: ((2, 2),), 7: ((2, 3), (3, 1), (4, 0)), 8: ((3, 2),), 9: ((3, 3), (4, 1), (4, 2), (4, 3)),
+        }.get(turn, ()):
+            spreads[index].phase(number)
+
+    def hops(chunk, event):
+        if event in (0, 1, 2):
+            tok_gather.step(chunk, event)
+        if event in (3, 4, 5, 6):
+            cot_gather.step(chunk, event - 3)
+        if event in (7, 8):
+            h2_gather.step(chunk, event - 6)
+        if event == 13:
+            close(chunk)
+
+    def light(chunk, event):
+        if event == 4:
+            mix_steps(chunk, (1,), (0,))
+        if event == 5:
+            mix_steps(chunk, (2,), (1, 2))
+        if event == 6:
+            mix_own(chunk)
+        if event == 10:
+            hidden_steps(chunk, (1,), (0,))
+        if event == 11:
+            hidden_steps(chunk, (2,), (1, 2))
+        if event == 12:
+            hidden_own(chunk)
+
+    def heavy(chunk, event):
+        if event == 3:
+            tok_gather.step(chunk, 3)
+            memory_unit(chunk)
+            mix_steps(chunk, (0,), ())
+        if event == 9:
+            h2_gather.step(chunk, 3)
+            feed_forward(chunk)
+            hidden_steps(chunk, (0,), ())
+
+    mem_load(0).start()
+    weight_stores = [
+        pltpu.make_async_copy(WG, gate_w_out, stage_sem.at[2]), pltpu.make_async_copy(WO, out_w_out, stage_sem.at[3]),
+    ]
+    for turn in range(20):
+        pumps(turn)
+        if turn == 3:
+            for store in weight_stores:
+                store.start()
+        for action in (hops, light, heavy):
+            for chunk in range(4):
+                action(chunk, turn - 2 * chunk)
+
+    for store in weight_stores:
+        store.wait()
+    for spread in spreads:
+        spread.finish()
+    for chunk in range(4):
+        for gather in (tok_gather, cot_gather, h2_gather):
+            gather.finish(chunk)
+        for which in range(2):
+            for step in range(1, 4):
+                stat_copy(chunk, step, which).wait_send()
+    h1_store(3).wait()
+    gate_store(3).wait()
+    for chunk in (2, 3):
+        mixed_store(chunk).wait()
+        for store in hidden_stores(chunk):
+            store.wait()
+    small_store(BS.at[0], block_out, 3, 10).wait()
+    small_store(FS, dx1_out, 3, 11).wait()
+    small_store(BS.at[1], branch_out, 3, 12).wait()
+
+
+def front_call(tokens, cotangent, mem, gate_w, out_w, up_a_w, up_b_w, down_w, gain1, gain2):
+    rows, width = tokens.shape
+    features, channels, hidden = 4 * width, mem.shape[1], up_a_w.shape[1]
+    part = rows // 4
+    bf, f32 = jnp.bfloat16, jnp.float32
+    shape = jax.ShapeDtypeStruct
+    anywhere, vmem = pl.BlockSpec(memory_space=pl.ANY), pl.BlockSpec(memory_space=pltpu.VMEM)
+    dma = pltpu.SemaphoreType.DMA
+    V = pltpu.VMEM
+    macs = rows * features * (6 * hidden + 2 * channels)
+    return pl.pallas_call(
+        front_kernel,
+        name="forward",
+        out_shape=(
+            shape((rows, features), bf), shape((rows, features), bf), shape((rows, features), bf), shape((rows, features), bf),
+            shape((rows, channels), f32), shape((rows, channels), bf), shape((rows, hidden), bf), shape((rows, hidden), bf),
+            shape((rows, hidden), bf), shape((features, channels), bf), shape((channels, features), bf), shape((rows, width), bf),
+            shape((rows, width), f32), shape((rows, width), bf), shape((rows, 1), f32), shape((1, width), f32),
+        ),
+        in_specs=[anywhere] * 8 + [vmem] * 2,
+        out_specs=(anywhere,) * 14 + (vmem,) * 2,
+        scratch_shapes=[
+            V((features, channels), bf), V((channels, features), bf), V((features, hidden), bf), V((features, hidden), bf),
+            V((hidden, features), bf), V((2, 5, part, width), bf), V((2, 5, part, width), bf), V((2, 5, part, width), bf),
+            V((part, features), bf), V((part, features), bf), V((part, features), bf), V((part, channels), f32), V((2, part, channels), bf),
+            V((part, channels), bf), V((2, part, hidden), bf), V((2, part, hidden), bf), V((2, part, hidden), bf), V((rows, width), f32),
+            V((rows, width), bf), V((part, width), f32), V((part, width), f32), V((part, width), f32), V((2, part, width), bf),
+            V((part, width), bf), V((rows, 1), f32), V((8, rows), f32), V((4, 8, rows), f32), V((8, rows), f32), V((4, 8, rows), f32),
+            dma((4,)), dma((13,)), dma((8,)), dma((4, 2, 3)), dma((4, 4)), dma((4, 2, 3)), dma((4, 4)), dma((4, 2, 3)), dma((4, 4)),
+            dma((4, 3)), dma((4, 5)), dma((4, 3)), dma((4, 5)), dma((4, 3)), dma((4, 5)), dma((5, 7)), dma((5, 8)), dma((5,)),
+            dma((2, 4, 3)), dma((2, 4, 3)),
+        ],
+        compiler_params=pltpu.CompilerParams(collective_id=2, has_side_effects=True, vmem_limit_bytes=VMEM_LIMIT),
+        cost_estimate=pl.CostEstimate(flops=2 * macs, bytes_accessed=96 * 2**20, transcendentals=rows * (channels + hidden)),
+    )(tokens, cotangent, mem, gate_w, out_w, up_a_w, up_b_w, down_w, gain1, gain2)
+
+
 def silu_grad(values):
     sigma = jax.nn.sigmoid(values)
     return sigma * (1.0 + values * (1.0 - sigma))
@@ -533,35 +967,7 @@
     ).astype(jnp.float32)
 
 
-def shards(
-    tokens,
-    memory,
-    dealing,
-    cotangent,
-    gain_first,
-    gain_second,
-    memory_gate,
-    memory_out,
-    hidden_gate,
-    hidden_up,
-    hidden_down,
-):
-    groups = lax.axis_size(("fsdp", "ctx"))
-    group_index = lax.axis_index(("fsdp", "ctx"))
-    rows = dealing.shape[0]
-    block = rows // groups
-    order = jnp.argsort(dealing)
-    sent_rows = memory[order].reshape(groups, block, memory.shape[1])
-    arrived = lax.all_to_all(sent_rows, ("fsdp", "ctx"), split_axis=0, concat_axis=0, tiled=True)
-    arrived_ids = lax.all_to_all(
-        dealing[order].reshape(groups, block),
-        ("fsdp", "ctx"),
-        split_axis=0,
-        concat_axis=0,
-        tiled=True,
-    )
-    places = arrived_ids.reshape(rows) - group_index * rows
-    memory_tokens = arrived.reshape(rows, memory.shape[1])[jnp.argsort(places)]
+def middle_of(tokens, memory_tokens, cotangent, gain_first, gain_second, memory_gate, memory_out, hidden_gate, hidden_up, hidden_down):
     memory_f = memory_tokens.astype(jnp.float32)
     gathered = (
         lax.all_gather(memory_gate, ("fsdp", "ctx"), axis=0, tiled=True),
@@ -606,35 +1012,80 @@
     gain_two_part = jnp.sum(d_second * unit_second, axis=0)
     d_middle = cotangent.astype(jnp.float32) + middle_norm
     unit_own = shard_tokens * inv_first
-    if lax.axis_size("fsdp") == 2 and lax.axis_size("ctx") == 4 and lax.axis_size("tp") == 4:
-        (
-            d_first, back, grad_down, grad_up_a, grad_up_b, grad_out, grad_gate, gains, stats,
-        ) = back_call(
-            d_middle.astype(jnp.bfloat16), full_cot, swished, second, d_a, d_b, mixed, first, gate_pre, memory_tokens,
-            out_w, gate_w, unit_own, gain_one[None], gain_two_part[None],
-        )
-        input_norm = inv_first * (d_first * gain_one - unit_own * (stats[0][:, None] / features))
-        grad_gain_first, grad_gain_second = gains[:, 0].reshape(features), gains[:, 1].reshape(features)
-        sums = (grad_gate, grad_out.T, grad_up_a, grad_up_b, grad_down.T)
-    else:
-        d_branch = lax.all_gather(d_middle.astype(jnp.bfloat16), "tp", axis=1, tiled=True)
-        d_mixed = contract_cols(d_branch, out_w)
-        back = (d_mixed * activated).astype(jnp.bfloat16)
-        d_gate = (d_mixed * memory_f * silu_grad(gate_pre)).astype(jnp.bfloat16)
-        d_first = sum_scatter(contract_cols(d_gate, gate_w))
-        scaled = d_first * gain_one
-        input_norm = inv_first * (scaled - unit_own * mean_over(scaled * unit_own, features))
-        gain_one_part = jnp.sum(d_first * unit_own, axis=0)
-        parts = lax.psum(jnp.stack([gain_one_part, gain_two_part]), ("fsdp", "ctx"))
-        gains = lax.all_gather(parts, "tp", axis=1, tiled=True)
-        grad_gain_first, grad_gain_second = gains[0], gains[1]
-        sums = (
-            grad_scatter(contract_rows(first, d_gate), 0),
-            grad_scatter(contract_rows(mixed, d_branch), 1),
-            grad_scatter(contract_rows(second, d_a), 0),
-            grad_scatter(contract_rows(second, d_b), 0),
-            grad_scatter(contract_rows(swished, full_cot), 1),
-        )
+    d_branch = lax.all_gather(d_middle.astype(jnp.bfloat16), "tp", axis=1, tiled=True)
+    d_mixed = contract_cols(d_branch, out_w)
+    back = (d_mixed * activated).astype(jnp.bfloat16)
+    d_gate = (d_mixed * memory_f * silu_grad(gate_pre)).astype(jnp.bfloat16)
+    d_first = sum_scatter(contract_cols(d_gate, gate_w))
+    scaled = d_first * gain_one
+    input_norm = inv_first * (scaled - unit_own * mean_over(scaled * unit_own, features))
+    gain_one_part = jnp.sum(d_first * unit_own, axis=0)
+    parts = lax.psum(jnp.stack([gain_one_part, gain_two_part]), ("fsdp", "ctx"))
+    gains = lax.all_gather(parts, "tp", axis=1, tiled=True)
+    grad_gain_first, grad_gain_second = gains[0], gains[1]
+    sums = (
+        grad_scatter(contract_rows(first, d_gate), 0),
+        grad_scatter(contract_rows(mixed, d_branch), 1),
+        grad_scatter(contract_rows(second, d_a), 0),
+        grad_scatter(contract_rows(second, d_b), 0),
+        grad_scatter(contract_rows(swished, full_cot), 1),
+    )
+    return block_out, d_middle, input_norm, back, grad_gain_first, grad_gain_second, sums
+
+
+def middle_on_line(tokens, memory_tokens, cotangent, gain_first, gain_second, memory_gate, memory_out, hidden_gate, hidden_up, hidden_down):
+    width = tokens.shape[1]
+    features = 4 * width
+    own = lambda array: lax.dynamic_slice_in_dim(array, lax.axis_index("tp") * width, width, 0)[None]
+    gain_one, gain_two = own(gain_first), own(gain_second)
+    (
+        _, full_cot, second, first, gate_pre, mixed, swished, d_a, d_b, gate_w, out_w, block_out, d_middle, d_branch, inv_first, gain_two_part,
+    ) = front_call(
+        tokens, cotangent, memory_tokens, memory_gate, memory_out, hidden_gate, hidden_up, hidden_down, gain_first[None], gain_two
+    )
+    unit_own = tokens.astype(jnp.float32) * inv_first
+    d_first, back, grad_down, grad_up_a, grad_up_b, grad_out, grad_gate, gains, stats = back_call(
+        d_branch, full_cot, swished, second, d_a, d_b, mixed, first, gate_pre, memory_tokens, out_w, gate_w, unit_own, gain_one, gain_two_part
+    )
+    input_norm = inv_first * (d_first * gain_one - unit_own * (stats[0][:, None] / features))
+    grad_gain_first, grad_gain_second = gains[:, 0].reshape(features), gains[:, 1].reshape(features)
+    sums = (grad_gate, grad_out.T, grad_up_a, grad_up_b, grad_down.T)
+    return block_out, d_middle, input_norm, back, grad_gain_first, grad_gain_second, sums
+
+
+def shards(
+    tokens,
+    memory,
+    dealing,
+    cotangent,
+    gain_first,
+    gain_second,
+    memory_gate,
+    memory_out,
+    hidden_gate,
+    hidden_up,
+    hidden_down,
+):
+    groups = lax.axis_size(("fsdp", "ctx"))
+    group_index = lax.axis_index(("fsdp", "ctx"))
+    rows = dealing.shape[0]
+    block = rows // groups
+    order = jnp.argsort(dealing)
+    sent_rows = memory[order].reshape(groups, block, memory.shape[1])
+    arrived = lax.all_to_all(sent_rows, ("fsdp", "ctx"), split_axis=0, concat_axis=0, tiled=True)
+    arrived_ids = lax.all_to_all(
+        dealing[order].reshape(groups, block),
+        ("fsdp", "ctx"),
+        split_axis=0,
+        concat_axis=0,
+        tiled=True,
+    )
+    places = arrived_ids.reshape(rows) - group_index * rows
+    memory_tokens = arrived.reshape(rows, memory.shape[1])[jnp.argsort(places)]
+    on_line = lax.axis_size("fsdp") == 2 and lax.axis_size("ctx") == 4 and lax.axis_size("tp") == 4
+    block_out, d_middle, input_norm, back, grad_gain_first, grad_gain_second, sums = (middle_on_line if on_line else middle_of)(
+        tokens, memory_tokens, cotangent, gain_first, gain_second, memory_gate, memory_out, hidden_gate, hidden_up, hidden_down
+    )
     grad_inputs = d_middle + input_norm
     back_rows = back[places].reshape(groups, block, memory.shape[1])
     returned = lax.all_to_all(back_rows, ("fsdp", "ctx"), split_axis=0, concat_axis=0, tiled=True)

time: 1060 us -> 641 us (0.60)
  waiting for transfers between devices: 542 us -> 28.1 us
  Pallas kernels: 261 us -> 515 us
  matrix products: 113 us -> 0 us
  blocking collectives: 22.2 us -> 0 us
  other arithmetic: 40.7 us -> 25.6 us
  between operations: 14.5 us -> 1.19 us
    all_gather x8 -> x0, waiting for transfers between devices: 370 us -> none  [the longest x1 82.9 us: shards(): lax.all_gather((unit_second * gain_two).astype(jnp.bfloat16), 'tp', axis=...]
    pallas_call x0 -> x1, Pallas kernels: none -> 359 us  [front_call(): pl.pallas_call(front_kernel, name='forward', out_shape=(shape((rows, feat...]
    reduce_scatter x3 -> x0, waiting for transfers between devices: 138 us -> none  [sum_scatter(): lax.psum_scatter(part.astype(jnp.bfloat16), 'tp', scatter_dimension=1, ti...]
    dot_general x8 -> x0, matrix products: 113 us -> none  [the longest x3 49.3 us: contract_cols(): lax.dot_general(left, right, (((1,), (1,)), ((), ())), preferred_element_...]
    pallas_call x1, Pallas kernels: 261 us -> 156 us  [back_call(): pl.pallas_call(back_kernel, name='backward', out_shape=(shape((rows, widt...]
    psum x2 -> x0, blocking collectives: 22.2 us -> none  [mean_over(): return lax.psum(jnp.sum(values, axis=-1, keepdims=True), 'tp') / features]
  transfers between devices with their start and end apart: 14 -> 3, of which waited for: 12 -> 2; matrix products, arithmetic and copies ran while one was open for 12% -> 5% of each run, Pallas kernels for 25% -> 0%
where the time goes in v3:
time: 641 us; the launch traced here: 631 us
  Pallas kernels  515 us (80%)
  local copies, waits for them, and re-layouts  48.6 us (8%)
  waiting for transfers between devices  28.1 us (4%)
  other arithmetic  25.6 us (4%)
  starting transfers between devices  13 us (2%)
    pallas_call x1, Pallas kernels, front_call(): pl.pallas_call(front_kernel, name='forward', out_shape=(shape((rows, feat...  359 us
    pallas_call x1, Pallas kernels, back_call(): pl.pallas_call(back_kernel, name='backward', out_shape=(shape((rows, widt...  156 us
    all_to_all x1, waiting for transfers between devices, shards(): lax.all_to_all(sent_rows, ('fsdp', 'ctx'), split_axis=0, concat_axis=0, t...  18.6 us
  transfers between devices with their start and end apart: 3, of which 2 were waited for; matrix products, arithmetic and copies ran while one was open for 5% of the time, Pallas kernels for 0%

profile of v3, /device:TPU:0, one launch (start us, length us, event | category | flops | bytes accessed | tf_op | source)
XLA Modules:
  0.0 631.5 jit_solution(1826028937511923709)
XLA Ops:
  0.7 5.1 sort.45
  5.8 8.8 %gather_fusion.1 = s32[1024]{0:T(1024)} fusion(s32[1024]{0:T(1024)S(1)} %copy-done, s32[1024]{0:T(1024)S(1)} %fusion), kind=kCustom, calls=%fused_computation.1 | custom fusion | bytes 12288 | tf_op jit(solution)/shard_map/gather | solution.py:1077
  14.6 5.2 all-to-all-start.1
  19.8 5.3 gather_fusion
  25.2 4.2 all-to-all-start
  29.3 1.3 dynamic_slice.7
  30.7 1.3 dynamic_slice.6
  32.0 4.4 sort.46
  36.4 18.6 %all-to-all-done = bf16[8,128,1024]{2,1,0:T(8,128)(2,1)S(1)} async-done(((bf16[8,128,1024]{2,1,0:T(8,128)(2,1)}), bf16[8,128,1024]{2,1,0:T(8,128)(2,1)S(1)}, u32[]{:S(2)}, u32[]{:S(2)}) %all-to-all-start) | async-done | bytes 2097184 | tf_op jit(solution)/shard_map/all_to_all | solution.py:1075
  55.0 5.3 gather_fusion.2
  60.4 358.9 %forward.1 = (bf16[1024,2048]{1,0:T(8,128)(2,1)}, bf16[1024,2048]{1,0:T(8,128)(2,1)}, bf16[1024,2048]{1,0:T(8,128)(2,1)}, bf16[1024,2048]{1,0:T(8,128)(2,1)}, f3...) custom-call(bf16[1024,512]{1,0:T(8,128)(2,1)} %tokens.1, ...), custom_call_target="tpu_custom_call" | custom-call | flops 60129542144 | bytes 100663296 | tf_op jit(solution)/shard_map/forward/pallas_call | solution.py:905
  420.5 1.5 convert_multiply_fusion.xhat_in
  422.1 156.1 %backward.1 = (f32[1024,512]{1,0:T(8,128)}, bf16[1024,1024]{1,0:T(8,128)(2,1)}, f32[256,2048]{1,0:T(8,128)}, f32[256,2048]{1,0:T(8,128)}, f32[256,2048]{1,0:T(8,...) custom-call(bf16[1024,512]{1,0:T(8,128)(2,1)} %get-tuple-element.42.branch_own, ...), custom_call_target="tpu_custom_call" | custom-call | flops 42949672960 | bytes 67108864 | tf_op jit(solution)/shard_map/backward/pallas_call | solution.py:495
  578.1 7.9 %gather_fusion.3 = bf16[1024,1024]{1,0:T(8,128)(2,1)} fusion(bf16[1024,1024]{1,0:T(8,128)(2,1)} %get-tuple-element.56, s32[1024]{0:T(1024)S(1)} %broadcast_clamp_fusion), kind=kCustom, calls=%fused_computation.3 | custom fusion | bytes 4198400 | tf_op jit(solution)/shard_map/gather | solution.py:1090
  586.0 3.6 all-to-all-start.2
  589.6 4.4 sort.47
  594.0 2.5 copy.23
  596.5 2.9 copy.24
  600.2 1.5 fusion.3
  601.7 4.1 multiply_add_fusion
  605.8 9.5 %all-to-all-done.2 = bf16[8,128,1024]{2,1,0:T(8,128)(2,1)S(1)} async-done(((bf16[8,128,1024]{2,1,0:T(8,128)(2,1)}), bf16[8,128,1024]{2,1,0:T(8,128)(2,1)S(1)}, u32[]{:S(2)}, u32[]{:S(2)}) %all-to-all-start.2) | async-done | bytes 2097184 | tf_op jit(solution)/shard_map/all_to_all | solution.py:1091
  615.3 5.3 gather_fusion.4
  620.6 4.2 convert_element_type.7
  627.4 1.3 copy.31
  (30 shorter events, 7.0 us)
Async XLA Ops:
  0.6 5.1 copy-start
  5.8 14.0 %copy-start.1 = (bf16[1024,1024]{1,0:T(8,128)(2,1)S(1)}, bf16[1024,1024]{1,0:T(8,128)(2,1)}, u32[]{:S(2)}) copy-start(bf16[1024,1024]{1,0:T(8,128)(2,1)} %param.12) | copy-start | bytes 6291460
  14.6 10.5 %all-to-all-start.1 = ((s32[8,1,128]{2,1,0:T(1,128)}), s32[8,1,128]{2,1,0:T(1,128)S(1)}, u32[]{:S(2)}, u32[]{:S(2)}) async-start(s32[8,1,128]{2,1,0:T(1,128)} %bitcast.2), calls=%async_computation.1 | async-start | bytes 8192 | tf_op jit(solution)/shard_map/all_to_all | solution.py:1076
  25.2 29.9 %all-to-all-start = ((bf16[8,128,1024]{2,1,0:T(8,128)(2,1)}), bf16[8,128,1024]{2,1,0:T(8,128)(2,1)S(1)}, u32[]{:S(2)}, u32[]{:S(2)}) async-start(bf16[8,128,1024]{2,1,0:T(8,128)(2,1)} %bitcast.19), calls=%async_computation | async-start | bytes 4194304 | tf_op jit(solution)/shard_map/all_to_all | solution.py:1075
  60.4 360.2 %copy-start.2 = (bf16[1024,512]{1,0:T(8,128)(2,1)S(1)}, bf16[1024,512]{1,0:T(8,128)(2,1)}, u32[]{:S(2)}) copy-start(bf16[1024,512]{1,0:T(8,128)(2,1)} %tokens.1) | copy-start | bytes 3145732
  586.0 29.3 %all-to-all-start.2 = ((bf16[8,128,1024]{2,1,0:T(8,128)(2,1)}), bf16[8,128,1024]{2,1,0:T(8,128)(2,1)S(1)}, u32[]{:S(2)}, u32[]{:S(2)}) async-start(bf16[8,128,1024]{2,1,0:T(8,128)(2,1)} %bitcast.20), calls=%async_computation.2 | async-start | bytes 4194304 | tf_op jit(solution)/shard_map/all_to_all | solution.py:1091
  596.5 5.2 copy-start.7
  620.6 4.2 copy-start.5
  624.8 1.6 copy-start.6
  624.8 2.6 copy-start.4
  627.4 2.3 copy-start.3

commit v4 on v3

--- a/solution.py
+++ b/solution.py
@@ -57,13 +57,51 @@
     )
 
 
+OTHERS = ((1, 1, 1), (1, 1, 0), (0, 1, 1), (1, 0, 1), (0, 1, 0), (1, 0, 0), (0, 0, 1))
+
+
 def greet(place):
     barrier = pltpu.get_barrier_semaphore()
-    for partner in (place.sibling(), place.first(), place.second()):
-        pl.semaphore_signal(barrier, inc=1, device_id=partner, device_id_type=MESH)
+    for flips in OTHERS:
+        pl.semaphore_signal(barrier, inc=1, device_id=(*place.at(*flips), place.t), device_id_type=MESH)
     for step in range(1, 4):
         pl.semaphore_signal(barrier, inc=1, device_id=place.along((place.t + step) % 4), device_id_type=MESH)
-    pl.semaphore_wait(barrier, 6)
+    pl.semaphore_wait(barrier, 10)
+
+
+class Exchange:
+    def __init__(self, place, source, target, send, recv):
+        self.place, self.source, self.target, self.send, self.recv = place, source, target, send, recv
+        self.me = place.f * 4 + place.c
+
+    def copy(self, index):
+        f, c = self.place.at(*OTHERS[index])
+        group = f * 4 + c
+        out = remote(self.source(group), self.target(self.me), self.send.at[index], self.recv.at[self.me], (f, c, self.place.t))
+        back = remote(self.source(group), self.target(group), self.send.at[index], self.recv.at[group], (f, c, self.place.t))
+        return out, back
+
+    def stay(self):
+        return pltpu.make_async_copy(self.source(self.me), self.target(self.me), self.send.at[7])
+
+    def start(self):
+        for index in range(7):
+            self.copy(index)[0].start()
+        self.stay().start()
+
+    def arrived(self):
+        for index in range(7):
+            self.copy(index)[1].wait_recv()
+        self.stay().wait()
+
+    def finish(self):
+        for index in range(7):
+            self.copy(index)[0].wait_send()
+
+
+def chosen(row, first, count):
+    places = lax.broadcasted_iota(jnp.int32, (count, row.shape[1]), 0) + first
+    return jnp.where(row == places, 1.0, 0.0).astype(jnp.bfloat16)
 
 
 class Gather:
@@ -169,11 +207,11 @@
 
 
 def back_kernel(
-    branch_own, cot_in, swi_in, h2_in, da_in, db_in, mixed_in, h1_in, gate_in, mem_in, out_w_in, gate_w_in, xhat_in, gain_ref, gg2_ref,
-    dh1_out, term_out, hd_out, hg_out, hu_out, mo_out, mg_out, gains_out, stats_out,
-    A1, A2, B1, B2, MX, DB, DG, WO, WG, SR, SS, H1S, H1R, H2S, H2R, OS, RZ, GP, MT, TS, XH, HO, GV, GR, GA, SV, SA,
+    branch_own, cot_in, swi_in, h2_in, da_in, db_in, mixed_in, h1_in, gate_in, mem_in, out_w_in, gate_w_in, xhat_in, gain_ref, gg2_ref, rank_ref, ids_ref,
+    dh1_out, memory_out, term_out, returned, hd_out, hg_out, hu_out, mo_out, mg_out, gains_out, stats_out,
+    A1, A2, B1, B2, MX, DB, DG, WO, WG, SR, SS, H1S, H1R, H2S, H2R, OS, RZ, GP, MT, TS, XH, HO, GV, GR, GA, SV, SA, PLACES,
     load_sem, gate_sem, ag_send, ag_recv, rs_send, rs_recv, sib_send, sib_recv, h1_send, h1_recv, h2_send, h2_recv,
-    out_sem, small_send, small_recv, sib_free, first_free, second_free,
+    out_sem, small_send, small_recv, x_send, x_recv, sib_free, first_free, second_free,
 ):
     place = Place()
     t = place.t
@@ -375,6 +413,48 @@
         if what == 0:
             return remote(SV, SA.at[t], small_send.at[2 + step], small_recv.at[2 + step], device)
         return remote(GV.at[3], GA.at[t], small_send.at[5 + step], small_recv.at[5 + step], device)
+
+    channel_count = span
+    block = DB.shape[0] // 8
+    exchange = Exchange(
+        place,
+        lambda group: B2.at[pl.ds(pl.multiple_of(group * block, block), block), pl.ds(channel_count, channel_count)],
+        lambda group: returned.at[pl.ds(pl.multiple_of(group * block, block), block)],
+        x_send, x_recv,
+    )
+
+    def send_terms():
+        loads["terms"].wait()
+        PLACES[...] = ids_ref[...] - (place.f * 4 + place.c) * DB.shape[0]
+
+        @pl.loop(0, chunks)
+        def _(part):
+            rows = pl.ds(pl.multiple_of(part * chunk_rows, chunk_rows), chunk_rows)
+            total = jnp.zeros((chunk_rows, channel_count), jnp.float32)
+            for chunk in range(chunks):
+                picked = chosen(PLACES[0:1, rows], chunk * chunk_rows, chunk_rows)
+                total += dot_tn(picked, B2[chunk * chunk_rows:(chunk + 1) * chunk_rows, 0:channel_count])
+            B2[rows, channel_count:2 * channel_count] = total.astype(jnp.bfloat16)
+
+        exchange.start()
+
+    def memory_grads():
+        exchange.arrived()
+        copy = pltpu.make_async_copy(returned, A2.at[:, pl.ds(0, channel_count)], load_sem.at[0])
+        copy.start()
+        copy.wait()
+
+        @pl.loop(0, chunks)
+        def _(part):
+            rows = pl.ds(pl.multiple_of(part * chunk_rows, chunk_rows), chunk_rows)
+            total = jnp.zeros((chunk_rows, channel_count), jnp.float32)
+            for chunk in range(chunks):
+                picked = chosen(rank_ref[0:1, rows], chunk * chunk_rows, chunk_rows)
+                total += dot_tn(picked, A2[chunk * chunk_rows:(chunk + 1) * chunk_rows, 0:channel_count])
+            GP[...] = total
+            store = pltpu.make_async_copy(GP, memory_out.at[rows], gate_sem.at[0])
+            store.start()
+            store.wait()
 
     for copy in gate_loads(0):
         copy.start()
@@ -417,7 +497,10 @@
             steps([(0, 1), (1, 1)], [(2, 0), (3, 0)])
         if (iteration, late) == (5, 1):
             steps([(2, 1), (3, 1)], [(0, 1), (1, 1)])
+            term_store(3).wait()
+            load("terms", term_out, B2.at[:, pl.ds(0, channel_count)], 4)
         if (iteration, late) == (6, 0):
+            send_terms()
             steps([(0, 2), (1, 2)], [(2, 1), (3, 1), (0, 2), (1, 2)])
         if (iteration, late) == (6, 1):
             steps([(2, 2), (3, 2)], [(2, 2), (3, 2)])
@@ -431,6 +514,8 @@
                 to_line(step, 0).start()
             GV[0, 1:2] = gg2_ref[...]
             sum_copy(0).start()
+        if (iteration, late) == (8, 0):
+            memory_grads()
         if late and 8 <= iteration < 11:
             step = iteration - 8
             sum_copy(step).wait_recv()
@@ -476,12 +561,12 @@
         for slot in range(2):
             h1_copy(job, slot).wait_send()
         h2_copy(job).wait_send()
-    term_store(3).wait()
+    exchange.finish()
     own_copies(3)[1].wait()
     out_copy(JOBS - 1).wait()
 
 
-def back_call(branch_own, cot, swi, h2, da, db, mixed, h1, gate, mem, out_w, gate_w, xhat, gain, gg2):
+def back_call(branch_own, cot, swi, h2, da, db, mixed, h1, gate, mem, out_w, gate_w, xhat, gain, gg2, rank, ids):
     rows, features = cot.shape
     channels, hidden = mixed.shape[1], swi.shape[1]
     width, slab, part = features // 4, features // 8, rows // 4
@@ -496,12 +581,13 @@
         back_kernel,
         name="backward",
         out_shape=(
-            shape((rows, width), f32), shape((rows, channels), bf), shape((slab, hidden), f32), shape((slab, hidden), f32),
+            shape((rows, width), f32), shape((rows, channels), f32), shape((rows, channels), bf), shape((rows, channels), bf),
+            shape((slab, hidden), f32), shape((slab, hidden), f32),
             shape((slab, hidden), f32), shape((slab, channels), f32), shape((slab, channels), f32), shape((4, 8, width), f32),
             shape((8, rows), f32),
         ),
-        in_specs=[anywhere] * 13 + [vmem] * 2,
-        out_specs=(anywhere,) * 7 + (vmem,) * 2,
+        in_specs=[anywhere] * 13 + [vmem] * 4,
+        out_specs=(anywhere,) * 9 + (vmem,) * 2,
         scratch_shapes=[
             V((rows, features), bf), V((rows, features), bf), V((rows, hidden), bf), V((rows, hidden), bf), V((rows, channels), bf),
             V((rows, features), bf), V((rows, channels), bf), V((channels, features), bf), V((features, channels), bf),
@@ -509,12 +595,12 @@
             V((2, slab, channels), bf), V((2, slab, channels), bf), V((slab, channels), f32), V((4, 5, part, width), bf),
             V((part, channels), f32), V((part, channels), bf), V((part, channels), bf), V((part, width), f32), V((part, width), f32),
             V((4, 8, width), f32), V((3, 8, width), f32), V((4, 8, width), f32), V((8, rows), f32), V((4, 8, rows), f32),
-            dma((8,)), dma((5,)), dma((4, 2, 3)), dma((4, 4)), dma((4, 3)), dma((4, 5)), dma((4,)), dma((JOBS, 4)), dma((2, 2)),
-            dma((JOBS, 2)), dma((2,)), dma((JOBS,)), dma, dma((9,)), dma((9,)), regular, regular, regular,
+            V((8, rows), jnp.int32), dma((8,)), dma((5,)), dma((4, 2, 3)), dma((4, 4)), dma((4, 3)), dma((4, 5)), dma((4,)), dma((JOBS, 4)), dma((2, 2)),
+            dma((JOBS, 2)), dma((2,)), dma((JOBS,)), dma, dma((9,)), dma((9,)), dma((8,)), dma((8,)), regular, regular, regular,
         ],
         compiler_params=pltpu.CompilerParams(collective_id=1, has_side_effects=True, vmem_limit_bytes=VMEM_LIMIT),
         cost_estimate=pl.CostEstimate(flops=2 * macs, bytes_accessed=64 * 2**20, transcendentals=rows * channels),
-    )(branch_own, cot, swi, h2, da, db, mixed, h1, gate, mem, out_w, gate_w, xhat, gain, gg2)
+    )(branch_own, cot, swi, h2, da, db, mixed, h1, gate, mem, out_w, gate_w, xhat, gain, gg2, rank, ids)
 
 
 class Spread:
@@ -580,12 +666,12 @@
 
 
 def front_kernel(
-    tokens, cotangent, mem_in, gate_w, out_w, up_a_w, up_b_w, down_w, gain1, gain2,
-    tok_full, cot_full, h2_full, h1_out, gate_out, mixed_out, swi_out, da_out, db_out, gate_w_out, out_w_out, block_out, dx1_out, branch_out,
-    inv_out, gg2_out,
-    WG, WO, WA, WB, WD, Z1, ZN, ZE, XC, CC, H1C, GPS, MXS, MT, SWI, DA, DB, X1, H2O, HO, DHQ, FS, BS, OWN, I2, SV, SA, SV2, SA2,
+    tokens, cotangent, mem_in, gate_w, out_w, up_a_w, up_b_w, down_w, gain1, gain2, deal_row, deal_column,
+    tok_full, cot_full, h2_full, h1_out, gate_out, mixed_out, swi_out, da_out, db_out, gate_w_out, out_w_out, block_out, dx1_out, branch_out, mem_out,
+    inv_out, gg2_out, rank_out, ids_out,
+    WG, WO, WA, WB, WD, Z1, ZN, ZE, XC, CC, H1C, GPS, MXS, MT, SWI, DA, DB, X1, H2O, HO, DHQ, FS, BS, OWN, I2, SV, SA, SV2, SA2, SENT,
     load_sem, store_sem, stage_sem, t_send, t_recv, c_send, c_recv, h_send, h_recv, r_send, r_recv, n_send, n_recv, e_send, e_recv,
-    w_send, w_recv, w_local, s_send, s_recv,
+    w_send, w_recv, w_local, s_send, s_recv, x_send, x_recv, i_send, i_recv,
 ):
     place = Place()
     t = place.t
@@ -628,8 +714,69 @@
         ))
     ]
 
-    def mem_load(chunk):
-        return pltpu.make_async_copy(mem_in.at[rows_of(chunk)], MT, load_sem.at[0])
+    block = rows // 8
+
+    def quarter(ref, index):
+        return ref.at[index // 2, :, pl.ds(pl.multiple_of((index % 2) * channels, channels), channels)]
+
+    def eighth(ref, group):
+        return ref.at[
+            group // 4, pl.ds(pl.multiple_of((group % 2) * block, block), block),
+            pl.ds(pl.multiple_of(((group // 2) % 2) * channels, channels), channels),
+        ]
+
+    def lanes(ref, group):
+        return ref.at[:, pl.ds(pl.multiple_of(group * block, block), block)]
+
+    rows_exchange = Exchange(place, lambda group: eighth(DA, group), lambda group: eighth(SWI, group), x_send, x_recv)
+    ids_exchange = Exchange(place, lambda group: lanes(SENT, group), lambda group: lanes(ids_out, group), i_send, i_recv)
+
+    def send_rows():
+        loads = [pltpu.make_async_copy(mem_in.at[rows_of(index)], quarter(DB, index), load_sem.at[4 + index]) for index in range(4)]
+        for copy in loads:
+            copy.start()
+        row = deal_row[...]
+        rank = jnp.zeros((1, rows), jnp.float32)
+        for chunk in range(4):
+            rank += jnp.sum(jnp.where(deal_column[rows_of(chunk)] < row, 1.0, 0.0), axis=0, keepdims=True)
+        rank_out[...] = jnp.broadcast_to(rank, (8, rows)).astype(jnp.int32)
+        spots = lax.broadcasted_iota(jnp.int32, (chunk_rows, rows), 1).astype(jnp.float32)
+        ordered = jnp.zeros((1, rows), jnp.float32)
+        for chunk in range(4):
+            column = deal_column[rows_of(chunk)]
+            place_of = jnp.sum(jnp.where(row < column, 1.0, 0.0), axis=1, keepdims=True)
+            ordered += jnp.sum(jnp.where(place_of == spots, column.astype(jnp.float32), 0.0), axis=0, keepdims=True)
+        SENT[...] = jnp.broadcast_to(ordered, (8, rows)).astype(jnp.int32)
+        ids_exchange.start()
+        for copy in loads:
+            copy.wait()
+
+        @pl.loop(0, 4)
+        def _(index):
+            total = jnp.zeros((chunk_rows, channels), jnp.float32)
+            for other in range(4):
+                picked = chosen(rank_out[0:1, rows_of(other)], index * chunk_rows, chunk_rows)
+                total += jnp.dot(picked, quarter(DB, other)[...], preferred_element_type=jnp.float32)
+            quarter(DA, index)[...] = total.astype(jnp.bfloat16)
+
+        rows_exchange.start()
+
+    def mem_store(chunk):
+        return pltpu.make_async_copy(MT, mem_out.at[rows_of(chunk)], load_sem.at[0])
+
+    def take_rows(chunk):
+        if chunk == 0:
+            ids_exchange.arrived()
+            rows_exchange.arrived()
+        else:
+            mem_store(chunk - 1).wait()
+        total = jnp.zeros((chunk_rows, channels), jnp.float32)
+        first = rows_exchange.me * rows + chunk * chunk_rows
+        for other in range(4):
+            picked = chosen(ids_out[0:1, rows_of(other)], first, chunk_rows)
+            total += jnp.dot(picked, quarter(SWI, other)[...], preferred_element_type=jnp.float32)
+        MT[...] = total.astype(jnp.bfloat16)
+        mem_store(chunk).start()
 
     def h1_store(chunk):
         return pltpu.make_async_copy(H1C, h1_out.at[rows_of(chunk)], store_sem.at[0])
@@ -692,7 +839,7 @@
             at = slice(block * width, (block + 1) * width)
             H1C[:, at] = (XC[:, at].astype(jnp.float32) * inverse * gain1[:, at]).astype(jnp.bfloat16)
         h1_store(chunk).start()
-        mem_load(chunk).wait()
+        take_rows(chunk)
         if chunk > 0:
             gate_store(chunk - 1).wait()
         if chunk > 1:
@@ -707,8 +854,6 @@
 
         gate_store(chunk).start()
         mixed_store(chunk).start()
-        if chunk + 1 < 4:
-            mem_load(chunk + 1).start()
 
     def mix_part(chunk, block):
         return jnp.dot(MXS[chunk % 2], WO[:, columns_of(block, width)], preferred_element_type=jnp.float32)
@@ -858,18 +1003,22 @@
             feed_forward(chunk)
             hidden_steps(chunk, (0,), ())
 
-    mem_load(0).start()
     weight_stores = [
         pltpu.make_async_copy(WG, gate_w_out, stage_sem.at[2]), pltpu.make_async_copy(WO, out_w_out, stage_sem.at[3]),
     ]
     for turn in range(20):
         pumps(turn)
+        if turn == 9:
+            rows_exchange.finish()
+            ids_exchange.finish()
         if turn == 3:
             for store in weight_stores:
                 store.start()
         for action in (hops, light, heavy):
-            for chunk in range(4):
+            for chunk in range(4) if action is not heavy else (3, 2, 1, 0):
                 action(chunk, turn - 2 * chunk)
+        if turn == 0:
+            send_rows()
 
     for store in weight_stores:
         store.wait()
@@ -881,6 +1030,7 @@
         for which in range(2):
             for step in range(1, 4):
                 stat_copy(chunk, step, which).wait_send()
+    mem_store(3).wait()
     h1_store(3).wait()
     gate_store(3).wait()
     for chunk in (2, 3):
@@ -892,7 +1042,7 @@
     small_store(BS.at[1], branch_out, 3, 12).wait()
 
 
-def front_call(tokens, cotangent, mem, gate_w, out_w, up_a_w, up_b_w, down_w, gain1, gain2):
+def front_call(tokens, cotangent, mem, gate_w, out_w, up_a_w, up_b_w, down_w, gain1, gain2, deal_row, deal_column):
     rows, width = tokens.shape
     features, channels, hidden = 4 * width, mem.shape[1], up_a_w.shape[1]
     part = rows // 4
@@ -909,10 +1059,11 @@
             shape((rows, features), bf), shape((rows, features), bf), shape((rows, features), bf), shape((rows, features), bf),
             shape((rows, channels), f32), shape((rows, channels), bf), shape((rows, hidden), bf), shape((rows, hidden), bf),
             shape((rows, hidden), bf), shape((features, channels), bf), shape((channels, features), bf), shape((rows, width), bf),
-            shape((rows, width), f32), shape((rows, width), bf), shape((rows, 1), f32), shape((1, width), f32),
+            shape((rows, width), f32), shape((rows, width), bf), shape((rows, channels), bf), shape((rows, 1), f32), shape((1, width), f32),
+            shape((8, rows), jnp.int32), shape((8, rows), jnp.int32),
         ),
-        in_specs=[anywhere] * 8 + [vmem] * 2,
-        out_specs=(anywhere,) * 14 + (vmem,) * 2,
+        in_specs=[anywhere] * 8 + [vmem] * 4,
+        out_specs=(anywhere,) * 15 + (vmem,) * 4,
         scratch_shapes=[
             V((features, channels), bf), V((channels, features), bf), V((features, hidden), bf), V((features, hidden), bf),
             V((hidden, features), bf), V((2, 5, part, width), bf), V((2, 5, part, width), bf), V((2, 5, part, width), bf),
@@ -920,13 +1071,13 @@
             V((part, channels), bf), V((2, part, hidden), bf), V((2, part, hidden), bf), V((2, part, hidden), bf), V((rows, width), f32),
             V((rows, width), bf), V((part, width), f32), V((part, width), f32), V((part, width), f32), V((2, part, width), bf),
             V((part, width), bf), V((rows, 1), f32), V((8, rows), f32), V((4, 8, rows), f32), V((8, rows), f32), V((4, 8, rows), f32),
-            dma((4,)), dma((13,)), dma((8,)), dma((4, 2, 3)), dma((4, 4)), dma((4, 2, 3)), dma((4, 4)), dma((4, 2, 3)), dma((4, 4)),
+            V((8, rows), jnp.int32), dma((8,)), dma((13,)), dma((8,)), dma((4, 2, 3)), dma((4, 4)), dma((4, 2, 3)), dma((4, 4)), dma((4, 2, 3)), dma((4, 4)),
             dma((4, 3)), dma((4, 5)), dma((4, 3)), dma((4, 5)), dma((4, 3)), dma((4, 5)), dma((5, 7)), dma((5, 8)), dma((5,)),
-            dma((2, 4, 3)), dma((2, 4, 3)),
+            dma((2, 4, 3)), dma((2, 4, 3)), dma((8,)), dma((8,)), dma((8,)), dma((8,)),
         ],
         compiler_params=pltpu.CompilerParams(collective_id=2, has_side_effects=True, vmem_limit_bytes=VMEM_LIMIT),
         cost_estimate=pl.CostEstimate(flops=2 * macs, bytes_accessed=96 * 2**20, transcendentals=rows * (channels + hidden)),
-    )(tokens, cotangent, mem, gate_w, out_w, up_a_w, up_b_w, down_w, gain1, gain2)
+    )(tokens, cotangent, mem, gate_w, out_w, up_a_w, up_b_w, down_w, gain1, gain2, deal_row, deal_column)
 
 
 def silu_grad(values):
@@ -1033,24 +1184,30 @@
     return block_out, d_middle, input_norm, back, grad_gain_first, grad_gain_second, sums
 
 
-def middle_on_line(tokens, memory_tokens, cotangent, gain_first, gain_second, memory_gate, memory_out, hidden_gate, hidden_up, hidden_down):
+def middle_on_line(
+    tokens, memory, dealing, cotangent, gain_first, gain_second, memory_gate, memory_out, hidden_gate, hidden_up, hidden_down
+):
     width = tokens.shape[1]
     features = 4 * width
     own = lambda array: lax.dynamic_slice_in_dim(array, lax.axis_index("tp") * width, width, 0)[None]
     gain_one, gain_two = own(gain_first), own(gain_second)
     (
-        _, full_cot, second, first, gate_pre, mixed, swished, d_a, d_b, gate_w, out_w, block_out, d_middle, d_branch, inv_first, gain_two_part,
+        _, full_cot, second, first, gate_pre, mixed, swished, d_a, d_b, gate_w, out_w, block_out, d_middle, d_branch, memory_tokens,
+        inv_first, gain_two_part, rank, ids,
     ) = front_call(
-        tokens, cotangent, memory_tokens, memory_gate, memory_out, hidden_gate, hidden_up, hidden_down, gain_first[None], gain_two
+        tokens, cotangent, memory, memory_gate, memory_out, hidden_gate, hidden_up, hidden_down, gain_first[None], gain_two,
+        dealing[None], dealing[:, None],
     )
     unit_own = tokens.astype(jnp.float32) * inv_first
-    d_first, back, grad_down, grad_up_a, grad_up_b, grad_out, grad_gate, gains, stats = back_call(
-        d_branch, full_cot, swished, second, d_a, d_b, mixed, first, gate_pre, memory_tokens, out_w, gate_w, unit_own, gain_one, gain_two_part
-    )
-    input_norm = inv_first * (d_first * gain_one - unit_own * (stats[0][:, None] / features))
-    grad_gain_first, grad_gain_second = gains[:, 0].reshape(features), gains[:, 1].reshape(features)
-    sums = (grad_gate, grad_out.T, grad_up_a, grad_up_b, grad_down.T)
-    return block_out, d_middle, input_norm, back, grad_gain_first, grad_gain_second, sums
+    d_first, grad_memory, _, _, grad_down, grad_up_a, grad_up_b, grad_out, grad_gate, gains, stats = back_call(
+        d_branch, full_cot, swished, second, d_a, d_b, mixed, first, gate_pre, memory_tokens, out_w, gate_w, unit_own, gain_one,
+        gain_two_part, rank, ids,
+    )
+    grad_inputs = d_middle + inv_first * (d_first * gain_one - unit_own * (stats[0][:, None] / features))
+    return (
+        block_out, grad_inputs, grad_memory, gains[:, 0].reshape(features), gains[:, 1].reshape(features), grad_gate, grad_out.T,
+        grad_up_a, grad_up_b, grad_down.T,
+    )
 
 
 def shards(
@@ -1066,6 +1223,10 @@
     hidden_up,
     hidden_down,
 ):
+    if lax.axis_size("fsdp") == 2 and lax.axis_size("ctx") == 4 and lax.axis_size("tp") == 4:
+        return middle_on_line(
+            tokens, memory, dealing, cotangent, gain_first, gain_second, memory_gate, memory_out, hidden_gate, hidden_up, hidden_down
+        )
     groups = lax.axis_size(("fsdp", "ctx"))
     group_index = lax.axis_index(("fsdp", "ctx"))
     rows = dealing.shape[0]
@@ -1082,8 +1243,7 @@
     )
     places = arrived_ids.reshape(rows) - group_index * rows
     memory_tokens = arrived.reshape(rows, memory.shape[1])[jnp.argsort(places)]
-    on_line = lax.axis_size("fsdp") == 2 and lax.axis_size("ctx") == 4 and lax.axis_size("tp") == 4
-    block_out, d_middle, input_norm, back, grad_gain_first, grad_gain_second, sums = (middle_on_line if on_line else middle_of)(
+    block_out, d_middle, input_norm, back, grad_gain_first, grad_gain_second, sums = middle_of(
         tokens, memory_tokens, cotangent, gain_first, gain_second, memory_gate, memory_out, hidden_gate, hidden_up, hidden_down
     )
     grad_inputs = d_middle + input_norm

time: 641 us -> 605 us (0.944)
  Pallas kernels: 515 us -> 566 us
  waiting for transfers between devices: 28.1 us -> 0 us
  local copies, waits for them, and re-layouts: 48.6 us -> 21.8 us
  other arithmetic: 25.6 us -> 7.61 us
  starting transfers between devices: 13 us -> 0 us
    gather x5 -> x0, local copies, waits for them, and re-layouts: 32.7 us -> none  [the longest x1 8.84 us: shards(): dealing[order].reshape(groups, block)]
    all_to_all x3 -> x0, waiting for transfers between devices: 28.1 us -> none  [the longest x1 18.6 us: shards(): lax.all_to_all(sent_rows, ('fsdp', 'ctx'), split_axis=0, concat_axis=0, t...]
    pallas_call x1, Pallas kernels: 359 us -> 384 us  [front_call(): pl.pallas_call(front_kernel, name='forward', out_shape=(shape((rows, feat...]
    pallas_call x1, Pallas kernels: 156 us -> 181 us  [back_call(): pl.pallas_call(back_kernel, name='backward', out_shape=(shape((rows, widt...]
    sort x3 -> x0, other arithmetic: 13.8 us -> none  [the longest x1 5.11 us: shards(): order = jnp.argsort(dealing)]
    all_to_all x3 -> x0, starting transfers between devices: 13 us -> none  [the longest x1 5.17 us: shards(): lax.all_to_all(dealing[order].reshape(groups, block), ('fsdp', 'ctx'), sp...]
    unnamed x22 -> x21, local copies, waits for them, and re-layouts: 11.7 us -> 15.8 us
  transfers between devices with their start and end apart: 3 -> 0, of which waited for: 2 -> 0; matrix products, arithmetic and copies ran while one was open for 5% -> 0% of each run, Pallas kernels for 0% -> 0%
where the time goes in v4:
time: 605 us; the launch traced here: 596 us
  Pallas kernels  566 us (94%)
  local copies, waits for them, and re-layouts  21.8 us (4%)
  other arithmetic  7.61 us (1%)
    pallas_call x1, Pallas kernels, front_call(): pl.pallas_call(front_kernel, name='forward', out_shape=(shape((rows, feat...  384 us
    pallas_call x1, Pallas kernels, back_call(): pl.pallas_call(back_kernel, name='backward', out_shape=(shape((rows, widt...  181 us
    unnamed x21, local copies, waits for them, and re-layouts  15.8 us

profile of v4, /device:TPU:0, one launch (start us, length us, event | category | flops | bytes accessed | tf_op | source)
XLA Modules:
  0.0 596.1 jit_solution(795074569098900612)
XLA Ops:
  0.6 1.3 dynamic_slice.7
  2.0 1.3 dynamic_slice.6
  3.3 1.7 copy.23.deal_column
  5.0 384.3 %forward.1 = (bf16[1024,2048]{1,0:T(8,128)(2,1)}, bf16[1024,2048]{1,0:T(8,128)(2,1)}, bf16[1024,2048]{1,0:T(8,128)(2,1)}, bf16[1024,2048]{1,0:T(8,128)(2,1)}, f3...) custom-call(bf16[1024,512]{1,0:T(8,128)(2,1)} %tokens.1, ...), custom_call_target="tpu_custom_call" | custom-call | flops 60129542144 | bytes 100663296 | tf_op jit(solution)/shard_map/forward/pallas_call | solution.py:1055
  389.4 1.2 reduce
  390.6 0.0 copy-done
  390.6 1.5 convert_multiply_fusion.xhat_in
  392.2 181.2 %backward.1 = (f32[1024,512]{1,0:T(8,128)}, f32[1024,1024]{1,0:T(8,128)}, bf16[1024,1024]{1,0:T(8,128)(2,1)}, bf16[1024,1024]{1,0:T(8,128)(2,1)}, f32[256,2048]{...) custom-call(bf16[1024,512]{1,0:T(8,128)(2,1)} %get-tuple-element.40., ...), custom_call_target="tpu_custom_call" | custom-call | flops 42949672960 | bytes 67108864 | tf_op jit(solution)/shard_map/backward/pallas_call | solution.py:580
  573.4 0.8 slice_multiply_fusion
  574.1 0.0 copy-done.6
  574.1 4.1 multiply_add_fusion
  578.2 1.6 fusion
  579.8 2.5 copy.24
  582.4 0.0 copy-done.3
  582.4 1.8 copy.25
  584.2 0.0 copy-done.4
  584.2 1.0 copy.31
  585.2 4.9 copy.32
  590.0 0.0 copy-done.5
  590.0 1.0 copy.33
  591.0 1.0 copy-done.2
  592.0 1.3 copy.34
  593.3 1.0 copy-done.1
  594.4 1.3 copy.35
  (7 shorter events, 0.0 us)
Async XLA Ops:
  5.0 385.6 %copy-start = (bf16[1024,512]{1,0:T(8,128)(2,1)S(1)}, bf16[1024,512]{1,0:T(8,128)(2,1)}, u32[]{:S(2)}) copy-start(bf16[1024,512]{1,0:T(8,128)(2,1)} %tokens.1) | copy-start | bytes 3145732
  392.2 182.0 %copy-start.6 = (f32[512]{0:T(512)S(1)}, f32[512]{0:T(512)}, u32[]{:S(2)}) copy-start(f32[512]{0:T(512)} %dynamic_slice.7) | copy-start | bytes 6148
  578.2 4.2 copy-start.3
  582.4 1.8 copy-start.4
  585.2 4.9 copy-start.5
  590.0 2.0 copy-start.2
  592.0 2.3 copy-start.1

commit v5 on v4

--- a/solution.py
+++ b/solution.py
@@ -1,3 +1,5 @@
+import functools
+
 import jax
 import jax.numpy as jnp
 from jax import lax
@@ -207,11 +209,11 @@
 
 
 def back_kernel(
-    branch_own, cot_in, swi_in, h2_in, da_in, db_in, mixed_in, h1_in, gate_in, mem_in, out_w_in, gate_w_in, xhat_in, gain_ref, gg2_ref, rank_ref, ids_ref,
-    dh1_out, memory_out, term_out, returned, hd_out, hg_out, hu_out, mo_out, mg_out, gains_out, stats_out,
-    A1, A2, B1, B2, MX, DB, DG, WO, WG, SR, SS, H1S, H1R, H2S, H2R, OS, RZ, GP, MT, TS, XH, HO, GV, GR, GA, SV, SA, PLACES,
+    branch_own, cot_in, swi_in, h2_in, da_in, db_in, mixed_in, h1_in, gate_in, mem_in, out_w_in, gate_w_in, xhat_in, gain_ref, gg2_ref, rank_ref, ids_ref, down_in,
+    dh1_out, down_out, memory_out, term_out, returned, hd_out, hg_out, hu_out, mo_out, mg_out, gains_out, stats_out,
+    A1, A2, B1, B2, MX, DB, DG, WO, WG, SR, SS, H1S, H1R, H2S, H2R, OS, RZ, GP, MT, XH, HO, GV, GR, GA, SV, SA, PLACES, ZN, NS, NO,
     load_sem, gate_sem, ag_send, ag_recv, rs_send, rs_recv, sib_send, sib_recv, h1_send, h1_recv, h2_send, h2_recv,
-    out_sem, small_send, small_recv, x_send, x_recv, sib_free, first_free, second_free,
+    out_sem, small_send, small_recv, x_send, x_recv, n_send, n_recv, n_load, n_free, sib_free, first_free, second_free,
 ):
     place = Place()
     t = place.t
@@ -236,18 +238,11 @@
     load("branch", branch_own, DB.at[:, own_columns], 0)
     load("cot", cot_in, A1, 1)
     load("swi", swi_in, B1, 2)
-    load("h2", h2_in, A2, 3)
-    load("da", da_in, B2, 4)
-    load("out_w", out_w_in, WO, 5)
-    load("gate_w", gate_w_in, WG, 6)
-    load("mixed", mixed_in, MX, 7)
     greet(place)
 
     gather = Gather(place, DB, ag_send, ag_recv, chunk_rows, width)
     scatter = Scatter(place, RZ, rs_send, rs_recv)
     need("branch")
-    for chunk in range(chunks):
-        gather.step(chunk, 0)
 
     jobs = [
         (A1, B1, 0, hd_out, 0), (A1, B1, span, hd_out, span), (A2, B2, 0, hg_out, 0), (A2, B2, span, hg_out, span),
@@ -345,35 +340,34 @@
             if job + ahead < JOBS:
                 pl.semaphore_signal(free, inc=1, device_id=device, device_id_type=MESH)
 
-    def gate_loads(chunk):
-        rows = pl.ds(chunk * chunk_rows, chunk_rows)
-        return (
-            pltpu.make_async_copy(gate_in.at[rows], GP, gate_sem.at[0]),
-            pltpu.make_async_copy(mem_in.at[rows], MT, gate_sem.at[1]),
-        )
+    def gate_load(chunk):
+        return pltpu.make_async_copy(gate_in.at[pl.ds(chunk * chunk_rows, chunk_rows)], GP, gate_sem.at[0])
+
+    def mem_load(chunk):
+        return pltpu.make_async_copy(mem_in.at[pl.ds(chunk * chunk_rows, chunk_rows)], MT, gate_sem.at[1])
 
     def term_store(chunk):
-        return pltpu.make_async_copy(TS, term_out.at[pl.ds(chunk * chunk_rows, chunk_rows)], gate_sem.at[2])
+        return pltpu.make_async_copy(MT, term_out.at[pl.ds(chunk * chunk_rows, chunk_rows)], gate_sem.at[2])
 
     def channels(chunk):
         rows = pl.ds(chunk * chunk_rows, chunk_rows)
-        for copy in gate_loads(chunk):
-            copy.wait()
         if chunk > 0:
             term_store(chunk - 1).wait()
+        mem_load(chunk).start()
+        gate_load(chunk).wait()
+        mem_load(chunk).wait()
 
         def body(half, at):
             d_mixed = dot_nt(DB[rows, :], WO[at, :])
             pre = GP[:, at]
             sigma = jax.nn.sigmoid(pre)
-            TS[:, at] = (d_mixed * (pre * sigma)).astype(jnp.bfloat16)
             DG[rows, at] = (d_mixed * MT[:, at].astype(jnp.float32) * (sigma * (1.0 + pre * (1.0 - sigma)))).astype(jnp.bfloat16)
+            MT[:, at] = (d_mixed * (pre * sigma)).astype(jnp.bfloat16)
 
         each_half(body)
         term_store(chunk).start()
         if chunk + 1 < chunks:
-            for copy in gate_loads(chunk + 1):
-                copy.start()
+            gate_load(chunk + 1).start()
 
     def first_part(chunk, block):
         return dot_nt(DG[pl.ds(chunk * chunk_rows, chunk_rows), :], WG[pl.ds(pl.multiple_of(block * width, width), width), :])
@@ -414,6 +408,59 @@
             return remote(SV, SA.at[t], small_send.at[2 + step], small_recv.at[2 + step], device)
         return remote(GV.at[3], GA.at[t], small_send.at[5 + step], small_recv.at[5 + step], device)
 
+    down_scatter = Scatter(place, ZN, n_send, n_recv)
+
+    def down_part(chunk, block, target, sem):
+        source = down_in.at[pl.ds(chunk * chunk_rows, chunk_rows), pl.ds(pl.multiple_of(block * width, width), width)]
+        return pltpu.make_async_copy(source, target, sem)
+
+    def down_store(chunk):
+        return pltpu.make_async_copy(NO, down_out.at[pl.ds(chunk * chunk_rows, chunk_rows)], n_load.at[2])
+
+    def down_own(chunk):
+        if chunk > 0:
+            down_store(chunk - 1).wait()
+        load = down_part(chunk, t, NO, n_load.at[3])
+        load.start()
+        load.wait()
+        down_scatter.own(chunk, NO)
+        down_store(chunk).start()
+        down_scatter.finish(chunk)
+        if chunk < 2:
+            for step in (-1, 1):
+                @pl.when((t + step >= 0) & (t + step <= 3))
+                def _():
+                    pl.semaphore_signal(
+                        n_free.at[(1 - step) // 2], inc=1, device_id=place.along(t + step), device_id_type=MESH
+                    )
+
+    is_end = (t == 0) | (t == 3)
+    down_order = {inside: [event[1:3] for event in BACK_ORDER if event[0] == "Ns" and event[3] == inside] for inside in (False, True)}
+
+    def only(inside, body):
+        pl.when(jnp.logical_not(is_end) if inside else is_end)(body)
+
+    def down_load(inside, index):
+        chunk, step = down_order[inside][index]
+        return down_part(chunk, down_scatter.block(step), NS.at[index % 2], n_load.at[index % 2])
+
+    def down_step(chunk, step, inside):
+        index = down_order[inside].index((chunk, step))
+        first_of_chunk = all(other != chunk for other, _ in down_order[inside][:index])
+
+        def body():
+            if index == 0:
+                down_load(inside, 0).start()
+            if index + 1 < 12:
+                down_load(inside, index + 1).start()
+            if chunk >= 2 and first_of_chunk:
+                for side, near in enumerate((t > 0, t < 3)):
+                    pl.when(near)(functools.partial(pl.semaphore_wait, n_free.at[side], 1))
+            down_load(inside, index).wait()
+            down_scatter.step(chunk, step, lambda block: NS[index % 2], inside)
+
+        only(inside, body)
+
     channel_count = span
     block = DB.shape[0] // 8
     exchange = Exchange(
@@ -424,7 +471,9 @@
     )
 
     def send_terms():
-        loads["terms"].wait()
+        term_store(3).wait()
+        load("terms", term_out, B2.at[:, pl.ds(0, channel_count)], 4)
+        need("terms")
         PLACES[...] = ids_ref[...] - (place.f * 4 + place.c) * DB.shape[0]
 
         @pl.loop(0, chunks)
@@ -456,92 +505,45 @@
             store.start()
             store.wait()
 
-    for copy in gate_loads(0):
-        copy.start()
-
-    def steps(ends, inside):
-        def run(pairs, inner):
-            for chunk, step in pairs:
-                first_step(chunk, step, inner)
-
-        by_place(place, lambda: run(ends, False), lambda: run(inside, True))
-
-    def events(iteration, late):
-        if (iteration, late) == (1, 0):
-            gather.step(0, 1)
-            gather.step(1, 1)
-        if (iteration, late) == (1, 1):
-            gather.step(2, 1)
-            gather.step(3, 1)
-        if (iteration, late) == (2, 1):
-            gather.step(0, 2)
-            gather.step(1, 2)
-        if (iteration, late) == (3, 0):
-            gather.step(2, 2)
-            gather.step(3, 2)
-            need("out_w", "gate_w")
-            gather.step(0, 3)
-            channels(0)
-        if (iteration, late) == (3, 1):
-            gather.step(1, 3)
-            channels(1)
-            steps([(0, 0), (1, 0)], [])
-        if (iteration, late) == (4, 0):
-            gather.step(2, 3)
-            channels(2)
-        if (iteration, late) == (4, 1):
-            gather.step(3, 3)
-            channels(3)
-            steps([(2, 0), (3, 0)], [(0, 0), (1, 0)])
-        if (iteration, late) == (5, 0):
-            steps([(0, 1), (1, 1)], [(2, 0), (3, 0)])
-        if (iteration, late) == (5, 1):
-            steps([(2, 1), (3, 1)], [(0, 1), (1, 1)])
-            term_store(3).wait()
-            load("terms", term_out, B2.at[:, pl.ds(0, channel_count)], 4)
-        if (iteration, late) == (6, 0):
-            send_terms()
-            steps([(0, 2), (1, 2)], [(2, 1), (3, 1), (0, 2), (1, 2)])
-        if (iteration, late) == (6, 1):
-            steps([(2, 2), (3, 2)], [(2, 2), (3, 2)])
-        if (iteration, late) == (7, 0):
-            own_step(0)
-            own_step(1)
-        if (iteration, late) == (7, 1):
-            own_step(2)
-            own_step(3)
+    gate_load(0).start()
+
+    def gains(number):
+        if number == 0:
             for step in range(1, 4):
                 to_line(step, 0).start()
             GV[0, 1:2] = gg2_ref[...]
             sum_copy(0).start()
-        if (iteration, late) == (8, 0):
-            memory_grads()
-        if late and 8 <= iteration < 11:
-            step = iteration - 8
-            sum_copy(step).wait_recv()
-            GV[step + 1] = GV[step] + GR[step]
-            if step < 2:
-                sum_copy(step + 1).start()
-            else:
-                for ahead in range(1, 4):
-                    to_line(ahead, 1).start()
-
+            return
+        sum_copy(number - 1).wait_recv()
+        GV[number] = GV[number - 1] + GR[number - 1]
+        if number < 3:
+            sum_copy(number).start()
+        else:
+            for ahead in range(1, 4):
+                to_line(ahead, 1).start()
+
+    actions = {
+        "D": gather.step, "S1": to_sibling, "S2": to_first, "S3": to_second, "S4": to_output, "Bc": channels, "Bo": own_step,
+        "Bs": lambda chunk, step, inside: only(inside, lambda: first_step(chunk, step, inside)), "Ns": down_step, "No": down_own,
+        "terms": send_terms, "mgrads": memory_grads, "G": gains,
+    }
+    wanted = {
+        ("S1", 0): ("cot", "swi"), ("S1", 2): ("h2", "da"), ("S1", 4): ("db",), ("S1", 6): ("mixed",), ("S1", 7): ("h1",),
+        ("Bc", 0): ("out_w", "gate_w"),
+    }
     GV[0] = jnp.zeros_like(GV[0])
-    for iteration in range(JOBS + 2):
-        if iteration < JOBS:
-            need(*{0: ("cot", "swi"), 2: ("h2", "da"), 4: ("db",), 6: ("mixed",), 7: ("h1",)}.get(iteration, ()))
-            to_sibling(iteration)
-            to_first(iteration)
-        events(iteration, 0)
-        if 1 <= iteration <= JOBS:
-            to_second(iteration - 1)
-        if iteration >= 2:
-            to_output(iteration - 2)
-            if iteration == 3:
-                load("db", db_in, B1, 2)
-                load("h1", h1_in, A1, 1)
-        events(iteration, 1)
-    events(10, 1)
+    for event in BACK_ORDER:
+        need(*wanted.get(event, ()))
+        actions[event[0]](*event[1:])
+        if event == ("S2", 0):
+            load("h2", h2_in, A2, 3)
+            load("da", da_in, B2, 4)
+            load("out_w", out_w_in, WO, 5)
+            load("gate_w", gate_w_in, WG, 6)
+            load("mixed", mixed_in, MX, 7)
+        if event == ("S4", 1):
+            load("db", db_in, B1, 2)
+            load("h1", h1_in, A1, 1)
 
     for step in range(1, 4):
         to_line(step, 0).wait()
@@ -562,11 +564,12 @@
             h1_copy(job, slot).wait_send()
         h2_copy(job).wait_send()
     exchange.finish()
+    down_store(3).wait()
     own_copies(3)[1].wait()
     out_copy(JOBS - 1).wait()
 
 
-def back_call(branch_own, cot, swi, h2, da, db, mixed, h1, gate, mem, out_w, gate_w, xhat, gain, gg2, rank, ids):
+def back_call(branch_own, cot, swi, h2, da, db, mixed, h1, gate, mem, out_w, gate_w, xhat, gain, gg2, rank, ids, down):
     rows, features = cot.shape
     channels, hidden = mixed.shape[1], swi.shape[1]
     width, slab, part = features // 4, features // 8, rows // 4
@@ -581,26 +584,68 @@
         back_kernel,
         name="backward",
         out_shape=(
-            shape((rows, width), f32), shape((rows, channels), f32), shape((rows, channels), bf), shape((rows, channels), bf),
+            shape((rows, width), f32), shape((rows, width), f32), shape((rows, channels), f32), shape((rows, channels), bf), shape((rows, channels), bf),
             shape((slab, hidden), f32), shape((slab, hidden), f32),
             shape((slab, hidden), f32), shape((slab, channels), f32), shape((slab, channels), f32), shape((4, 8, width), f32),
             shape((8, rows), f32),
         ),
-        in_specs=[anywhere] * 13 + [vmem] * 4,
-        out_specs=(anywhere,) * 9 + (vmem,) * 2,
+        in_specs=[anywhere] * 13 + [vmem] * 4 + [anywhere],
+        out_specs=(anywhere,) * 10 + (vmem,) * 2,
         scratch_shapes=[
             V((rows, features), bf), V((rows, features), bf), V((rows, hidden), bf), V((rows, hidden), bf), V((rows, channels), bf),
             V((rows, features), bf), V((rows, channels), bf), V((channels, features), bf), V((features, channels), bf),
             V((3, 4, slab, channels), bf), V((4, slab, channels), bf), V((2, 2, slab, channels), bf), V((3, 2, slab, channels), bf),
             V((2, slab, channels), bf), V((2, slab, channels), bf), V((slab, channels), f32), V((4, 5, part, width), bf),
-            V((part, channels), f32), V((part, channels), bf), V((part, channels), bf), V((part, width), f32), V((part, width), f32),
+            V((part, channels), f32), V((part, channels), bf), V((part, width), f32), V((part, width), f32),
             V((4, 8, width), f32), V((3, 8, width), f32), V((4, 8, width), f32), V((8, rows), f32), V((4, 8, rows), f32),
-            V((8, rows), jnp.int32), dma((8,)), dma((5,)), dma((4, 2, 3)), dma((4, 4)), dma((4, 3)), dma((4, 5)), dma((4,)), dma((JOBS, 4)), dma((2, 2)),
-            dma((JOBS, 2)), dma((2,)), dma((JOBS,)), dma, dma((9,)), dma((9,)), dma((8,)), dma((8,)), regular, regular, regular,
+            V((8, rows), jnp.int32), V((2, 5, part, width), bf), V((2, part, width), f32), V((part, width), f32), dma((8,)), dma((5,)), dma((4, 2, 3)), dma((4, 4)), dma((4, 3)), dma((4, 5)), dma((4,)), dma((JOBS, 4)), dma((2, 2)),
+            dma((JOBS, 2)), dma((2,)), dma((JOBS,)), dma, dma((9,)), dma((9,)), dma((8,)), dma((8,)), dma((4, 3)), dma((4, 5)), dma((4,)), pltpu.SemaphoreType.REGULAR((2,)), regular, regular, regular,
         ],
         compiler_params=pltpu.CompilerParams(collective_id=1, has_side_effects=True, vmem_limit_bytes=VMEM_LIMIT),
         cost_estimate=pl.CostEstimate(flops=2 * macs, bytes_accessed=64 * 2**20, transcendentals=rows * channels),
-    )(branch_own, cot, swi, h2, da, db, mixed, h1, gate, mem, out_w, gate_w, xhat, gain, gg2, rank, ids)
+    )(branch_own, cot, swi, h2, da, db, mixed, h1, gate, mem, out_w, gate_w, xhat, gain, gg2, rank, ids, down)
+
+
+FRONT_ORDER = (
+    ("W", 1, 0), ("T", 0, 0), ("T", 1, 0), ("C", 0, 0), ("W", 0, 0), ("rows",), ("T", 1, 1), ("T", 0, 1), ("C", 1, 0),
+    ("W", 1, 1), ("T", 2, 0), ("C", 2, 0), ("W", 0, 1), ("W", 2, 0), ("T", 0, 2), ("T", 0, 3), ("T", 3, 0), ("W", 3, 0),
+    ("T", 1, 2), ("W", 1, 2), ("T", 3, 1), ("W", 0, 2), ("C", 0, 1), ("take",), ("T", 2, 1), ("C", 2, 1), ("W", 0, 3),
+    ("F1", 0), ("W", 1, 3), ("Rs", 0, 0, False), ("W", 4, 0), ("Rs", 0, 0, True), ("Rs", 0, 1, False), ("T", 1, 3),
+    ("T", 3, 2), ("C", 1, 1), ("F1", 1), ("Rs", 1, 0, True), ("W", 2, 1), ("Rs", 1, 0, False), ("Rs", 0, 1, True),
+    ("Rs", 1, 2, False), ("T", 2, 2), ("Rs", 1, 1, True), ("Rs", 0, 2, True), ("C", 1, 2), ("Rs", 0, 2, False),
+    ("Ro", 0), ("Rs", 1, 2, True), ("Rs", 1, 1, False), ("H", 0, 0), ("Ro", 1), ("H", 1, 0), ("W", 3, 1), ("T", 2, 3),
+    ("F1", 2), ("H", 0, 1), ("Rs", 2, 0, False), ("Rs", 2, 0, True), ("H", 1, 1), ("W", 4, 1), ("T", 3, 3), ("F1", 3),
+    ("Rs", 3, 0, False), ("C", 0, 2), ("Rs", 2, 1, False), ("H", 0, 2), ("W", 2, 2), ("Rs", 2, 1, True),
+    ("Rs", 3, 1, False), ("Rs", 3, 0, True), ("C", 1, 3), ("Rs", 2, 2, False), ("C", 3, 0), ("W", 3, 2), ("H", 1, 2),
+    ("Rs", 2, 2, True), ("Rs", 3, 2, True), ("W", 4, 2), ("W", 3, 3), ("Ro", 2), ("C", 2, 2), ("Rs", 3, 2, False),
+    ("H", 2, 0), ("C", 3, 1), ("C", 0, 3), ("Rs", 3, 1, True), ("W", 2, 3), ("H", 0, 3), ("W", 4, 3), ("F2", 0),
+    ("Es", 0, 0, False), ("Es", 0, 1, False), ("Es", 0, 2, False), ("H", 2, 1), ("H", 1, 3), ("F2", 1),
+    ("Es", 1, 0, False), ("Es", 0, 0, True), ("Es", 1, 1, False), ("Es", 0, 2, True), ("H", 2, 2), ("H", 2, 3),
+    ("NP", 0), ("Es", 0, 1, True), ("Ro", 3), ("H", 3, 0), ("C", 3, 2), ("C", 2, 3), ("Es", 1, 0, True), ("Eo", 0),
+    ("NP", 1), ("close", 0), ("Es", 1, 2, True), ("H", 3, 1), ("Es", 1, 2, False), ("Es", 1, 1, True), ("F2", 2),
+    ("Es", 2, 0, False), ("H", 3, 2), ("Eo", 1), ("C", 3, 3), ("Es", 2, 1, False), ("Es", 2, 2, False), ("close", 1),
+    ("Es", 2, 2, True), ("Es", 2, 0, True), ("H", 3, 3), ("F2", 3), ("Es", 3, 0, False), ("Es", 3, 1, False),
+    ("Es", 2, 1, True), ("Es", 3, 0, True), ("NP", 2), ("Es", 3, 2, False), ("Es", 3, 2, True), ("Es", 3, 1, True),
+    ("Eo", 2), ("NP", 3), ("close", 2), ("Eo", 3), ("close", 3),
+)
+BACK_ORDER = (
+    ("D", 0, 0), ("S1", 0), ("D", 1, 0), ("S2", 0), ("Ns", 0, 1, False), ("D", 2, 0), ("Ns", 1, 0, False), ("S1", 1),
+    ("D", 3, 0), ("S2", 1), ("S1", 2), ("Ns", 1, 1, False), ("D", 0, 1), ("S3", 0), ("S2", 2), ("D", 0, 2), ("D", 2, 1),
+    ("Ns", 0, 0, False), ("D", 0, 3), ("Ns", 0, 2, False), ("Bc", 0), ("S3", 1), ("D", 1, 1), ("S4", 0), ("S1", 3),
+    ("S2", 3), ("Ns", 1, 2, False), ("D", 1, 2), ("D", 1, 3), ("D", 2, 2), ("Ns", 0, 0, True), ("Bs", 0, 1, False),
+    ("S3", 2), ("Bc", 1), ("D", 3, 1), ("Bs", 1, 0, False), ("S4", 1), ("Bs", 0, 0, False), ("Ns", 1, 0, True),
+    ("S1", 4), ("D", 3, 2), ("D", 2, 3), ("S2", 4), ("Bc", 2), ("D", 3, 3), ("S4", 2), ("Bs", 1, 1, False),
+    ("Bs", 0, 2, True), ("Bs", 2, 0, False), ("Bc", 3), ("Bs", 3, 0, False), ("Ns", 0, 1, True), ("Ns", 0, 2, True),
+    ("S3", 3), ("Bs", 1, 2, False), ("Ns", 1, 1, True), ("Bs", 0, 0, True), ("S3", 4), ("S1", 5), ("No", 0),
+    ("Bs", 1, 0, True), ("S2", 5), ("S4", 3), ("S1", 6), ("Bs", 3, 1, False), ("Bs", 2, 1, False), ("Bs", 1, 1, True),
+    ("S4", 4), ("Bs", 2, 0, True), ("Ns", 2, 0, False), ("Ns", 1, 2, True), ("Ns", 2, 1, False), ("Bs", 0, 2, False),
+    ("S3", 5), ("Bs", 3, 2, False), ("Bs", 3, 0, True), ("terms",), ("S2", 6), ("Bs", 1, 2, True), ("No", 1),
+    ("Ns", 3, 0, False), ("Bs", 2, 1, True), ("Bs", 2, 2, False), ("S4", 5), ("Bs", 3, 1, True), ("S1", 7),
+    ("Ns", 2, 0, True), ("Ns", 3, 1, False), ("Ns", 2, 2, False), ("Bs", 3, 2, True), ("S2", 7), ("Bs", 0, 1, True),
+    ("Bo", 0), ("Ns", 2, 1, True), ("Bs", 2, 2, True), ("Ns", 2, 2, True), ("mgrads",), ("Ns", 3, 2, False),
+    ("Ns", 3, 0, True), ("S3", 6), ("Bo", 1), ("Bo", 2), ("Bo", 3), ("G", 0), ("Ns", 3, 2, True), ("Ns", 3, 1, True),
+    ("S3", 7), ("G", 1), ("G", 2), ("No", 2), ("G", 3), ("No", 3), ("S4", 6), ("S4", 7),
+)
 
 
 class Spread:
@@ -667,11 +712,11 @@
 
 def front_kernel(
     tokens, cotangent, mem_in, gate_w, out_w, up_a_w, up_b_w, down_w, gain1, gain2, deal_row, deal_column,
-    tok_full, cot_full, h2_full, h1_out, gate_out, mixed_out, swi_out, da_out, db_out, gate_w_out, out_w_out, block_out, dx1_out, branch_out, mem_out,
+    tok_full, cot_full, h2_full, h1_out, gate_out, mixed_out, swi_out, da_out, db_out, gate_w_out, out_w_out, down_out, middle_out, dx1_out, branch_out, mem_out,
     inv_out, gg2_out, rank_out, ids_out,
-    WG, WO, WA, WB, WD, Z1, ZN, ZE, XC, CC, H1C, GPS, MXS, MT, SWI, DA, DB, X1, H2O, HO, DHQ, FS, BS, OWN, I2, SV, SA, SV2, SA2, SENT,
-    load_sem, store_sem, stage_sem, t_send, t_recv, c_send, c_recv, h_send, h_recv, r_send, r_recv, n_send, n_recv, e_send, e_recv,
-    w_send, w_recv, w_local, s_send, s_recv, x_send, x_recv, i_send, i_recv,
+    WG, WO, WA, WB, WD, Z1, ZE, XC, CC, H1C, GPS, MXS, MT, SWI, DA, DB, X1, H2O, HO, DHQ, FS, NS, BS, OWN, I2, SV, SA, SV2, SA2, SENT,
+    load_sem, store_sem, stage_sem, t_send, t_recv, c_send, c_recv, h_send, h_recv, r_send, r_recv, e_send, e_recv,
+    w_send, w_recv, w_local, s_send, s_recv, x_send, x_recv, i_send, i_recv, n_sem,
 ):
     place = Place()
     t = place.t
@@ -701,7 +746,6 @@
     cot_gather = Gather(place, cot_full, c_send, c_recv, chunk_rows, width, cotangent)
     h2_gather = Gather(place, h2_full, h_send, h_recv, chunk_rows, width, H2O)
     mix_scatter = Scatter(place, Z1, r_send, r_recv)
-    down_scatter = Scatter(place, ZN, n_send, n_recv)
     up_scatter = Scatter(place, ZE, e_send, e_recv)
     spreads = [
         Spread(place, index, shard, view, w_send, w_recv, w_local)
@@ -762,21 +806,25 @@
         rows_exchange.start()
 
     def mem_store(chunk):
-        return pltpu.make_async_copy(MT, mem_out.at[rows_of(chunk)], load_sem.at[0])
-
-    def take_rows(chunk):
-        if chunk == 0:
-            ids_exchange.arrived()
-            rows_exchange.arrived()
-        else:
-            mem_store(chunk - 1).wait()
-        total = jnp.zeros((chunk_rows, channels), jnp.float32)
-        first = rows_exchange.me * rows + chunk * chunk_rows
-        for other in range(4):
-            picked = chosen(ids_out[0:1, rows_of(other)], first, chunk_rows)
-            total += jnp.dot(picked, quarter(SWI, other)[...], preferred_element_type=jnp.float32)
-        MT[...] = total.astype(jnp.bfloat16)
-        mem_store(chunk).start()
+        return pltpu.make_async_copy(MXS.at[chunk % 2], mem_out.at[rows_of(chunk)], load_sem.at[4 + chunk])
+
+    def take_rows():
+        ids_exchange.arrived()
+        rows_exchange.arrived()
+        for chunk in range(4):
+            if chunk > 1:
+                mem_store(chunk - 2).wait()
+            first = rows_exchange.me * rows + chunk * chunk_rows
+            total = jnp.zeros((chunk_rows, channels), jnp.float32)
+            for other in range(4):
+                picked = chosen(ids_out[0:1, rows_of(other)], first, chunk_rows)
+                total += jnp.dot(picked, quarter(SWI, other)[...], preferred_element_type=jnp.float32)
+            MXS[chunk % 2] = total.astype(jnp.bfloat16)
+            mem_store(chunk).start()
+        for chunk in (2, 3):
+            mem_store(chunk).wait()
+        rows_exchange.finish()
+        ids_exchange.finish()
 
     def h1_store(chunk):
         return pltpu.make_async_copy(H1C, h1_out.at[rows_of(chunk)], store_sem.at[0])
@@ -826,6 +874,7 @@
         if chunk == 0:
             own_tokens.wait()
         load = fetch(tok_full.at[rows_of(chunk)], XC, 1)
+        mem_load = fetch(mem_out.at[rows_of(chunk)], MT, 0)
         if chunk > 0:
             h1_store(chunk - 1).wait()
         load.wait()
@@ -839,7 +888,7 @@
             at = slice(block * width, (block + 1) * width)
             H1C[:, at] = (XC[:, at].astype(jnp.float32) * inverse * gain1[:, at]).astype(jnp.bfloat16)
         h1_store(chunk).start()
-        take_rows(chunk)
+        mem_load.wait()
         if chunk > 0:
             gate_store(chunk - 1).wait()
         if chunk > 1:
@@ -860,6 +909,8 @@
 
     def mix_own(chunk):
         load = fetch(tokens.at[rows_of(chunk)], OWN, 2)
+        if chunk > 0:
+            small_store(X1.at[rows_of(chunk)], middle_out, chunk - 1, 10).wait()
         HO[...] = mix_part(chunk, t)
         mix_scatter.own(chunk, HO)
         load.wait()
@@ -868,8 +919,8 @@
         H2O[rows_of(chunk)] = (middle * gain2[...]).astype(jnp.bfloat16)
         own_h2_store(chunk).start()
         SV[:, rows_of(chunk)] = to_row(jnp.sum(middle * middle, axis=1, keepdims=True))
+        small_store(X1.at[rows_of(chunk)], middle_out, chunk, 10).start()
         mix_scatter.finish(chunk)
-        h2_gather.step(chunk, 0)
         for step in range(1, 4):
             stat_copy(chunk, step, 0).start()
 
@@ -902,16 +953,21 @@
         for store in hidden_stores(chunk):
             store.start()
 
-    def down_part(chunk, block):
-        return jnp.dot(SWI[chunk % 2], WD[:, columns_of(block, width)], preferred_element_type=jnp.float32)
+    def down_store(chunk, block):
+        return pltpu.make_async_copy(NS.at[block % 2], down_out.at[rows_of(chunk), columns_of(block, width)], n_sem.at[block % 2])
+
+    def down_parts(chunk):
+        for block in range(4):
+            if chunk > 0 or block > 1:
+                down_store(chunk, block).wait()
+            NS[block % 2] = jnp.dot(SWI[chunk % 2], WD[:, columns_of(block, width)], preferred_element_type=jnp.float32)
+            down_store(chunk, block).start()
 
     def up_part(chunk, block):
         at = columns_of(block, width)
         return dot_nt(DA[chunk % 2], WA[at, :]) + dot_nt(DB[chunk % 2], WB[at, :])
 
     def hidden_own(chunk):
-        if chunk > 0:
-            small_store(BS.at[0], block_out, chunk - 1, 10).wait()
         HO[...] = up_part(chunk, t)
         up_scatter.own(chunk, HO)
         middle = X1[rows_of(chunk)]
@@ -924,12 +980,7 @@
         scaled = d_second * gain2[...]
         DHQ[...] = scaled
         SV2[:, rows_of(chunk)] = to_row(jnp.sum(scaled * middle, axis=1, keepdims=True) * I2[rows_of(chunk)])
-        HO[...] = down_part(chunk, t)
-        down_scatter.own(chunk, HO)
-        BS[0] = (middle + HO[...]).astype(jnp.bfloat16)
-        small_store(BS.at[0], block_out, chunk, 10).start()
         up_scatter.finish(chunk)
-        down_scatter.finish(chunk)
         for step in range(1, 4):
             stat_copy(chunk, step, 1).start()
 
@@ -938,87 +989,38 @@
         mean = stats(chunk, 1) / features
         if chunk > 0:
             small_store(FS, dx1_out, chunk - 1, 11).wait()
-            small_store(BS.at[1], branch_out, chunk - 1, 12).wait()
+            small_store(BS, branch_out, chunk - 1, 12).wait()
         load.wait()
         unit = X1[rows_of(chunk)] * I2[rows_of(chunk)]
         total = OWN[...].astype(jnp.float32) + DHQ[...] - unit * mean
         FS[...] = total
-        BS[1] = total.astype(jnp.bfloat16)
+        BS[...] = total.astype(jnp.bfloat16)
         small_store(FS, dx1_out, chunk, 11).start()
-        small_store(BS.at[1], branch_out, chunk, 12).start()
-
-    def mix_steps(chunk, ends, inside):
-        def run(steps, inner):
-            for step in steps:
-                mix_scatter.step(chunk, step, lambda block: mix_part(chunk, block), inner)
-
-        by_place(place, lambda: run(ends, False), lambda: run(inside, True))
-
-    def hidden_steps(chunk, ends, inside):
-        def run(steps, inner):
-            for step in steps:
-                up_scatter.step(chunk, step, lambda block: up_part(chunk, block), inner)
-                down_scatter.step(chunk, step, lambda block: down_part(chunk, block), inner)
-
-        by_place(place, lambda: run(ends, False), lambda: run(inside, True))
-
-    def pumps(turn):
-        for index, number in {
-            0: ((0, 0),), 1: ((0, 1), (1, 0)), 2: ((0, 2), (1, 1)), 3: ((0, 3), (1, 2), (2, 0), (1, 3)), 5: ((2, 1), (3, 0)),
-            6: ((2, 2),), 7: ((2, 3), (3, 1), (4, 0)), 8: ((3, 2),), 9: ((3, 3), (4, 1), (4, 2), (4, 3)),
-        }.get(turn, ()):
-            spreads[index].phase(number)
-
-    def hops(chunk, event):
-        if event in (0, 1, 2):
-            tok_gather.step(chunk, event)
-        if event in (3, 4, 5, 6):
-            cot_gather.step(chunk, event - 3)
-        if event in (7, 8):
-            h2_gather.step(chunk, event - 6)
-        if event == 13:
-            close(chunk)
-
-    def light(chunk, event):
-        if event == 4:
-            mix_steps(chunk, (1,), (0,))
-        if event == 5:
-            mix_steps(chunk, (2,), (1, 2))
-        if event == 6:
-            mix_own(chunk)
-        if event == 10:
-            hidden_steps(chunk, (1,), (0,))
-        if event == 11:
-            hidden_steps(chunk, (2,), (1, 2))
-        if event == 12:
-            hidden_own(chunk)
-
-    def heavy(chunk, event):
-        if event == 3:
-            tok_gather.step(chunk, 3)
-            memory_unit(chunk)
-            mix_steps(chunk, (0,), ())
-        if event == 9:
-            h2_gather.step(chunk, 3)
-            feed_forward(chunk)
-            hidden_steps(chunk, (0,), ())
+        small_store(BS, branch_out, chunk, 12).start()
 
     weight_stores = [
         pltpu.make_async_copy(WG, gate_w_out, stage_sem.at[2]), pltpu.make_async_copy(WO, out_w_out, stage_sem.at[3]),
     ]
-    for turn in range(20):
-        pumps(turn)
-        if turn == 9:
-            rows_exchange.finish()
-            ids_exchange.finish()
-        if turn == 3:
-            for store in weight_stores:
-                store.start()
-        for action in (hops, light, heavy):
-            for chunk in range(4) if action is not heavy else (3, 2, 1, 0):
-                action(chunk, turn - 2 * chunk)
-        if turn == 0:
-            send_rows()
+    is_end = (t == 0) | (t == 3)
+
+    def scatter_step(scatter, part, chunk, step, inside):
+        pl.when(jnp.logical_not(is_end) if inside else is_end)(
+            lambda: scatter.step(chunk, step, lambda block: part(chunk, block), inside)
+        )
+
+    actions = {
+        "T": tok_gather.step, "C": cot_gather.step, "H": h2_gather.step, "F1": memory_unit, "F2": feed_forward, "Ro": mix_own,
+        "Eo": hidden_own, "close": close, "rows": send_rows, "take": take_rows, "NP": down_parts,
+        "Rs": functools.partial(scatter_step, mix_scatter, mix_part), "Es": functools.partial(scatter_step, up_scatter, up_part),
+    }
+    for name, *where in FRONT_ORDER:
+        if name == "W":
+            index, number = where
+            spreads[index].phase(number)
+            if number == 3 and index < 2:
+                weight_stores[index].start()
+        else:
+            actions[name](*where)
 
     for store in weight_stores:
         store.wait()
@@ -1030,16 +1032,17 @@
         for which in range(2):
             for step in range(1, 4):
                 stat_copy(chunk, step, which).wait_send()
-    mem_store(3).wait()
     h1_store(3).wait()
     gate_store(3).wait()
     for chunk in (2, 3):
         mixed_store(chunk).wait()
         for store in hidden_stores(chunk):
             store.wait()
-    small_store(BS.at[0], block_out, 3, 10).wait()
+    small_store(X1.at[rows_of(3)], middle_out, 3, 10).wait()
+    for block in (2, 3):
+        down_store(3, block).wait()
     small_store(FS, dx1_out, 3, 11).wait()
-    small_store(BS.at[1], branch_out, 3, 12).wait()
+    small_store(BS, branch_out, 3, 12).wait()
 
 
 def front_call(tokens, cotangent, mem, gate_w, out_w, up_a_w, up_b_w, down_w, gain1, gain2, deal_row, deal_column):
@@ -1058,22 +1061,22 @@
         out_shape=(
             shape((rows, features), bf), shape((rows, features), bf), shape((rows, features), bf), shape((rows, features), bf),
             shape((rows, channels), f32), shape((rows, channels), bf), shape((rows, hidden), bf), shape((rows, hidden), bf),
-            shape((rows, hidden), bf), shape((features, channels), bf), shape((channels, features), bf), shape((rows, width), bf),
-            shape((rows, width), f32), shape((rows, width), bf), shape((rows, channels), bf), shape((rows, 1), f32), shape((1, width), f32),
+            shape((rows, hidden), bf), shape((features, channels), bf), shape((channels, features), bf), shape((rows, features), f32),
+            shape((rows, width), f32), shape((rows, width), f32), shape((rows, width), bf), shape((rows, channels), bf), shape((rows, 1), f32), shape((1, width), f32),
             shape((8, rows), jnp.int32), shape((8, rows), jnp.int32),
         ),
         in_specs=[anywhere] * 8 + [vmem] * 4,
-        out_specs=(anywhere,) * 15 + (vmem,) * 4,
+        out_specs=(anywhere,) * 16 + (vmem,) * 4,
         scratch_shapes=[
             V((features, channels), bf), V((channels, features), bf), V((features, hidden), bf), V((features, hidden), bf),
-            V((hidden, features), bf), V((2, 5, part, width), bf), V((2, 5, part, width), bf), V((2, 5, part, width), bf),
+            V((hidden, features), bf), V((2, 5, part, width), bf), V((2, 5, part, width), bf),
             V((part, features), bf), V((part, features), bf), V((part, features), bf), V((part, channels), f32), V((2, part, channels), bf),
             V((part, channels), bf), V((2, part, hidden), bf), V((2, part, hidden), bf), V((2, part, hidden), bf), V((rows, width), f32),
-            V((rows, width), bf), V((part, width), f32), V((part, width), f32), V((part, width), f32), V((2, part, width), bf),
+            V((rows, width), bf), V((part, width), f32), V((part, width), f32), V((part, width), f32), V((2, part, width), f32), V((part, width), bf),
             V((part, width), bf), V((rows, 1), f32), V((8, rows), f32), V((4, 8, rows), f32), V((8, rows), f32), V((4, 8, rows), f32),
             V((8, rows), jnp.int32), dma((8,)), dma((13,)), dma((8,)), dma((4, 2, 3)), dma((4, 4)), dma((4, 2, 3)), dma((4, 4)), dma((4, 2, 3)), dma((4, 4)),
-            dma((4, 3)), dma((4, 5)), dma((4, 3)), dma((4, 5)), dma((4, 3)), dma((4, 5)), dma((5, 7)), dma((5, 8)), dma((5,)),
-            dma((2, 4, 3)), dma((2, 4, 3)), dma((8,)), dma((8,)), dma((8,)), dma((8,)),
+            dma((4, 3)), dma((4, 5)), dma((4, 3)), dma((4, 5)), dma((5, 7)), dma((5, 8)), dma((5,)),
+            dma((2, 4, 3)), dma((2, 4, 3)), dma((8,)), dma((8,)), dma((8,)), dma((8,)), dma((2,)),
         ],
         compiler_params=pltpu.CompilerParams(collective_id=2, has_side_effects=True, vmem_limit_bytes=VMEM_LIMIT),
         cost_estimate=pl.CostEstimate(flops=2 * macs, bytes_accessed=96 * 2**20, transcendentals=rows * (channels + hidden)),
@@ -1192,17 +1195,18 @@
     own = lambda array: lax.dynamic_slice_in_dim(array, lax.axis_index("tp") * width, width, 0)[None]
     gain_one, gain_two = own(gain_first), own(gain_second)
     (
-        _, full_cot, second, first, gate_pre, mixed, swished, d_a, d_b, gate_w, out_w, block_out, d_middle, d_branch, memory_tokens,
+        _, full_cot, second, first, gate_pre, mixed, swished, d_a, d_b, gate_w, out_w, down, middle, d_middle, d_branch, memory_tokens,
         inv_first, gain_two_part, rank, ids,
     ) = front_call(
         tokens, cotangent, memory, memory_gate, memory_out, hidden_gate, hidden_up, hidden_down, gain_first[None], gain_two,
         dealing[None], dealing[:, None],
     )
     unit_own = tokens.astype(jnp.float32) * inv_first
-    d_first, grad_memory, _, _, grad_down, grad_up_a, grad_up_b, grad_out, grad_gate, gains, stats = back_call(
+    d_first, down_sum, grad_memory, _, _, grad_down, grad_up_a, grad_up_b, grad_out, grad_gate, gains, stats = back_call(
         d_branch, full_cot, swished, second, d_a, d_b, mixed, first, gate_pre, memory_tokens, out_w, gate_w, unit_own, gain_one,
-        gain_two_part, rank, ids,
-    )
+        gain_two_part, rank, ids, down,
+    )
+    block_out = (middle + down_sum).astype(jnp.bfloat16)
     grad_inputs = d_middle + inv_first * (d_first * gain_one - unit_own * (stats[0][:, None] / features))
     return (
         block_out, grad_inputs, grad_memory, gains[:, 0].reshape(features), gains[:, 1].reshape(features), grad_gate, grad_out.T,

time: 605 us -> 519 us (0.86)
  Pallas kernels: 566 us -> 478 us
    pallas_call x1, Pallas kernels: 384 us -> 296 us  [front_call(): pl.pallas_call(front_kernel, name='forward', out_shape=(shape((rows, feat...]
    unnamed x21 -> x18, local copies, waits for them, and re-layouts: 15.8 us -> 14.9 us
where the time goes in v5:
time: 519 us; the launch traced here: 509 us
  Pallas kernels  478 us (92%)
  local copies, waits for them, and re-layouts  20.9 us (4%)
  other arithmetic  9.2 us (2%)
    pallas_call x1, Pallas kernels, front_call(): pl.pallas_call(front_kernel, name='forward', out_shape=(shape((rows, feat...  296 us
    pallas_call x1, Pallas kernels, back_call(): pl.pallas_call(back_kernel, name='backward', out_shape=(shape((rows, widt...  182 us
    unnamed x18, local copies, waits for them, and re-layouts  14.9 us

profile of v5, /device:TPU:0, one launch (start us, length us, event | category | flops | bytes accessed | tf_op | source)
XLA Modules:
  0.0 509.1 jit_solution(17805027278610402897)
XLA Ops:
  0.6 1.3 dynamic_slice.7
  2.0 1.3 dynamic_slice.6
  3.3 1.7 copy.23.deal_column
  5.0 0.0 copy-start
  5.0 296.3 %forward.1 = (bf16[1024,2048]{1,0:T(8,128)(2,1)}, bf16[1024,2048]{1,0:T(8,128)(2,1)}, bf16[1024,2048]{1,0:T(8,128)(2,1)}, bf16[1024,2048]{1,0:T(8,128)(2,1)}, f3...) custom-call(bf16[1024,512]{1,0:T(8,128)(2,1)} %tokens.1, ...), custom_call_target="tpu_custom_call" | custom-call | flops 60129542144 | bytes 100663296 | tf_op jit(solution)/shard_map/forward/pallas_call | solution.py:1058
  301.4 1.2 reduce
  302.6 0.0 copy-done
  302.6 1.5 convert_multiply_fusion.xhat_in
  304.2 0.0 copy-start.5
  304.2 181.5 %backward.1 = (f32[1024,512]{1,0:T(8,128)}, f32[1024,512]{1,0:T(8,128)}, f32[1024,1024]{1,0:T(8,128)}, bf16[1024,1024]{1,0:T(8,128)(2,1)}, bf16[1024,1024]{1,0:T...) custom-call(bf16[1024,512]{1,0:T(8,128)(2,1)} %get-tuple-element.40., ...), custom_call_target="tpu_custom_call" | custom-call | flops 42949672960 | bytes 67108864 | tf_op jit(solution)/shard_map/backward/pallas_call | solution.py:583
  485.7 0.8 slice_multiply_fusion
  486.5 0.0 copy-done.5
  486.5 5.7 %multiply_add_fusion = (f32[1024,512]{1,0:T(8,128)}, bf16[1024,512]{1,0:T(8,128)(2,1)}) fusion(f32[1024,512]{1,0:T(8,128)} %get-tuple-element.58, f32[1024,512]{1,0:T(8,128)} %get-tuple-element.59, f32[1024]{0:T(1024)S(1)} %bitcast.12, f32[512]{0:T(512)S(1)} %copy-done.5, f32[1024]{0:T(1024)S(1)} %reduce, bf16[1024,512]{1,0:T(8,128)(2,1)S(1)} %copy-done, ...), kind=kLoop, calls=%fused_computation | loop fusion | flops 4718592 | bytes 12593152 | tf_op jit(solution)/shard_map/add | solution.py:1210
  492.1 1.6 fusion
  493.8 2.5 copy.24
  496.3 0.0 copy-done.3
  496.3 1.8 copy.25
  498.1 4.9 copy.30
  503.0 0.0 copy-done.4
  503.0 1.0 copy.31
  504.0 1.0 copy-done.2
  505.0 1.3 copy.32
  506.3 1.0 copy-done.1
  507.3 1.3 copy.33
  (4 shorter events, 0.0 us)
Async XLA Ops:
  5.0 297.6 %copy-start = (bf16[1024,512]{1,0:T(8,128)(2,1)S(1)}, bf16[1024,512]{1,0:T(8,128)(2,1)}, u32[]{:S(2)}) copy-start(bf16[1024,512]{1,0:T(8,128)(2,1)} %tokens.1) | copy-start | bytes 3145732
  304.2 182.3 %copy-start.5 = (f32[512]{0:T(512)S(1)}, f32[512]{0:T(512)}, u32[]{:S(2)}) copy-start(f32[512]{0:T(512)} %dynamic_slice.7) | copy-start | bytes 6148
  492.1 4.2 copy-start.3
  498.1 4.9 copy-start.4
  503.0 2.0 copy-start.2
  505.0 2.3 copy-start.1

commit v6 on v5

--- a/solution.py
+++ b/solution.py
@@ -8,7 +8,7 @@
 from jax.sharding import PartitionSpec as P
 
 EPS = 1e-06
-VMEM_LIMIT = 62 * 2**20
+VMEM_LIMIT = 63 * 2**20 + 2**19
 
 
 MESH = pl.DeviceIdType.MESH
@@ -390,12 +390,15 @@
         HO[...] = first_part(chunk, t)
         scatter.own(chunk, HO)
         load_xhat.wait()
-        product = HO[...] * XH[...]
+        d_first, unit = HO[...], XH[...]
+        product = jnp.sum(d_first * unit, axis=0, keepdims=True)
         if chunk == 0:
-            GV[0, 0:1] = jnp.sum(product, axis=0, keepdims=True)
+            GV[0, 0:1] = product
         else:
-            GV[0, 0:1] += jnp.sum(product, axis=0, keepdims=True)
-        SV[:, pl.ds(chunk * chunk_rows, chunk_rows)] = to_row(jnp.sum(product * gain_ref[...], axis=1, keepdims=True))
+            GV[0, 0:1] += product
+        scaled = d_first * gain_ref[:, own_columns]
+        HO[...] = scaled
+        SV[:, pl.ds(chunk * chunk_rows, chunk_rows)] = to_row(jnp.sum(scaled * unit, axis=1, keepdims=True))
         store.start()
 
     def sum_copy(step):
@@ -500,8 +503,8 @@
             for chunk in range(chunks):
                 picked = chosen(rank_ref[0:1, rows], chunk * chunk_rows, chunk_rows)
                 total += dot_tn(picked, A2[chunk * chunk_rows:(chunk + 1) * chunk_rows, 0:channel_count])
-            GP[...] = total
-            store = pltpu.make_async_copy(GP, memory_out.at[rows], gate_sem.at[0])
+            MT[...] = total.astype(jnp.bfloat16)
+            store = pltpu.make_async_copy(MT, memory_out.at[rows], gate_sem.at[0])
             store.start()
             store.wait()
 
@@ -584,7 +587,7 @@
         back_kernel,
         name="backward",
         out_shape=(
-            shape((rows, width), f32), shape((rows, width), f32), shape((rows, channels), f32), shape((rows, channels), bf), shape((rows, channels), bf),
+            shape((rows, width), f32), shape((rows, width), f32), shape((rows, channels), bf), shape((rows, channels), bf), shape((rows, channels), bf),
             shape((slab, hidden), f32), shape((slab, hidden), f32),
             shape((slab, hidden), f32), shape((slab, channels), f32), shape((slab, channels), f32), shape((4, 8, width), f32),
             shape((8, rows), f32),
@@ -607,25 +610,25 @@
 
 
 FRONT_ORDER = (
-    ("W", 1, 0), ("T", 0, 0), ("T", 1, 0), ("C", 0, 0), ("W", 0, 0), ("rows",), ("T", 1, 1), ("T", 0, 1), ("C", 1, 0),
-    ("W", 1, 1), ("T", 2, 0), ("C", 2, 0), ("W", 0, 1), ("W", 2, 0), ("T", 0, 2), ("T", 0, 3), ("T", 3, 0), ("W", 3, 0),
-    ("T", 1, 2), ("W", 1, 2), ("T", 3, 1), ("W", 0, 2), ("C", 0, 1), ("take",), ("T", 2, 1), ("C", 2, 1), ("W", 0, 3),
-    ("F1", 0), ("W", 1, 3), ("Rs", 0, 0, False), ("W", 4, 0), ("Rs", 0, 0, True), ("Rs", 0, 1, False), ("T", 1, 3),
-    ("T", 3, 2), ("C", 1, 1), ("F1", 1), ("Rs", 1, 0, True), ("W", 2, 1), ("Rs", 1, 0, False), ("Rs", 0, 1, True),
-    ("Rs", 1, 2, False), ("T", 2, 2), ("Rs", 1, 1, True), ("Rs", 0, 2, True), ("C", 1, 2), ("Rs", 0, 2, False),
-    ("Ro", 0), ("Rs", 1, 2, True), ("Rs", 1, 1, False), ("H", 0, 0), ("Ro", 1), ("H", 1, 0), ("W", 3, 1), ("T", 2, 3),
-    ("F1", 2), ("H", 0, 1), ("Rs", 2, 0, False), ("Rs", 2, 0, True), ("H", 1, 1), ("W", 4, 1), ("T", 3, 3), ("F1", 3),
-    ("Rs", 3, 0, False), ("C", 0, 2), ("Rs", 2, 1, False), ("H", 0, 2), ("W", 2, 2), ("Rs", 2, 1, True),
-    ("Rs", 3, 1, False), ("Rs", 3, 0, True), ("C", 1, 3), ("Rs", 2, 2, False), ("C", 3, 0), ("W", 3, 2), ("H", 1, 2),
-    ("Rs", 2, 2, True), ("Rs", 3, 2, True), ("W", 4, 2), ("W", 3, 3), ("Ro", 2), ("C", 2, 2), ("Rs", 3, 2, False),
-    ("H", 2, 0), ("C", 3, 1), ("C", 0, 3), ("Rs", 3, 1, True), ("W", 2, 3), ("H", 0, 3), ("W", 4, 3), ("F2", 0),
-    ("Es", 0, 0, False), ("Es", 0, 1, False), ("Es", 0, 2, False), ("H", 2, 1), ("H", 1, 3), ("F2", 1),
-    ("Es", 1, 0, False), ("Es", 0, 0, True), ("Es", 1, 1, False), ("Es", 0, 2, True), ("H", 2, 2), ("H", 2, 3),
-    ("NP", 0), ("Es", 0, 1, True), ("Ro", 3), ("H", 3, 0), ("C", 3, 2), ("C", 2, 3), ("Es", 1, 0, True), ("Eo", 0),
-    ("NP", 1), ("close", 0), ("Es", 1, 2, True), ("H", 3, 1), ("Es", 1, 2, False), ("Es", 1, 1, True), ("F2", 2),
-    ("Es", 2, 0, False), ("H", 3, 2), ("Eo", 1), ("C", 3, 3), ("Es", 2, 1, False), ("Es", 2, 2, False), ("close", 1),
-    ("Es", 2, 2, True), ("Es", 2, 0, True), ("H", 3, 3), ("F2", 3), ("Es", 3, 0, False), ("Es", 3, 1, False),
-    ("Es", 2, 1, True), ("Es", 3, 0, True), ("NP", 2), ("Es", 3, 2, False), ("Es", 3, 2, True), ("Es", 3, 1, True),
+    ("T", 0, 0), ("W", 0, 0), ("T", 1, 0), ("T", 2, 0), ("T", 3, 0), ("W", 1, 0), ("C", 1, 0), ("rows",), ("W", 0, 1),
+    ("T", 1, 1), ("W", 1, 1), ("W", 4, 0), ("T", 0, 1), ("C", 2, 0), ("T", 1, 2), ("T", 0, 2), ("C", 0, 0), ("take",),
+    ("W", 2, 0), ("T", 2, 1), ("W", 1, 2), ("W", 3, 0), ("C", 2, 1), ("C", 3, 0), ("T", 3, 1), ("T", 0, 3), ("T", 1, 3),
+    ("W", 0, 2), ("W", 0, 3), ("W", 1, 3), ("F1", 0), ("Rs", 0, 1, False), ("Rs", 0, 0, False), ("Rs", 0, 2, False),
+    ("C", 3, 1), ("F1", 1), ("Rs", 1, 0, False), ("Rs", 0, 0, True), ("C", 1, 1), ("T", 2, 2), ("Rs", 1, 0, True),
+    ("T", 3, 2), ("Rs", 1, 1, False), ("Rs", 0, 2, True), ("W", 4, 1), ("Rs", 1, 2, False), ("T", 3, 3),
+    ("Rs", 1, 2, True), ("Rs", 0, 1, True), ("Rs", 1, 1, True), ("Ro", 0), ("H", 0, 0), ("C", 0, 1), ("W", 2, 1),
+    ("H", 0, 1), ("T", 2, 3), ("F1", 2), ("Rs", 2, 0, False), ("C", 0, 2), ("Rs", 2, 1, False), ("C", 1, 2),
+    ("Rs", 2, 2, False), ("Rs", 2, 0, True), ("Ro", 1), ("H", 1, 0), ("W", 3, 1), ("W", 4, 2), ("F1", 3),
+    ("Rs", 2, 1, True), ("W", 2, 2), ("Rs", 2, 2, True), ("H", 1, 1), ("Rs", 3, 0, False), ("Rs", 3, 1, False),
+    ("W", 3, 2), ("Rs", 3, 0, True), ("H", 0, 2), ("C", 1, 3), ("W", 2, 3), ("H", 1, 2), ("W", 4, 3), ("Ro", 2),
+    ("Rs", 3, 1, True), ("Rs", 3, 2, True), ("H", 2, 0), ("C", 0, 3), ("Rs", 3, 2, False), ("H", 0, 3), ("W", 3, 3),
+    ("F2", 0), ("Es", 0, 0, False), ("Es", 0, 1, False), ("H", 2, 1), ("Ro", 3), ("C", 2, 2), ("H", 3, 0), ("H", 1, 3),
+    ("F2", 1), ("Es", 1, 0, False), ("Es", 1, 1, False), ("Es", 0, 2, True), ("Es", 0, 2, False), ("H", 2, 2),
+    ("Es", 1, 2, False), ("Es", 0, 0, True), ("C", 3, 2), ("H", 3, 1), ("C", 2, 3), ("H", 2, 3), ("F2", 2),
+    ("Es", 2, 1, False), ("Es", 2, 0, False), ("Es", 0, 1, True), ("Es", 1, 2, True), ("H", 3, 2), ("Es", 2, 2, False),
+    ("NP", 0), ("Es", 1, 0, True), ("Eo", 0), ("H", 3, 3), ("C", 3, 3), ("F2", 3), ("close", 0), ("Es", 3, 0, False),
+    ("Es", 2, 0, True), ("Es", 2, 2, True), ("Es", 3, 1, False), ("Es", 1, 1, True), ("NP", 1), ("NP", 2), ("Eo", 1),
+    ("Es", 3, 0, True), ("Es", 2, 1, True), ("Es", 3, 2, True), ("Es", 3, 2, False), ("Es", 3, 1, True), ("close", 1),
     ("Eo", 2), ("NP", 3), ("close", 2), ("Eo", 3), ("close", 3),
 )
 BACK_ORDER = (
@@ -711,10 +714,10 @@
 
 
 def front_kernel(
-    tokens, cotangent, mem_in, gate_w, out_w, up_a_w, up_b_w, down_w, gain1, gain2, deal_row, deal_column,
-    tok_full, cot_full, h2_full, h1_out, gate_out, mixed_out, swi_out, da_out, db_out, gate_w_out, out_w_out, down_out, middle_out, dx1_out, branch_out, mem_out,
+    tokens, cotangent, mem_in, gate_w, out_w, up_a_w, up_b_w, down_w, gain1, gain2, deal_row,
+    tok_full, cot_full, h2_full, h1_out, gate_out, mixed_out, swi_out, da_out, db_out, gate_w_out, out_w_out, down_out, middle_out, dx1_out, branch_out, mem_out, xhat_out,
     inv_out, gg2_out, rank_out, ids_out,
-    WG, WO, WA, WB, WD, Z1, ZE, XC, CC, H1C, GPS, MXS, MT, SWI, DA, DB, X1, H2O, HO, DHQ, FS, NS, BS, OWN, I2, SV, SA, SV2, SA2, SENT,
+    WG, WO, WA, WB, WD, Z1, ZE, XC, CC, H1C, GPS, MXS, MT, SWI, DA, DB, X1, H2O, HO, DHQ, FS, NS, BS, I2, SV, SA, SV2, SA2, SENT,
     load_sem, store_sem, stage_sem, t_send, t_recv, c_send, c_recv, h_send, h_recv, r_send, r_recv, e_send, e_recv,
     w_send, w_recv, w_local, s_send, s_recv, x_send, x_recv, i_send, i_recv, n_sem,
 ):
@@ -779,17 +782,18 @@
         loads = [pltpu.make_async_copy(mem_in.at[rows_of(index)], quarter(DB, index), load_sem.at[4 + index]) for index in range(4)]
         for copy in loads:
             copy.start()
-        row = deal_row[...]
+        row = deal_row[...].astype(jnp.float32)
+        columns = [to_column(row[:, index * chunk_rows:(index + 1) * chunk_rows]) for index in range(4)]
         rank = jnp.zeros((1, rows), jnp.float32)
         for chunk in range(4):
-            rank += jnp.sum(jnp.where(deal_column[rows_of(chunk)] < row, 1.0, 0.0), axis=0, keepdims=True)
+            rank += jnp.sum(jnp.where(columns[chunk] < row, 1.0, 0.0), axis=0, keepdims=True)
         rank_out[...] = jnp.broadcast_to(rank, (8, rows)).astype(jnp.int32)
         spots = lax.broadcasted_iota(jnp.int32, (chunk_rows, rows), 1).astype(jnp.float32)
         ordered = jnp.zeros((1, rows), jnp.float32)
         for chunk in range(4):
-            column = deal_column[rows_of(chunk)]
+            column = columns[chunk]
             place_of = jnp.sum(jnp.where(row < column, 1.0, 0.0), axis=1, keepdims=True)
-            ordered += jnp.sum(jnp.where(place_of == spots, column.astype(jnp.float32), 0.0), axis=0, keepdims=True)
+            ordered += jnp.sum(jnp.where(place_of == spots, column, 0.0), axis=0, keepdims=True)
         SENT[...] = jnp.broadcast_to(ordered, (8, rows)).astype(jnp.int32)
         ids_exchange.start()
         for copy in loads:
@@ -836,9 +840,9 @@
         return pltpu.make_async_copy(MXS.at[chunk % 2], mixed_out.at[rows_of(chunk)], store_sem.at[2 + chunk % 2])
 
     def hidden_stores(chunk):
-        slot = chunk % 2
+        slot = chunk % 3
         return [
-            pltpu.make_async_copy(source.at[slot], target.at[rows_of(chunk)], store_sem.at[4 + 2 * index + slot])
+            pltpu.make_async_copy(source.at[slot], target.at[rows_of(chunk)], store_sem.at[4 + 3 * index + slot])
             for index, (source, target) in enumerate(((SWI, swi_out), (DA, da_out), (DB, db_out)))
         ]
 
@@ -883,7 +887,9 @@
             values = XC[:, block * width:(block + 1) * width].astype(jnp.float32)
             square += jnp.sum(values * values, axis=1, keepdims=True)
         inverse = lax.rsqrt(square / features + EPS)
-        inv_out[rows_of(chunk)] = inverse
+        inv_out[:, rows_of(chunk)] = to_row(inverse)
+        HO[...] = XC[:, own_columns].astype(jnp.float32) * inverse
+        small_store(HO, xhat_out, chunk, 16).start()
         for block in range(4):
             at = slice(block * width, (block + 1) * width)
             H1C[:, at] = (XC[:, at].astype(jnp.float32) * inverse * gain1[:, at]).astype(jnp.bfloat16)
@@ -903,23 +909,24 @@
 
         gate_store(chunk).start()
         mixed_store(chunk).start()
+        small_store(HO, xhat_out, chunk, 16).wait()
 
     def mix_part(chunk, block):
         return jnp.dot(MXS[chunk % 2], WO[:, columns_of(block, width)], preferred_element_type=jnp.float32)
 
     def mix_own(chunk):
-        load = fetch(tokens.at[rows_of(chunk)], OWN, 2)
+        load = fetch(tokens.at[rows_of(chunk)], CC.at[:, 0:width], 2)
         if chunk > 0:
-            small_store(X1.at[rows_of(chunk)], middle_out, chunk - 1, 10).wait()
+            small_store(X1.at[rows_of(chunk)], middle_out, chunk - 1, 13).wait()
         HO[...] = mix_part(chunk, t)
         mix_scatter.own(chunk, HO)
         load.wait()
-        middle = OWN[...].astype(jnp.float32) + HO[...]
+        middle = CC[:, 0:width].astype(jnp.float32) + HO[...]
         X1[rows_of(chunk)] = middle
-        H2O[rows_of(chunk)] = (middle * gain2[...]).astype(jnp.bfloat16)
+        H2O[rows_of(chunk)] = (middle * gain2[:, own_columns]).astype(jnp.bfloat16)
         own_h2_store(chunk).start()
         SV[:, rows_of(chunk)] = to_row(jnp.sum(middle * middle, axis=1, keepdims=True))
-        small_store(X1.at[rows_of(chunk)], middle_out, chunk, 10).start()
+        small_store(X1.at[rows_of(chunk)], middle_out, chunk, 13).start()
         mix_scatter.finish(chunk)
         for step in range(1, 4):
             stat_copy(chunk, step, 0).start()
@@ -930,9 +937,9 @@
             own_cot.wait()
         loads = [fetch(h2_full.at[rows_of(chunk)], XC, 1), fetch(cot_full.at[rows_of(chunk)], CC, 3)]
         inverse = lax.rsqrt(stats(chunk, 0) / features + EPS)
-        I2[rows_of(chunk)] = inverse
-        if chunk > 1:
-            for store in hidden_stores(chunk - 2):
+        I2[:, rows_of(chunk)] = to_row(inverse)
+        if chunk > 2:
+            for store in hidden_stores(chunk - 3):
                 store.wait()
         for load in loads:
             load.wait()
@@ -945,10 +952,10 @@
             d_swi = dot_nt(CC[...], WD[at, :])
             sigma = jax.nn.sigmoid(up_a)
             swish = up_a * sigma
-            SWI[chunk % 2, :, at] = (swish * up_b).astype(jnp.bfloat16)
+            SWI[chunk % 3, :, at] = (swish * up_b).astype(jnp.bfloat16)
             d_swi = d_swi * inverse
-            DA[chunk % 2, :, at] = (d_swi * up_b * (sigma * (1.0 + up_a * (1.0 - sigma)))).astype(jnp.bfloat16)
-            DB[chunk % 2, :, at] = (d_swi * swish).astype(jnp.bfloat16)
+            DA[chunk % 3, :, at] = (d_swi * up_b * (sigma * (1.0 + up_a * (1.0 - sigma)))).astype(jnp.bfloat16)
+            DB[chunk % 3, :, at] = (d_swi * swish).astype(jnp.bfloat16)
 
         for store in hidden_stores(chunk):
             store.start()
@@ -960,12 +967,12 @@
         for block in range(4):
             if chunk > 0 or block > 1:
                 down_store(chunk, block).wait()
-            NS[block % 2] = jnp.dot(SWI[chunk % 2], WD[:, columns_of(block, width)], preferred_element_type=jnp.float32)
+            NS[block % 2] = jnp.dot(SWI[chunk % 3], WD[:, columns_of(block, width)], preferred_element_type=jnp.float32)
             down_store(chunk, block).start()
 
     def up_part(chunk, block):
         at = columns_of(block, width)
-        return dot_nt(DA[chunk % 2], WA[at, :]) + dot_nt(DB[chunk % 2], WB[at, :])
+        return dot_nt(DA[chunk % 3], WA[at, :]) + dot_nt(DB[chunk % 3], WB[at, :])
 
     def hidden_own(chunk):
         HO[...] = up_part(chunk, t)
@@ -977,26 +984,26 @@
             gg2_out[...] = grads
         else:
             gg2_out[...] += grads
-        scaled = d_second * gain2[...]
+        scaled = d_second * gain2[:, own_columns]
         DHQ[...] = scaled
-        SV2[:, rows_of(chunk)] = to_row(jnp.sum(scaled * middle, axis=1, keepdims=True) * I2[rows_of(chunk)])
+        SV2[:, rows_of(chunk)] = to_row(jnp.sum(scaled * middle, axis=1, keepdims=True) * to_column(I2[0:1, rows_of(chunk)]))
         up_scatter.finish(chunk)
         for step in range(1, 4):
             stat_copy(chunk, step, 1).start()
 
     def close(chunk):
-        load = fetch(cotangent.at[rows_of(chunk)], OWN, 2)
+        load = fetch(cotangent.at[rows_of(chunk)], CC.at[:, 0:width], 2)
         mean = stats(chunk, 1) / features
         if chunk > 0:
-            small_store(FS, dx1_out, chunk - 1, 11).wait()
-            small_store(BS, branch_out, chunk - 1, 12).wait()
+            small_store(FS, dx1_out, chunk - 1, 14).wait()
+            small_store(BS, branch_out, chunk - 1, 15).wait()
         load.wait()
-        unit = X1[rows_of(chunk)] * I2[rows_of(chunk)]
-        total = OWN[...].astype(jnp.float32) + DHQ[...] - unit * mean
+        unit = X1[rows_of(chunk)] * to_column(I2[0:1, rows_of(chunk)])
+        total = CC[:, 0:width].astype(jnp.float32) + DHQ[...] - unit * mean
         FS[...] = total
         BS[...] = total.astype(jnp.bfloat16)
-        small_store(FS, dx1_out, chunk, 11).start()
-        small_store(BS, branch_out, chunk, 12).start()
+        small_store(FS, dx1_out, chunk, 14).start()
+        small_store(BS, branch_out, chunk, 15).start()
 
     weight_stores = [
         pltpu.make_async_copy(WG, gate_w_out, stage_sem.at[2]), pltpu.make_async_copy(WO, out_w_out, stage_sem.at[3]),
@@ -1036,16 +1043,17 @@
     gate_store(3).wait()
     for chunk in (2, 3):
         mixed_store(chunk).wait()
+    for chunk in (1, 2, 3):
         for store in hidden_stores(chunk):
             store.wait()
-    small_store(X1.at[rows_of(3)], middle_out, 3, 10).wait()
+    small_store(X1.at[rows_of(3)], middle_out, 3, 13).wait()
     for block in (2, 3):
         down_store(3, block).wait()
-    small_store(FS, dx1_out, 3, 11).wait()
-    small_store(BS, branch_out, 3, 12).wait()
-
-
-def front_call(tokens, cotangent, mem, gate_w, out_w, up_a_w, up_b_w, down_w, gain1, gain2, deal_row, deal_column):
+    small_store(FS, dx1_out, 3, 14).wait()
+    small_store(BS, branch_out, 3, 15).wait()
+
+
+def front_call(tokens, cotangent, mem, gate_w, out_w, up_a_w, up_b_w, down_w, gain1, gain2, deal_row):
     rows, width = tokens.shape
     features, channels, hidden = 4 * width, mem.shape[1], up_a_w.shape[1]
     part = rows // 4
@@ -1062,25 +1070,26 @@
             shape((rows, features), bf), shape((rows, features), bf), shape((rows, features), bf), shape((rows, features), bf),
             shape((rows, channels), f32), shape((rows, channels), bf), shape((rows, hidden), bf), shape((rows, hidden), bf),
             shape((rows, hidden), bf), shape((features, channels), bf), shape((channels, features), bf), shape((rows, features), f32),
-            shape((rows, width), f32), shape((rows, width), f32), shape((rows, width), bf), shape((rows, channels), bf), shape((rows, 1), f32), shape((1, width), f32),
+            shape((rows, width), f32), shape((rows, width), f32), shape((rows, width), bf), shape((rows, channels), bf), shape((rows, width), f32), shape((8, rows), f32),
+            shape((1, width), f32),
             shape((8, rows), jnp.int32), shape((8, rows), jnp.int32),
         ),
-        in_specs=[anywhere] * 8 + [vmem] * 4,
-        out_specs=(anywhere,) * 16 + (vmem,) * 4,
+        in_specs=[anywhere] * 8 + [vmem] * 3,
+        out_specs=(anywhere,) * 17 + (vmem,) * 4,
         scratch_shapes=[
             V((features, channels), bf), V((channels, features), bf), V((features, hidden), bf), V((features, hidden), bf),
-            V((hidden, features), bf), V((2, 5, part, width), bf), V((2, 5, part, width), bf),
+            V((hidden, features), bf), V((2, 5, part, width), bf), V((3, 5, part, width), bf),
             V((part, features), bf), V((part, features), bf), V((part, features), bf), V((part, channels), f32), V((2, part, channels), bf),
-            V((part, channels), bf), V((2, part, hidden), bf), V((2, part, hidden), bf), V((2, part, hidden), bf), V((rows, width), f32),
+            V((part, channels), bf), V((3, part, hidden), bf), V((3, part, hidden), bf), V((3, part, hidden), bf), V((rows, width), f32),
             V((rows, width), bf), V((part, width), f32), V((part, width), f32), V((part, width), f32), V((2, part, width), f32), V((part, width), bf),
-            V((part, width), bf), V((rows, 1), f32), V((8, rows), f32), V((4, 8, rows), f32), V((8, rows), f32), V((4, 8, rows), f32),
-            V((8, rows), jnp.int32), dma((8,)), dma((13,)), dma((8,)), dma((4, 2, 3)), dma((4, 4)), dma((4, 2, 3)), dma((4, 4)), dma((4, 2, 3)), dma((4, 4)),
+            V((8, rows), f32), V((8, rows), f32), V((4, 8, rows), f32), V((8, rows), f32), V((4, 8, rows), f32),
+            V((8, rows), jnp.int32), dma((8,)), dma((17,)), dma((8,)), dma((4, 2, 3)), dma((4, 4)), dma((4, 2, 3)), dma((4, 4)), dma((4, 2, 3)), dma((4, 4)),
             dma((4, 3)), dma((4, 5)), dma((4, 3)), dma((4, 5)), dma((5, 7)), dma((5, 8)), dma((5,)),
             dma((2, 4, 3)), dma((2, 4, 3)), dma((8,)), dma((8,)), dma((8,)), dma((8,)), dma((2,)),
         ],
         compiler_params=pltpu.CompilerParams(collective_id=2, has_side_effects=True, vmem_limit_bytes=VMEM_LIMIT),
         cost_estimate=pl.CostEstimate(flops=2 * macs, bytes_accessed=96 * 2**20, transcendentals=rows * (channels + hidden)),
-    )(tokens, cotangent, mem, gate_w, out_w, up_a_w, up_b_w, down_w, gain1, gain2, deal_row, deal_column)
+    )(tokens, cotangent, mem, gate_w, out_w, up_a_w, up_b_w, down_w, gain1, gain2, deal_row)
 
 
 def silu_grad(values):
@@ -1192,22 +1201,20 @@
 ):
     width = tokens.shape[1]
     features = 4 * width
-    own = lambda array: lax.dynamic_slice_in_dim(array, lax.axis_index("tp") * width, width, 0)[None]
-    gain_one, gain_two = own(gain_first), own(gain_second)
     (
         _, full_cot, second, first, gate_pre, mixed, swished, d_a, d_b, gate_w, out_w, down, middle, d_middle, d_branch, memory_tokens,
-        inv_first, gain_two_part, rank, ids,
+        unit_own, inv_first, gain_two_part, rank, ids,
     ) = front_call(
-        tokens, cotangent, memory, memory_gate, memory_out, hidden_gate, hidden_up, hidden_down, gain_first[None], gain_two,
-        dealing[None], dealing[:, None],
-    )
-    unit_own = tokens.astype(jnp.float32) * inv_first
-    d_first, down_sum, grad_memory, _, _, grad_down, grad_up_a, grad_up_b, grad_out, grad_gate, gains, stats = back_call(
-        d_branch, full_cot, swished, second, d_a, d_b, mixed, first, gate_pre, memory_tokens, out_w, gate_w, unit_own, gain_one,
+        tokens, cotangent, memory, memory_gate, memory_out, hidden_gate, hidden_up, hidden_down, gain_first[None], gain_second[None],
+        dealing[None],
+    )
+    scaled, down_sum, grad_memory, _, _, grad_down, grad_up_a, grad_up_b, grad_out, grad_gate, gains, stats = back_call(
+        d_branch, full_cot, swished, second, d_a, d_b, mixed, first, gate_pre, memory_tokens, out_w, gate_w, unit_own, gain_first[None],
         gain_two_part, rank, ids, down,
     )
     block_out = (middle + down_sum).astype(jnp.bfloat16)
-    grad_inputs = d_middle + inv_first * (d_first * gain_one - unit_own * (stats[0][:, None] / features))
+    grad_inputs = d_middle + inv_first[0][:, None] * (scaled - unit_own * (stats[0][:, None] / features))
+    grad_memory = grad_memory.astype(jnp.float32)
     return (
         block_out, grad_inputs, grad_memory, gains[:, 0].reshape(features), gains[:, 1].reshape(features), grad_gate, grad_out.T,
         grad_up_a, grad_up_b, grad_down.T,

time: 519 us -> 505 us (0.973)
  local copies, waits for them, and re-layouts: 20.9 us -> 12.3 us
    unnamed x18 -> x15, local copies, waits for them, and re-layouts: 14.9 us -> 9.98 us
where the time goes in v6:
time: 505 us; the launch traced here: 496 us
  Pallas kernels  473 us (94%)
  local copies, waits for them, and re-layouts  12.3 us (2%)
  other arithmetic  9.43 us (2%)
    pallas_call x1, Pallas kernels, front_call(): pl.pallas_call(front_kernel, name='forward', out_shape=(shape((rows, feat...  292 us
    pallas_call x1, Pallas kernels, back_call(): pl.pallas_call(back_kernel, name='backward', out_shape=(shape((rows, widt...  182 us

profile of v6, /device:TPU:0, one launch (start us, length us, event | category | flops | bytes accessed | tf_op | source)
XLA Modules:
  0.0 496.0 jit_solution(1986332367293788105)
XLA Ops:
  0.6 291.7 %forward.1 = (bf16[1024,2048]{1,0:T(8,128)(2,1)}, bf16[1024,2048]{1,0:T(8,128)(2,1)}, bf16[1024,2048]{1,0:T(8,128)(2,1)}, bf16[1024,2048]{1,0:T(8,128)(2,1)}, f3...) custom-call(bf16[1024,512]{1,0:T(8,128)(2,1)} %tokens.1, ...), custom_call_target="tpu_custom_call" | custom-call | flops 60129542144 | bytes 100663296 | tf_op jit(solution)/shard_map/forward/pallas_call | solution.py:1066
  292.3 0.8 slice.12
  293.1 181.5 %backward.1 = (f32[1024,512]{1,0:T(8,128)}, f32[1024,512]{1,0:T(8,128)}, bf16[1024,1024]{1,0:T(8,128)(2,1)}, bf16[1024,1024]{1,0:T(8,128)(2,1)}, bf16[1024,1024]...) custom-call(bf16[1024,512]{1,0:T(8,128)(2,1)} %get-tuple-element.41., ...), custom_call_target="tpu_custom_call" | custom-call | flops 42949672960 | bytes 67108864 | tf_op jit(solution)/shard_map/backward/pallas_call | solution.py:586
  474.6 0.8 slice_multiply_fusion
  475.4 0.0 copy-start.4
  475.4 6.2 %multiply_add_fusion = (f32[1024,512]{1,0:T(8,128)}, bf16[1024,512]{1,0:T(8,128)(2,1)}) fusion(f32[1024,512]{1,0:T(8,128)} %get-tuple-element.59, f32[1024,512]{1,0:T(8,128)} %get-tuple-element.61, f32[1024,512]{1,0:T(8,128)} %get-tuple-element.53.xhat_in, f32[1024]{0:T(1024)S(1)} %bitcast.12, f32[1024]{0:T(1024)S(1)} %bitcast.11, ...), kind=kLoop, calls=%fused_computation | loop fusion | flops 3145728 | bytes 13639680 | tf_op jit(solution)/shard_map/add | solution.py:1216
  481.6 1.5 fusion
  483.1 0.0 copy-done.4
  483.1 1.3 copy.21
  484.4 0.0 copy-start
  484.4 3.0 copy.22
  487.4 0.0 copy-done
  487.4 0.0 copy-start.3
  487.4 2.5 convert_element_type.7
  489.9 0.0 copy-done.3
  489.9 0.0 copy-start.2
  489.9 1.0 copy.26
  490.9 1.0 copy-done.2
  491.9 0.0 copy-start.1
  491.9 1.3 copy.27
  493.2 1.0 copy-done.1
  494.2 1.3 copy.28
Async XLA Ops:
  475.4 7.7 %copy-start.4 = (f32[256,1024]{1,0:T(8,128)S(1)}, f32[256,1024]{1,0:T(8,128)}, u32[]{:S(2)}) copy-start(f32[256,1024]{1,0:T(8,128)} %get-tuple-element.66) | copy-start | bytes 3145732
  484.4 3.0 copy-start
  487.4 2.5 copy-start.3
  489.9 2.0 copy-start.2
  491.9 2.3 copy-start.1

commit v7 on v6

--- a/solution.py
+++ b/solution.py
@@ -237,7 +237,7 @@
     own_columns = pl.ds(pl.multiple_of(t * width, width), width)
     load("branch", branch_own, DB.at[:, own_columns], 0)
     load("cot", cot_in, A1, 1)
-    load("swi", swi_in, B1, 2)
+    load("swi", swi_in.at[:, 0:span], B1.at[:, 0:span], 2)
     greet(place)
 
     gather = Gather(place, DB, ag_send, ag_recv, chunk_rows, width)
@@ -531,13 +531,15 @@
         "terms": send_terms, "mgrads": memory_grads, "G": gains,
     }
     wanted = {
-        ("S1", 0): ("cot", "swi"), ("S1", 2): ("h2", "da"), ("S1", 4): ("db",), ("S1", 6): ("mixed",), ("S1", 7): ("h1",),
+        ("S1", 0): ("cot", "swi"), ("S1", 1): ("swi_rest",), ("S1", 2): ("h2", "da"), ("S1", 4): ("db",), ("S1", 6): ("mixed",), ("S1", 7): ("h1",),
         ("Bc", 0): ("out_w", "gate_w"),
     }
     GV[0] = jnp.zeros_like(GV[0])
     for event in BACK_ORDER:
         need(*wanted.get(event, ()))
         actions[event[0]](*event[1:])
+        if event == ("S1", 0):
+            load("swi_rest", swi_in.at[:, span:2 * span], B1.at[:, span:2 * span], 8)
         if event == ("S2", 0):
             load("h2", h2_in, A2, 3)
             load("da", da_in, B2, 4)
@@ -601,7 +603,7 @@
             V((2, slab, channels), bf), V((2, slab, channels), bf), V((slab, channels), f32), V((4, 5, part, width), bf),
             V((part, channels), f32), V((part, channels), bf), V((part, width), f32), V((part, width), f32),
             V((4, 8, width), f32), V((3, 8, width), f32), V((4, 8, width), f32), V((8, rows), f32), V((4, 8, rows), f32),
-            V((8, rows), jnp.int32), V((2, 5, part, width), bf), V((2, part, width), f32), V((part, width), f32), dma((8,)), dma((5,)), dma((4, 2, 3)), dma((4, 4)), dma((4, 3)), dma((4, 5)), dma((4,)), dma((JOBS, 4)), dma((2, 2)),
+            V((8, rows), jnp.int32), V((2, 5, part, width), bf), V((2, part, width), f32), V((part, width), f32), dma((9,)), dma((5,)), dma((4, 2, 3)), dma((4, 4)), dma((4, 3)), dma((4, 5)), dma((4,)), dma((JOBS, 4)), dma((2, 2)),
             dma((JOBS, 2)), dma((2,)), dma((JOBS,)), dma, dma((9,)), dma((9,)), dma((8,)), dma((8,)), dma((4, 3)), dma((4, 5)), dma((4,)), pltpu.SemaphoreType.REGULAR((2,)), regular, regular, regular,
         ],
         compiler_params=pltpu.CompilerParams(collective_id=1, has_side_effects=True, vmem_limit_bytes=VMEM_LIMIT),

time: 505 us -> 504 us (level)
  no operation moved by 1% of the time
where the time goes in v7:
time: 504 us; the launch traced here: 494 us
  Pallas kernels  472 us (94%)
  local copies, waits for them, and re-layouts  12.3 us (2%)
  other arithmetic  9.43 us (2%)
    pallas_call x1, Pallas kernels, front_call(): pl.pallas_call(front_kernel, name='forward', out_shape=(shape((rows, feat...  292 us
    pallas_call x1, Pallas kernels, back_call(): pl.pallas_call(back_kernel, name='backward', out_shape=(shape((rows, widt...  180 us

profile of v7, /device:TPU:0, one launch (start us, length us, event | category | flops | bytes accessed | tf_op | source)
XLA Modules:
  0.0 494.4 jit_solution(7567441227476079124)
XLA Ops:
  0.6 291.7 %forward.1 = (bf16[1024,2048]{1,0:T(8,128)(2,1)}, bf16[1024,2048]{1,0:T(8,128)(2,1)}, bf16[1024,2048]{1,0:T(8,128)(2,1)}, bf16[1024,2048]{1,0:T(8,128)(2,1)}, f3...) custom-call(bf16[1024,512]{1,0:T(8,128)(2,1)} %tokens.1, ...), custom_call_target="tpu_custom_call" | custom-call | flops 60129542144 | bytes 100663296 | tf_op jit(solution)/shard_map/forward/pallas_call | solution.py:1068
  292.3 0.8 slice.12
  293.1 179.9 %backward.1 = (f32[1024,512]{1,0:T(8,128)}, f32[1024,512]{1,0:T(8,128)}, bf16[1024,1024]{1,0:T(8,128)(2,1)}, bf16[1024,1024]{1,0:T(8,128)(2,1)}, bf16[1024,1024]...) custom-call(bf16[1024,512]{1,0:T(8,128)(2,1)} %get-tuple-element.41., ...), custom_call_target="tpu_custom_call" | custom-call | flops 42949672960 | bytes 67108864 | tf_op jit(solution)/shard_map/backward/pallas_call | solution.py:588
  473.0 0.8 slice_multiply_fusion
  473.7 0.0 copy-start.4
  473.7 6.2 %multiply_add_fusion = (f32[1024,512]{1,0:T(8,128)}, bf16[1024,512]{1,0:T(8,128)(2,1)}) fusion(f32[1024,512]{1,0:T(8,128)} %get-tuple-element.59, f32[1024,512]{1,0:T(8,128)} %get-tuple-element.61, f32[1024,512]{1,0:T(8,128)} %get-tuple-element.53.xhat_in, f32[1024]{0:T(1024)S(1)} %bitcast.12, f32[1024]{0:T(1024)S(1)} %bitcast.11, ...), kind=kLoop, calls=%fused_computation | loop fusion | flops 3145728 | bytes 13639680 | tf_op jit(solution)/shard_map/add | solution.py:1218
  479.9 1.5 fusion
  481.4 0.0 copy-done.4
  481.5 1.3 copy.21
  482.8 0.0 copy-start
  482.8 3.0 copy.22
  485.8 0.0 copy-done
  485.8 0.0 copy-start.3
  485.8 2.5 convert_element_type.7
  488.3 0.0 copy-done.3
  488.3 0.0 copy-start.2
  488.3 1.0 copy.26
  489.2 1.0 copy-done.2
  490.2 0.0 copy-start.1
  490.2 1.3 copy.27
  491.6 1.0 copy-done.1
  492.6 1.3 copy.28
Async XLA Ops:
  473.7 7.7 %copy-start.4 = (f32[256,1024]{1,0:T(8,128)S(1)}, f32[256,1024]{1,0:T(8,128)}, u32[]{:S(2)}) copy-start(f32[256,1024]{1,0:T(8,128)} %get-tuple-element.66) | copy-start | bytes 3145732
  482.8 3.0 copy-start
  485.8 2.5 copy-start.3
  488.3 2.0 copy-start.2
  490.2 2.3 copy-start.1
